TPU v7x, 256 devices: a whole 4x4x8 slice. The times are simulated.
256 devices in a mesh: ctx: 32 (over x_lo, z, core), head: 8 (over y, x_hi).
Axes of the slice: x: 4 (x_hi: 2, x_lo: 2; x = x_hi * 2 + x_lo), y: 4, z: 8, core: 2. Of those that a mesh axis runs over, the one named last changes fastest.
Arguments:
- q_latent: bfloat16 [4096, 1536], P(('ctx', 'head')), may hold values from -320 to 320
- q_gain: float32 [1536], replicated, may hold values from 0.5 to 8
- kv_cache: bfloat16 [4096, 576], P(('ctx', 'head')), may hold values from -320 to 320
- kv_gain: float32 [512], replicated, may hold values from 0.5 to 8
- w_query: bfloat16 [1536, 12288], P(None, 'head'), may hold values from -0.15625 to 0.15625
- w_kv: bfloat16 [512, 16384], P(None, 'head'), may hold values from -0.25 to 0.25
- doc_lengths: int32 [3], replicated, may hold values from 1 to 2048, 4096 in all
Outputs:
- attn_out: bfloat16 [4096, 8192], P('ctx', 'head')
Inputs may be any that keep to these rules, and one draw needn't show every extreme that they name: `doc_lengths`: 3 documents, lengths in order summing to 4096; the longest has exactly 2048 tokens.
All inputs are finite; a program needn't handle non-finite values.
Results may differ from a plain program's by a relative error of at most 0.0075.
The roundings to bfloat16 on the way count: a program that leaves them out, or rounds other values in their place, can miss the bound.
Values may be sent and summed in bfloat16 or wider, within the bound.
No kernel may reach another device: no remote copies, remote signals or barrier semaphores. Data moves between devices by JAX's collectives and lax.ppermute only.
A program may use at most 192 MiB of HBM per device.

v0:
```python
import math

import jax
import jax.numpy as jnp
from jax import lax
from jax.sharding import PartitionSpec as P

KL = 512
RD = 64
ND = 128
VD = 128


epsilon = 1e-06


def rms_scale(rows, gain):
    values = rows.astype(jnp.float32)
    return values * lax.rsqrt(jnp.mean(values * values, axis=-1, keepdims=True) + epsilon) * gain


def doc_tables(doc_lengths, positions):
    doc_ends = jnp.cumsum(doc_lengths)
    passed = positions[:, None] >= doc_ends[None, :]
    doc_index = jnp.sum(passed.astype(jnp.int32), axis=1)
    doc_start = jnp.sum(jnp.where(passed, doc_lengths[None, :], 0), axis=1)
    return (doc_index, doc_start)


def rotate_pairs(values, offsets):
    half_width = values.shape[-1] // 2
    freq_index = jnp.arange(half_width, dtype=jnp.float32)
    frequency = jnp.exp(freq_index * (-2.0 * math.log(10000.0) / values.shape[-1]))
    angles = offsets.astype(jnp.float32)[:, None] * frequency[None, :]
    cosine = jnp.cos(angles)[:, None, :]
    sine_part = jnp.sin(angles)[:, None, :]
    lower_half = values[..., :half_width]
    upper_half = values[..., half_width:]
    return jnp.concatenate(
        [
            lower_half * cosine - upper_half * sine_part,
            upper_half * cosine + lower_half * sine_part,
        ],
        axis=-1,
    )


def project_queries(latent_rows, q_gain, w_query, offsets, nope_width, rope_width):
    normed = rms_scale(latent_rows, q_gain).astype(jnp.bfloat16)
    projected = jnp.dot(normed, w_query, preferred_element_type=jnp.float32)
    head_count = w_query.shape[1] // (nope_width + rope_width)
    projected = projected.reshape(latent_rows.shape[0], head_count, nope_width + rope_width)
    rotated = rotate_pairs(projected[..., nope_width:], offsets)
    return jnp.concatenate([projected[..., :nope_width], rotated], axis=-1).astype(jnp.bfloat16)


def body(q_latent, q_gain, kv_cache, kv_gain, w_query, w_kv, doc_lengths):
    tok_dev = q_latent.shape[0] * lax.axis_size("head")
    heads_here = w_query.shape[1] // (ND + RD)
    ctx_first = lax.axis_index("ctx") * tok_dev
    score_scale = 1.0 / math.sqrt(ND + RD)
    block_rows = lax.all_gather(q_latent, "head", axis=0, tiled=True)
    positions = ctx_first + jnp.arange(block_rows.shape[0], dtype=jnp.int32)
    unused_index, doc_start = doc_tables(doc_lengths, positions)
    made = project_queries(block_rows, q_gain, w_query, positions - doc_start, ND, RD)
    queries = made.reshape(block_rows.shape[0], heads_here * (ND + RD))
    queries = queries.reshape(tok_dev, heads_here, ND + RD)
    q_nope = queries[..., :ND]
    q_rope = queries[..., ND:]
    block_rows = lax.all_gather(kv_cache, "head", axis=0, tiled=True)
    normed = rms_scale(block_rows[:, :KL], kv_gain).astype(jnp.bfloat16)
    payload = jnp.concatenate([normed, block_rows[:, KL:]], axis=1)
    query_pos = ctx_first + jnp.arange(tok_dev, dtype=jnp.int32)
    query_doc, unused_start = doc_tables(doc_lengths, query_pos)
    block_rows = lax.all_gather(payload, "ctx", axis=0, tiled=True)
    running_max = jnp.full((tok_dev, heads_here), -1e30, jnp.float32)
    rows_here = block_rows.shape[0]
    expanded = jnp.dot(block_rows[:, :KL], w_kv, preferred_element_type=jnp.float32).astype(
        jnp.bfloat16
    )
    expanded = expanded.reshape(rows_here, heads_here, ND + VD)
    key_rope = block_rows[:, block_rows.shape[1] - RD :]
    key_pos = jnp.arange(rows_here, dtype=jnp.int32)
    key_doc, unused_offset = doc_tables(doc_lengths, key_pos)
    allowed = (key_pos[None, :] <= query_pos[:, None]) & (key_doc[None, :] == query_doc[:, None])
    scores = jnp.einsum(
        "qhd,khd->qhk", q_nope, expanded[..., :ND], preferred_element_type=jnp.float32
    )
    scores = scores + jnp.einsum(
        "qhr,kr->qhk", q_rope, key_rope, preferred_element_type=jnp.float32
    )
    scores = scores * score_scale
    masked = jnp.where(allowed[:, None, :], scores, -1e30)
    new_max = jnp.maximum(running_max, jnp.max(masked, axis=-1))
    weights = jnp.where(allowed[:, None, :], jnp.exp(scores - new_max[..., None]), 0.0)
    row_total = jnp.sum(weights, axis=-1)
    mixed = jnp.einsum(
        "qhk,khv->qhv",
        weights.astype(jnp.bfloat16),
        expanded[..., ND:],
        preferred_element_type=jnp.float32,
    )
    weighted = mixed
    running_max, row_total, weighted = (new_max, row_total, weighted)
    outputs = weighted / row_total[..., None]
    return outputs.reshape(tok_dev, heads_here * VD).astype(jnp.bfloat16)


def solution(mesh):
    placed = (
        P(("ctx", "head"), None),
        P(),
        P(("ctx", "head"), None),
        P(),
        P(None, "head"),
        P(None, "head"),
        P(),
    )
    return jax.shard_map(
        body, mesh=mesh, in_specs=placed, out_specs=P("ctx", "head"), check_vma=False
    )
```

profile of v0, /device:TPU:1, one launch (start us, length us, event | category | flops | bytes accessed | tf_op | source)
XLA Modules:
  0.0 187.2 jit_solution(7557123522005346459)
XLA Ops:
  6.5 0.0 copy-start
  6.5 0.0 all-gather.2.cloned.1.call-start
  6.5 30.0 %all_gather.9 = bf16[128,576]{1,0:T(8,128)(2,1)S(1)} all-gather(bf16[16,576]{1,0:T(8,128)(2,1)} %param.9), channel_id=1, replica_groups=mesh['ctx'=32,'head'=8] {'head'}, dimensions={0}, use_global_device_ids=true | all-gather | bytes 165888 | tf_op jit(solution)/shard_map/all_gather | solution.py:70
  36.5 0.1 copy.51
  36.7 0.1 fusion.35
  36.8 0.1 copy.52
  36.9 0.8 fusion.37
  37.7 0.7 pad_maximum_fusion
  38.4 0.0 all-gather.2.cloned.1.call-update
  38.4 0.8 reduce-window.8
  39.2 0.1 convert_reduce_fusion
  39.4 0.7 fusion.41
  40.1 29.8 %all_gather.11 = bf16[128,1536]{1,0:T(8,128)(2,1)S(1)} all-gather(bf16[16,1536]{1,0:T(8,128)(2,1)} %param.7), channel_id=1, replica_groups=mesh['ctx'=32,'head'=8] {'head'}, dimensions={0}, use_global_device_ids=true | all-gather | bytes 442368 | tf_op jit(solution)/shard_map/all_gather | solution.py:62
  69.9 0.2 fusion.28
  70.1 0.1 multiply_cosine_fusion
  70.2 4.4 %fusion.31 = f32[128,1536]{0,1:T(8,128)S(1)} fusion(bf16[1536,1536]{1,0:T(8,128)(2,1)} %param.11, bf16[128,1536]{1,0:T(8,128)(2,1)S(1)} %all_gather.11, f32[1536]{0:T(1024)} %param.8, f32[128]{0:T(128)S(1)} %add_rsqrt_fusion), kind=kOutput, calls=%fused_computation.27 | convolution fusion | flops 604766208 | bytes 5904896 | tf_op jit(solution)/shard_map/dot_general | solution.py:50
  74.7 1.9 %fusion.12 = pred[128,4096]{0,1:T(8,128)(4,1)S(1)} fusion(s32[128]{0:T(128)S(1)} %get-tuple-element.5, s32[128]{0:T(128)S(1)} %iota_add_fusion, s32[4096]{0:T(1024)S(1)} %convert_reduce_fusion), kind=kLoop, calls=%fused_computation.16 | loop fusion | flops 1572864 | bytes 541696 | tf_op jit(solution)/shard_map/and | solution.py:85
  76.6 45.4 %all-gather.2.cloned.1.call-done = bf16[4096,576]{0,1:T(8,128)(2,1)} async-done(((bf16[128,576]{0,1:T(8,128)(2,1)}), bf16[4096,576]{0,1:T(8,128)(2,1)}) %all-gather.2.cloned.1.call-update) | async-done | bytes 4718608 | tf_op jit(solution)/shard_map/all_gather | solution.py:75
  122.0 0.0 copy-done
  122.0 14.5 %convolution_convert_fusion = bf16[4096,2048]{0,1:T(8,128)(2,1)} fusion(bf16[512,2048]{1,0:T(8,128)(2,1)S(1)} %copy-done, bf16[4096,576]{0,1:T(8,128)(2,1)} %all-gather.2.cloned.1.call-done), kind=kOutput, calls=%fused_computation.4 | convolution fusion | flops 8598323200 | bytes 23068672 | tf_op jit(solution)/shard_map/dot_general | solution.py:78
  136.5 11.7 %fusion.5 = f32[8,4096,128]{2,1,0:T(8,128)} fusion(bf16[4096,8,256]{0,2,1:T(8,128)(2,1)} %bitcast.22, f32[128,8,192]{0,2,1:T(8,128)S(1)} %bitcast.25), kind=kOutput, calls=%fused_computation.8 | convolution fusion | flops 1073741824 | bytes 25427968 | tf_op jit(solution)/shard_map/qhd,khd->qhk/dot_general | solution.py:86
  148.2 10.7 %select_reduce_fusion = (f32[128,8]{0,1:T(8,128)S(1)}, f32[128,8,4096]{0,2,1:T(8,128)}) fusion(pred[128,4096]{0,1:T(8,128)(4,1)S(1)} %fusion.12, bf16[4096,576]{0,1:T(8,128)(2,1)} %all-gather.2.cloned.1.call-done, bf16[128,8,32]{0,2,1:T(8,128)(2,1)S(1)} %get-tuple-element.8, bf16[128,8,32]{0,2,1:T(8,128)(2,1)S(1)} %get-tuple-element.7, ...), kind=kOutput, calls=%fused_computation.3 | convolution fusion | flops 553909248 | bytes 34738176 | tf_op jit(solution)/shard_map/qhr,kr->qhk/dot_general | solution.py:89
  158.9 8.6 %fusion.1 = f32[128,8]{0,1:T(8,128)S(1)} fusion(f32[128,8,4096]{0,2,1:T(8,128)} %get-tuple-element.12, f32[128,8]{0,1:T(8,128)S(1)} %broadcast_maximum_fusion, pred[128,4096]{0,1:T(8,128)(4,1)S(1)} %fusion.12), kind=kLoop, calls=%fused_computation.5 | loop fusion | flops 12581888 | bytes 17309696 | tf_op jit(solution)/shard_map/reduce_sum | solution.py:96
  167.5 11.9 %fusion.23 = bf16[128,8,128]{0,2,1:T(8,128)(2,1)S(1)} fusion(f32[128,8,4096]{0,2,1:T(8,128)} %get-tuple-element.12, f32[128,8]{0,1:T(8,128)S(1)} %broadcast_maximum_fusion, pred[128,4096]{0,1:T(8,128)(4,1)S(1)} %fusion.12, bf16[4096,8,256]{0,2,1:T(8,128)(2,1)} %bitcast.23, f32[128,8]{0,1:T(8,128)S(1)} %fusion.1), kind=kOutput, calls=%fused_computation.19 | convolution fusion | flops 1086586880 | bytes 25960448 | tf_op jit(solution)/shard_map/qhk,khv->qhv/dot_general | solution.py:97
  179.5 0.9 copy.46
  (9 shorter events, 0.1 us)
Async XLA Ops:
  6.5 115.4 %copy-start = (bf16[512,2048]{1,0:T(8,128)(2,1)S(1)}, bf16[512,2048]{1,0:T(8,128)(2,1)}, u32[]{:S(2)}) copy-start(bf16[512,2048]{1,0:T(8,128)(2,1)} %param.12) | copy-start | bytes 6291460
  6.5 115.4 %all-gather.2.cloned.1.call-start = ((), (), s32[]{:S(2)}) async-start(), calls=%async_computation | async-start | bytes 4866048 | tf_op jit(solution)/shard_map/all_gather | solution.py:75
Sparse Core Ops, SparseCore 0:
  38.5 83.4 all-gather.1
where the time goes:
time: 187 us
  blocking collectives  59.8 us (32%)
  matrix products  53.3 us (29%)
  waiting for transfers between devices  45.4 us (24%)
  other arithmetic  14.1 us (8%)
  between operations  13.5 us (7%)
    all_gather x1, waiting for transfers between devices, body(): block_rows = lax.all_gather(payload, 'ctx', axis=0, tiled=True)  45.4 us
    all_gather x1, blocking collectives, body(): block_rows = lax.all_gather(kv_cache, 'head', axis=0, tiled=True)  30 us
    all_gather x1, blocking collectives, body(): block_rows = lax.all_gather(q_latent, 'head', axis=0, tiled=True)  29.8 us
    dot_general x1, matrix products, body(): jnp.dot(block_rows[:, :KL], w_kv, preferred_element_type=jnp.float32)  14.5 us
    dot_general x1, matrix products, body(): jnp.einsum('qhk,khv->qhv', weights.astype(jnp.bfloat16), expanded[..., ND...  11.9 us
    dot_general x1, matrix products, body(): jnp.einsum('qhd,khd->qhk', q_nope, expanded[..., :ND], preferred_element_...  11.7 us
    dot_general x1, matrix products, body(): jnp.einsum('qhr,kr->qhk', q_rope, key_rope, preferred_element_type=jnp.fl...  10.7 us
    reduce_sum x1, other arithmetic, body(): row_total = jnp.sum(weights, axis=-1)  8.61 us
  transfers between devices with their start and end apart: 1, of which 1 were waited for; matrix products, arithmetic and copies ran while one was open for 4% of the time, Pallas kernels for 0%

commit v1 on v0

v1 whole, which is shorter than its diff:
```python
import math

import jax
import jax.numpy as jnp
import numpy as np
from jax import lax
from jax.experimental import pallas as pl
from jax.experimental.pallas import tpu as pltpu
from jax.sharding import PartitionSpec as P

KL = 512
RD = 64
ND = 128
VD = 128
LANES = 128
EPSILON = 1e-06
MASKED = -1e30
FLOOR = -1e29
SCORE_SCALE = math.log2(math.e) / math.sqrt(ND + RD)


def norm_kernel(q_ref, qg_ref, kv_ref, kg_ref, q_out, kv_out):
    def scaled(values, gain):
        mean = jnp.mean(values * values, axis=-1, keepdims=True)
        return values * lax.rsqrt(mean + EPSILON) * gain

    q_out[...] = scaled(q_ref[...].astype(jnp.float32), qg_ref[...]).astype(jnp.bfloat16)
    latent = kv_ref[:, :KL].astype(jnp.float32)
    kv_out[:, :KL] = scaled(latent, kg_ref[...]).astype(jnp.bfloat16)
    kv_out[:, KL:] = kv_ref[:, KL:]


def query_kernel(places, own, after, before, across, cos_ref, sin_ref, w_ref, out_ref, rows_ref):
    @pl.when(pl.program_id(0) == 0)
    def _():
        for n, ref in enumerate((own, after, before, across)):
            for half in range(2):
                at = pl.multiple_of(places[2 * n + half], 16)
                rows_ref[pl.ds(at, 16), :] = ref[16 * half : 16 * half + 16, :]

    made = jnp.dot(rows_ref[...], w_ref[...], preferred_element_type=jnp.float32)
    lane = lax.broadcasted_iota(jnp.int32, (made.shape[0], LANES), 1)

    def rotated(rope):
        turned = jnp.where(
            lane < RD // 2, pltpu.roll(rope, LANES - RD // 2, 1), pltpu.roll(rope, RD // 2, 1)
        )
        return rope * cos_ref[...] + turned * sin_ref[...]

    out_ref[0, :, :ND] = made[:, :ND].astype(jnp.bfloat16)
    out_ref[0, :, ND:] = rotated(made[:, ND : ND + LANES]).astype(jnp.bfloat16)
    second = ND + RD
    out_ref[1, :, :ND] = made[:, second : second + ND].astype(jnp.bfloat16)
    rope = pltpu.roll(made[:, second + RD : second + RD + LANES], RD, 1)
    out_ref[1, :, ND:] = rotated(rope).astype(jnp.bfloat16)


def attend_kernel(n_pieces, first, last, *refs):
    q_ref, key_pos, query_pos, query_start, w_ref = refs[:5]
    pieces = refs[5 : 5 + n_pieces]
    at = 5 + n_pieces
    if not first:
        max_in, sum_in, acc_in = refs[at : at + 3]
        at += 3
    if last:
        (out_ref,) = refs[at : at + 1]
        at += 1
    else:
        max_out, sum_out, acc_out = refs[at : at + 3]
        at += 3
    rows_ref, rope_ref, bias_ref = refs[at:]
    size = pieces[0].shape[0]

    @pl.when(pl.program_id(0) == 0)
    def _():
        for n, ref in enumerate(pieces):
            low = pl.ds(n * size, size)
            high = pl.ds((n_pieces + n) * size, size)
            rows_ref[low, :] = ref[:, :KL]
            rows_ref[high, :] = ref[:, KL : 2 * KL]
            rope = ref[:, 2 * KL :]
            rope_ref[low, :] = rope
            rope_ref[high, :] = jnp.concatenate([rope[:, RD:], rope[:, :RD]], axis=1)
        allowed = (key_pos[...] <= query_pos[...]) & (key_pos[...] >= query_start[...])
        bias_ref[...] = jnp.where(allowed, 0.0, MASKED)

    for head in range(q_ref.shape[0]):
        w = w_ref[:, head * (ND + VD) : (head + 1) * (ND + VD)]
        expanded = jnp.dot(rows_ref[...], w, preferred_element_type=jnp.float32)
        expanded = expanded.astype(jnp.bfloat16)
        keys = jnp.concatenate([expanded[:, :ND], rope_ref[...]], axis=1)
        scores = lax.dot_general(
            q_ref[head], keys, (((1,), (1,)), ((), ())), preferred_element_type=jnp.float32
        )
        scores = scores * SCORE_SCALE + bias_ref[...]
        top = jnp.max(scores, axis=1, keepdims=True)
        if first:
            new_max = jnp.maximum(top, FLOOR)
        else:
            old_max = max_in[head][:, :1]
            new_max = jnp.maximum(top, old_max)
        weights = jnp.exp2(scores - new_max)
        total = jnp.sum(weights, axis=1, keepdims=True)
        mixed = jnp.dot(
            weights.astype(jnp.bfloat16), expanded[:, ND:], preferred_element_type=jnp.float32
        )
        if not first:
            faded = jnp.exp2(old_max - new_max)
            total = total + faded * sum_in[head][:, :1]
            mixed = mixed + faded * acc_in[head]
        if last:
            out_ref[:, head * VD : (head + 1) * VD] = (mixed / total).astype(jnp.bfloat16)
        else:
            max_out[head] = jnp.broadcast_to(new_max, mixed.shape)
            sum_out[head] = jnp.broadcast_to(total, mixed.shape)
            acc_out[head] = mixed


def attend(queries, key_pos, query_pos, query_start, w_kv, pieces, state, last):
    heads, rows, width = queries.shape
    group = 2
    first = state is None
    count = key_pos.shape[1]

    def whole(a):
        return pl.BlockSpec(a.shape, lambda h: (0,) * a.ndim)

    part = pl.BlockSpec((group, rows, VD), lambda h: (h, 0, 0))
    in_specs = [
        pl.BlockSpec((group, rows, width), lambda h: (h, 0, 0)),
        whole(key_pos),
        whole(query_pos),
        whole(query_start),
        pl.BlockSpec((KL, group * (ND + VD)), lambda h: (0, h)),
        *[whole(p) for p in pieces],
    ]
    args = [queries, key_pos, query_pos, query_start, w_kv, *pieces]
    if not first:
        in_specs += [part] * 3
        args += list(state)
    if last:
        out_shape = jax.ShapeDtypeStruct((rows, heads * VD), jnp.bfloat16)
        out_specs = pl.BlockSpec((rows, group * VD), lambda h: (0, h))
    else:
        out_shape = [jax.ShapeDtypeStruct((heads, rows, VD), jnp.float32)] * 3
        out_specs = [part] * 3

    def kernel(*refs):
        attend_kernel(len(pieces), first, last, *refs)

    return pl.pallas_call(
        kernel,
        grid=(heads // group,),
        in_specs=in_specs,
        out_specs=out_specs,
        out_shape=out_shape,
        scratch_shapes=[
            pltpu.VMEM((count, KL), jnp.bfloat16),
            pltpu.VMEM((count, LANES), jnp.bfloat16),
            pltpu.VMEM((rows, count), jnp.float32),
        ],
        compiler_params=pltpu.CompilerParams(vmem_limit_bytes=48 * 2**20),
    )(*args)


def body(q_latent, q_gain, kv_cache, kv_gain, w_query, w_kv, doc_lengths):
    ctx_size, head_size = lax.axis_size("ctx"), lax.axis_size("head")
    chips, ys = ctx_size // 2, head_size // 2
    reach = chips // 4
    mine = q_latent.shape[0]
    tok_dev = mine * head_size
    heads_here = w_query.shape[1] // (ND + RD)
    ctx, head = lax.axis_index("ctx"), lax.axis_index("head")
    chip, core, y, xh = ctx // 2, ctx % 2, head // 2, head % 2

    swap = [(n, n ^ 1) for n in range(ctx_size)]
    across_x = [(n, n ^ 1) for n in range(head_size)]

    def chip_shift(step):
        return [
            (2 * n + c, 2 * ((n + step + reach * c) % chips) + c)
            for n in range(chips)
            for c in range(2)
        ]

    def y_shift(step):
        return [(2 * n + x, 2 * ((n + step) % ys) + x) for n in range(ys) for x in range(2)]

    q_rows, kv_rows = pl.pallas_call(
        norm_kernel,
        out_shape=[
            jax.ShapeDtypeStruct(q_latent.shape, jnp.bfloat16),
            jax.ShapeDtypeStruct(kv_cache.shape, jnp.bfloat16),
        ],
    )(q_latent, q_gain[None, :], kv_cache, kv_gain[None, :])

    kv_other = lax.ppermute(kv_rows, "head", across_x)
    q_other = lax.ppermute(q_rows, "head", across_x)

    piece = jnp.concatenate(
        [kv_rows[:, :KL], kv_other[:, :KL], kv_rows[:, KL:], kv_other[:, KL:]], axis=1
    )
    swapped = lax.ppermute(piece, "ctx", swap)
    even = jnp.where(core == 0, piece, swapped)
    odd = jnp.where(core == 0, swapped, piece)
    pair = jnp.concatenate([even, odd], axis=0)
    window = [lax.ppermute(pair, "ctx", chip_shift(step)) for step in range(1, reach + 1)]

    q_pair = jnp.concatenate([q_rows, q_other], axis=0)
    q_after = lax.ppermute(q_pair, "head", y_shift(1))
    q_before = lax.ppermute(q_pair, "head", y_shift(-1))
    q_across = lax.ppermute(q_pair, "head", y_shift(2))

    held = jnp.concatenate([piece, *window], axis=0)
    from_after = lax.ppermute(held, "head", y_shift(1))
    from_before = lax.ppermute(held, "head", y_shift(-1))
    from_across = lax.ppermute(held, "head", y_shift(2))

    query_pos = ctx * tok_dev + jnp.arange(tok_dev, dtype=jnp.int32)
    doc_end = jnp.zeros((), jnp.int32)
    query_start = jnp.zeros_like(query_pos)
    for doc in range(doc_lengths.shape[0]):
        doc_end = doc_end + doc_lengths[doc]
        query_start = query_start + jnp.where(query_pos >= doc_end, doc_lengths[doc], 0)
    half_width = RD // 2
    freq_index = jnp.arange(half_width, dtype=jnp.float32)
    frequency = jnp.exp(freq_index * (-2.0 * math.log(10000.0) / RD))
    angles = (query_pos - query_start).astype(jnp.float32)[:, None] * frequency[None, :]
    cosine, sine = jnp.cos(angles), jnp.sin(angles)
    blank = jnp.zeros((tok_dev, LANES - RD), jnp.float32)
    cos_table = jnp.concatenate([cosine, cosine, blank], axis=1)
    sin_table = jnp.concatenate([-sine, sine, blank], axis=1)

    sources = [y, (y - 1) % ys, (y + 1) % ys, (y + 2) % ys]
    places = jnp.stack([s * 2 * mine + x * mine for s in sources for x in (xh, 1 - xh)])
    row_spec = pl.BlockSpec(q_pair.shape, lambda h, *_: (0, 0))
    table_spec = pl.BlockSpec(cos_table.shape, lambda h, *_: (0, 0))
    pair_width = 2 * (ND + RD)
    queries = pl.pallas_call(
        query_kernel,
        grid_spec=pltpu.PrefetchScalarGridSpec(
            num_scalar_prefetch=1,
            grid=(heads_here // 2,),
            in_specs=[row_spec] * 4
            + [table_spec] * 2
            + [pl.BlockSpec((w_query.shape[0], pair_width), lambda h, *_: (0, h))],
            out_specs=pl.BlockSpec((2, tok_dev, 2 * LANES), lambda h, *_: (h, 0, 0)),
            scratch_shapes=[pltpu.VMEM((tok_dev, w_query.shape[0]), jnp.bfloat16)],
        ),
        out_shape=jax.ShapeDtypeStruct((heads_here, tok_dev, 2 * LANES), jnp.bfloat16),
        compiler_params=pltpu.CompilerParams(vmem_limit_bytes=48 * 2**20),
    )(places, q_pair, q_after, q_before, q_across, cos_table, sin_table, w_query)

    def held_rows(c):
        rows = [c * tok_dev + np.arange(mine)]
        for step in range(1, reach + 1):
            for parity in range(2):
                rows.append((parity - 2 * (step + reach * c)) * tok_dev + np.arange(mine))
        return np.concatenate(rows).astype(np.int32)

    table = np.stack([held_rows(0), held_rows(1)])
    own_rows = jnp.where(core == 0, table[0], table[1]) + 2 * chip * tok_dev
    partner_rows = jnp.where(core == 0, table[1], table[0]) + 2 * chip * tok_dev

    def key_positions(which):
        halves = []
        for x in (xh, 1 - xh):
            for s in which:
                for rows in (own_rows, partner_rows):
                    halves.append(rows + s * 2 * mine + x * mine)
        return jnp.concatenate(halves)[None, :]

    at = (query_pos[:, None], query_start[:, None], w_kv)

    own_swapped = lax.ppermute(held, "ctx", swap)
    state = attend(queries, key_positions(sources[:1]), *at, [held, own_swapped], None, False)
    after_swapped = lax.ppermute(from_after, "ctx", swap)
    before_swapped = lax.ppermute(from_before, "ctx", swap)
    near = [from_after, after_swapped, from_before, before_swapped]
    state = attend(queries, key_positions(sources[1:3]), *at, near, state, False)
    across_swapped = lax.ppermute(from_across, "ctx", swap)
    far = [from_across, across_swapped]
    return attend(queries, key_positions(sources[3:]), *at, far, state, True)


def solution(mesh):
    placed = (
        P(("ctx", "head"), None),
        P(),
        P(("ctx", "head"), None),
        P(),
        P(None, "head"),
        P(None, "head"),
        P(),
    )
    return jax.shard_map(
        body, mesh=mesh, in_specs=placed, out_specs=P("ctx", "head"), check_vma=False
    )
```

time: 187 us -> 104 us (0.56)
  blocking collectives: 59.8 us -> 0 us
  matrix products: 53.3 us -> 0 us
  Pallas kernels: 0 us -> 34.8 us
  waiting for transfers between devices: 45.4 us -> 10.6 us
  starting transfers between devices: 0.01 us -> 32.8 us
  local copies, waits for them, and re-layouts: 1.08 us -> 15.7 us
  between operations: 13.5 us -> 2.06 us
  other arithmetic: 14.1 us -> 7.05 us
    all_gather x2 -> x0, blocking collectives: 59.8 us -> none  [the longest x1 30 us: body(): block_rows = lax.all_gather(kv_cache, 'head', axis=0, tiled=True)]
    dot_general x5 -> x0, matrix products: 53.3 us -> none  [the longest x1 14.5 us: body(): jnp.dot(block_rows[:, :KL], w_kv, preferred_element_type=jnp.float32)]
    all_gather x1 -> x0, waiting for transfers between devices: 45.4 us -> none  [body(): block_rows = lax.all_gather(payload, 'ctx', axis=0, tiled=True)]
    pallas_call x0 -> x5, Pallas kernels: none -> 34.8 us  [the longest x3 29.3 us: attend(): pl.pallas_call(kernel, grid=(heads // group,), in_specs=in_specs, out_spe...]
    ppermute x0 -> x17, starting transfers between devices: none -> 32.8 us  [the longest x4 7.02 us: body(): lax.ppermute(pair, 'ctx', chip_shift(step))]
    ppermute x0 -> x17, waiting for transfers between devices: none -> 10.6 us  [the longest x4 4.54 us: body(): lax.ppermute(pair, 'ctx', chip_shift(step))]
    reduce_sum x5 -> x0, other arithmetic: 9.71 us -> none  [the longest x1 8.61 us: body(): row_total = jnp.sum(weights, axis=-1)]
    unnamed x4 -> x20, local copies, waits for them, and re-layouts: 0.22 us -> 5.32 us
  transfers between devices with their start and end apart: 1 -> 17, of which waited for: 1 -> 6; matrix products, arithmetic and copies ran while one was open for 4% -> 17% of each run, Pallas kernels for 0% -> 23%
where the time goes in v1:
time: 104 us; the launch traced here: 103 us
  Pallas kernels  34.8 us (33%)
  starting transfers between devices  32.8 us (32%)
  local copies, waits for them, and re-layouts  15.7 us (15%)
  waiting for transfers between devices  10.6 us (10%)
  other arithmetic  7.05 us (7%)
  between operations  2.06 us (2%)
    pallas_call x3, Pallas kernels, attend(): pl.pallas_call(kernel, grid=(heads // group,), in_specs=in_specs, out_spe...  29.3 us
    ppermute x4, starting transfers between devices, body(): lax.ppermute(pair, 'ctx', chip_shift(step))  7.02 us
    ppermute x1, starting transfers between devices, body(): own_swapped = lax.ppermute(held, 'ctx', swap)  6.59 us
    unnamed x20, local copies, waits for them, and re-layouts  5.32 us
    ppermute x4, waiting for transfers between devices, body(): lax.ppermute(pair, 'ctx', chip_shift(step))  4.54 us
    pallas_call x1, Pallas kernels, body(): pl.pallas_call(query_kernel, grid_spec=pltpu.PrefetchScalarGridSpec(num_s...  4.01 us
    ppermute x1, starting transfers between devices, body(): kv_other = lax.ppermute(kv_rows, 'head', across_x)  3.57 us
    ppermute x1, starting transfers between devices, body(): swapped = lax.ppermute(piece, 'ctx', swap)  3.18 us
  transfers between devices with their start and end apart: 17, of which 6 were waited for; matrix products, arithmetic and copies ran while one was open for 17% of the time, Pallas kernels for 23%

profile of v1, /device:TPU:1, one launch (start us, length us, event | category | flops | bytes accessed | tf_op | source)
XLA Modules:
  0.0 103.0 jit_solution(14933825427510049122)
XLA Ops:
  0.0 1.4 %broadcast_in_dim.42.qg_ref = f32[1,1536]{1,0:T(1,128)} reshape(f32[1536]{0:T(1024)} %param.12) | data formatting | bytes 12288 | tf_op jit(solution)/shard_map/broadcast_in_dim | solution.py:195
  1.4 1.5 %shard_map.109 = (bf16[16,1536]{1,0:T(8,128)(2,1)}, bf16[16,576]{1,0:T(8,128)(2,1)}) custom-call(bf16[16,1536]{1,0:T(8,128)(2,1)} %q_ref.1, f32[1,1536]{1,0:T(1,128)} %broadcast_in_dim.42.qg_ref, bf16[16,576]{1,0:T(8,128)(2,1)} %kv_ref.1, f32[1,512]{1,0:T(1,128)} %bitcast.12), custom_call_target="tpu_custom_call" | custom-call | tf_op jit(solution)/shard_map/pallas_call | solution.py:189
  3.0 3.6 %collective-permute-start.4 = (bf16[16,576]{1,0:T(8,128)(2,1)}, bf16[16,576]{1,0:T(8,128)(2,1)S(1)}, u32[]{:S(2)}, u32[]{:S(2)}) collective-permute-start(bf16[16,576]{1,0:T(8,128)(2,1)} %get-tuple-element.14), channel_id=1, source_target_pairs={{0,1},{1,0},{2,3},{3,2},{4,5},{5,4},{6,7},{7,6},{8,9},{9,8},{10,11... | collective-permute-start | bytes 55304 | tf_op jit(solution)/shard_map/ppermute | solution.py:197
  6.6 0.0 collective-permute-start
  6.6 1.4 %fusion.32 = (s32[1]{0:T(128)}, s32[1]{0:T(128)}, s32[1]{0:T(128)}) fusion(s32[3]{0:T(128)} %param.17), kind=kLoop, calls=%fused_computation.56 | loop fusion | bytes 24 | tf_op jit(solution)/shard_map/slice | solution.py:223
  9.9 1.9 %fusion.31 = f32[128]{0:T(128)S(1)} fusion(s32[]{:T(128)} %bitcast.11, s32[]{:T(128)S(6)} %add.261, s32[]{:T(128)} %bitcast.10, s32[]{:T(128)S(6)} %add.259, s32[]{:T(128)} %bitcast.9, s32[]{:T(128)S(6)} %mul.36), kind=kLoop, calls=%fused_computation.54 | loop fusion | flops 1408 | bytes 536 | tf_op jit(solution)/shard_map/convert_element_type | solution.py:228
  11.8 0.3 fusion.3
  12.1 0.7 slice.27
  12.8 0.7 slice.29
  13.5 0.1 pad.15.clone
  13.6 0.0 collective-permute-done.4
  13.6 0.1 concatenate.31
  13.7 3.2 %collective-permute-start.5 = (bf16[16,1152]{1,0:T(8,128)(2,1)S(1)}, bf16[16,1152]{1,0:T(8,128)(2,1)S(1)}, u32[]{:S(2)}, u32[]{:S(2)}) collective-permute-start(bf16[16,1152]{1,0:T(8,128)(2,1)S(1)} %concatenate.31), channel_id=1, source_target_pairs={{0,8},{8,0},{16,24},{24,16},{32,40},{40,32},{48,56},{56,48},{64,72... | collective-permute-start | bytes 110600 | tf_op jit(solution)/shard_map/ppermute | solution.py:203
  16.8 0.1 maximum_maximum_fusion.1
  17.0 0.7 collective-permute-done.5
  17.7 4.8 %collective-permute-start.6 = (bf16[32,1152]{1,0:T(8,128)(2,1)S(1)}, bf16[32,1152]{1,0:T(8,128)(2,1)S(1)}, u32[]{:S(2)}, u32[]{:S(2)}) collective-permute-start(bf16[32,1152]{1,0:T(8,128)(2,1)S(1)} %pad_maximum_fusion), channel_id=1, source_target_pairs={{0,16},{8,88},{16,32},{24,104},{32,48},{40,120},{48,64},{56,136},{... | collective-permute-start | bytes 221192 | tf_op jit(solution)/shard_map/ppermute | solution.py:207
  22.6 1.4 %constant_dynamic-update-slice_fusion.1 = bf16[32,1536]{1,0:T(8,128)(2,1)} fusion(bf16[16,1536]{1,0:T(8,128)(2,1)} %get-tuple-element.13), kind=kLoop, calls=%fused_computation.14 | loop fusion | bytes 98304
  24.0 1.2 %collective-permute-start.7 = (bf16[32,1152]{1,0:T(8,128)(2,1)S(1)}, bf16[32,1152]{1,0:T(8,128)(2,1)S(1)}, u32[]{:S(2)}, u32[]{:S(2)}) collective-permute-start(bf16[32,1152]{1,0:T(8,128)(2,1)S(1)} %pad_maximum_fusion), channel_id=1, source_target_pairs={{0,32},{8,104},{16,48},{24,120},{32,64},{40,136},{48,80},{56,152},... | collective-permute-start | bytes 221192 | tf_op jit(solution)/shard_map/ppermute | solution.py:207
  25.2 0.5 collective-permute-start.8
  25.6 0.6 collective-permute-start.9
  26.2 0.0 collective-permute-done.6
  26.2 3.7 %collective-permute-done.7 = bf16[32,1152]{1,0:T(8,128)(2,1)S(1)} collective-permute-done((bf16[32,1152]{1,0:T(8,128)(2,1)S(1)}, bf16[32,1152]{1,0:T(8,128)(2,1)S(1)}, u32[]{:S(2)}, u32[]{:S(2)}) %collective-permute-start.7) | collective-permute-done | bytes 73760 | tf_op jit(solution)/shard_map/ppermute | solution.py:207
  29.9 0.5 collective-permute-done.8
  30.4 0.4 collective-permute-done.9
  30.8 1.4 %collective-permute-start.12 = (bf16[144,1152]{1,0:T(8,128)(2,1)S(1)}, bf16[144,1152]{1,0:T(8,128)(2,1)S(1)}, u32[]{:S(2)}, u32[]{:S(2)}) collective-permute-start(bf16[144,1152]{1,0:T(8,128)(2,1)S(1)} %constant_dynamic-update-slice_fusion.2.refs_5_), channel_id=1, source_target_pairs={{0,2},{1,3},{2,4},{3,5},{4,6},{5,7},{6,0},{7,1},{8,10},{9,11},{10,... | collective-permute-start | bytes 995336 | tf_op jit(solution)/shard_map/ppermute | solution.py:215
  32.2 1.5 %collective-permute-start.14 = (bf16[144,1152]{1,0:T(8,128)(2,1)S(1)}, bf16[144,1152]{1,0:T(8,128)(2,1)S(1)}, u32[]{:S(2)}, u32[]{:S(2)}) collective-permute-start(bf16[144,1152]{1,0:T(8,128)(2,1)S(1)} %constant_dynamic-update-slice_fusion.2.refs_5_), channel_id=1, source_target_pairs={{0,6},{1,7},{2,0},{3,1},{4,2},{5,3},{6,4},{7,5},{8,14},{9,15},{10,... | collective-permute-start | bytes 995336 | tf_op jit(solution)/shard_map/ppermute | solution.py:216
  33.7 1.6 %collective-permute-start.10 = (bf16[144,1152]{1,0:T(8,128)(2,1)S(1)}, bf16[144,1152]{1,0:T(8,128)(2,1)S(1)}, u32[]{:S(2)}, u32[]{:S(2)}) collective-permute-start(bf16[144,1152]{1,0:T(8,128)(2,1)S(1)} %constant_dynamic-update-slice_fusion.2.refs_5_), channel_id=1, source_target_pairs={{0,4},{1,5},{2,6},{3,7},{4,0},{5,1},{6,2},{7,3},{8,12},{9,13},{10,... | collective-permute-start | bytes 995336 | tf_op jit(solution)/shard_map/ppermute | solution.py:217
  35.2 1.4 %fusion.19 = (s32[144]{0:T(256)}, s32[144]{0:T(256)}, s32[144]{0:T(256)}, s32[144]{0:T(256)}, s32[144]{0:T(256)}, /*index=5*/s32[144]{0:T(256)}, s32[144]{0:T(25...) fusion(s32[144]{0:T(256)} %constant.84.clone, ...), kind=kLoop, calls=%fused_computation.42 | loop fusion | flops 4032 | bytes 10397 | tf_op jit(solution)/shard_map/add | solution.py:270
  36.6 0.0 collective-permute-done
  36.6 1.4 %constant_dynamic-update-slice_fusion.own = bf16[32,1536]{1,0:T(8,128)(2,1)} fusion(bf16[32,1536]{1,0:T(8,128)(2,1)} %constant_dynamic-update-slice_fusion.1, bf16[16,1536]{1,0:T(8,128)(2,1)} %collective-permute-done), kind=kLoop, calls=%fused_computation.13 | loop fusion | bytes 98304 | tf_op jit(solution)/shard_map/concatenate | solution.py:209
  38.0 0.4 collective-permute-start.1
  38.4 6.6 %collective-permute-start.16 = (bf16[144,1152]{1,0:T(8,128)(2,1)S(1)}, bf16[144,1152]{1,0:T(8,128)(2,1)}, u32[]{:S(2)}, u32[]{:S(2)}) collective-permute-start(bf16[144,1152]{1,0:T(8,128)(2,1)S(1)} %constant_dynamic-update-slice_fusion.2.refs_5_), channel_id=1, source_target_pairs={{0,8},{8,0},{16,24},{24,16},{32,40},{40,32},{48,56},{56,48},{64,72... | collective-permute-start | bytes 995336 | tf_op jit(solution)/shard_map/ppermute | solution.py:275
  45.0 0.0 collective-permute-done.12.refs_5_
  45.0 3.1 %collective-permute-start.13 = (bf16[144,1152]{1,0:T(8,128)(2,1)S(1)}, bf16[144,1152]{1,0:T(8,128)(2,1)}, u32[]{:S(2)}, u32[]{:S(2)}) collective-permute-start(bf16[144,1152]{1,0:T(8,128)(2,1)S(1)} %collective-permute-done.12.refs_5_), channel_id=1, source_target_pairs={{0,8},{8,0},{16,24},{24,16},{32,40},{40,32},{48,56},{56,48},{64,72... | collective-permute-start | bytes 995336 | tf_op jit(solution)/shard_map/ppermute | solution.py:277
  48.1 0.0 collective-permute-done.14.refs_7_
  48.1 0.7 collective-permute-start.15
  48.8 0.0 collective-permute-done.10.refs_5_
  48.8 2.9 %collective-permute-start.11 = (bf16[144,1152]{1,0:T(8,128)(2,1)S(1)}, bf16[144,1152]{1,0:T(8,128)(2,1)}, u32[]{:S(2)}, u32[]{:S(2)}) collective-permute-start(bf16[144,1152]{1,0:T(8,128)(2,1)S(1)} %collective-permute-done.10.refs_5_), channel_id=1, source_target_pairs={{0,8},{8,0},{16,24},{24,16},{32,40},{40,32},{48,56},{56,48},{64,72... | collective-permute-start | bytes 995336 | tf_op jit(solution)/shard_map/ppermute | solution.py:281
  51.8 0.8 pad_add_fusion.1
  52.6 0.6 broadcast_in_dim.53.refs_1_
  53.2 1.4 %concatenate.34 = s32[1152]{0:T(1024)} concatenate(s32[144]{0:T(256)} %get-tuple-element.33, s32[144]{0:T(256)} %get-tuple-element.35, s32[144]{0:T(256)} %get-tuple-element.34, s32[144]{0:T(256)} %get-tuple-element.36, s32[144]{0:T(256)} %get-tuple-element.31, s32[144]{0:T(256)} %get-tuple-element.27, s32[144]{0:T(256)} %get-tuple-element.30, s32[144]{0:T(256)} %get-tuple-element.26), dimensions={0} | concatenate | bytes 9216 | tf_op jit(solution)/shard_map/concatenate | solution.py:271
  54.5 1.3 %broadcast_in_dim.52.refs_1_ = s32[1,1152]{1,0:T(1,128)} reshape(s32[1152]{0:T(1024)} %concatenate.34) | data formatting | bytes 9216 | tf_op jit(solution)/shard_map/broadcast_in_dim | solution.py:271
  55.8 0.0 collective-permute-done.1.after
  55.8 0.4 collective-permute-start.2
  56.3 0.8 pad_add_fusion
  57.0 0.6 broadcast_in_dim.48.refs_1_
  57.6 0.6 stack.35.places
  58.2 2.3 %collective-permute-done.2.before = bf16[32,1536]{1,0:T(8,128)(2,1)} collective-permute-done((bf16[32,1536]{1,0:T(8,128)(2,1)}, bf16[32,1536]{1,0:T(8,128)(2,1)}, u32[]{:S(2)}, u32[]{:S(2)}) %collective-permute-start.2) | collective-permute-done | bytes 98336 | tf_op jit(solution)/shard_map/ppermute | solution.py:211
  60.6 0.4 collective-permute-start.3
  61.0 1.9 %select_add_fusion = (s32[128,1]{1,0:T(8,128)S(1)}, s32[128,1]{1,0:T(8,128)S(1)}) fusion(s32[]{:T(128)} %bitcast.11, s32[]{:T(128)S(6)} %add.261, s32[]{:T(128)} %bitcast.10, s32[]{:T(128)S(6)} %add.259, s32[]{:T(128)} %bitcast.9, s32[]{:T(128)S(6)} %mul.36), kind=kLoop, calls=%fused_computation.5 | loop fusion | flops 1152 | bytes 1048 | tf_op jit(solution)/shard_map/add | solution.py:224
  62.8 2.9 %collective-permute-done.3.across = bf16[32,1536]{1,0:T(8,128)(2,1)S(1)} collective-permute-done((bf16[32,1536]{1,0:T(8,128)(2,1)}, bf16[32,1536]{1,0:T(8,128)(2,1)S(1)}, u32[]{:S(2)}, u32[]{:S(2)}) %collective-permute-start.3) | collective-permute-done | bytes 98336 | tf_op jit(solution)/shard_map/ppermute | solution.py:212
  65.7 2.3 %copy-done.2 = bf16[1536,1536]{1,0:T(8,128)(2,1)S(1)} copy-done((bf16[1536,1536]{1,0:T(8,128)(2,1)S(1)}, bf16[1536,1536]{1,0:T(8,128)(2,1)}, u32[]{:S(2)}) %copy-start.2) | copy-done | bytes 4718616
  68.1 0.9 copy-done.3
  69.0 0.6 copy-done.7
  69.6 4.0 %shard_map.110.refs_0_ = bf16[8,128,256]{2,1,0:T(8,128)(2,1)S(1)} custom-call(s32[8]{0:T(128)S(1)} %copy-done.7, bf16[32,1536]{1,0:T(8,128)(2,1)S(1)} %copy-done.3, bf16[32,1536]{1,0:T(8,128)(2,1)} %collective-permute-done.1.after, bf16[32,1536]{1,0:T(8,128)(2,1)} %collective-permute-done.2.before, bf16[32,1536]{1,0:T(8,128)(2,1)S(1)} %collective-permute-done.3.across, ...), custom_call_target="tpu_custom_call" | custom-call | tf_op jit(solution)/shard_map/pallas_call | solution.py:239
  73.6 0.0 copy-start.1
  73.6 0.0 copy-start.6
  73.6 0.0 collective-permute-done.16.refs_6_
  73.7 8.0 %shard_map.111 = (f32[8,128,128]{2,1,0:T(8,128)S(1)}, f32[8,128,128]{2,1,0:T(8,128)S(1)}, f32[8,128,128]{2,1,0:T(8,128)S(1)}) custom-call(bf16[8,128,256]{2,1,0:T(8,128)(2,1)S(1)} %shard_map.110.refs_0_, s32[1,576]{1,0:T(1,128)S(1)} %copy-done.5, s32[128,1]{1,0:T(8,128)S(1)} %get-tuple-element.49.refs_2_, s32[128,1]{1,0:T(8,128)S(1)} %get-tuple-element.48.refs_3_, ...), custom_call_target="tpu_custom_call" | custom-call | tf_op jit(solution)/shard_map/pallas_call | solution.py:151
  81.7 0.0 collective-permute-done.13.refs_6_
  81.7 0.0 collective-permute-done.15.refs_8_
  81.7 11.8 %shard_map.112 = (f32[8,128,128]{2,1,0:T(8,128)S(1)}, f32[8,128,128]{2,1,0:T(8,128)S(1)}, f32[8,128,128]{2,1,0:T(8,128)S(1)}) custom-call(bf16[8,128,256]{2,1,0:T(8,128)(2,1)S(1)} %shard_map.110.refs_0_, s32[1,1152]{1,0:T(1,128)S(1)} %copy-done.4, s32[128,1]{1,0:T(8,128)S(1)} %get-tuple-element.49.refs_2_, s32[128,1]{1,0:T(8,128)S(1)} %get-tuple-element.48.refs_3_, ...), custom_call_target="tpu_custom_call" | custom-call | tf_op jit(solution)/shard_map/pallas_call | solution.py:151
  93.6 0.0 collective-permute-done.11.refs_6_
  93.6 9.4 %shard_map.113 = bf16[128,1024]{1,0:T(8,128)(2,1)} custom-call(bf16[8,128,256]{2,1,0:T(8,128)(2,1)S(1)} %shard_map.110.refs_0_, s32[1,576]{1,0:T(1,128)S(1)} %copy-done.6, s32[128,1]{1,0:T(8,128)S(1)} %get-tuple-element.49.refs_2_, s32[128,1]{1,0:T(8,128)S(1)} %get-tuple-element.48.refs_3_, bf16[512,2048]{1,0:T(8,128)(2,1)S(1)} %copy-done.1, ...), custom_call_target="tpu_custom_call" | custom-call | tf_op jit(solution)/shard_map/pallas_call | solution.py:151
  (21 shorter events, 0.1 us)
Async XLA Ops:
  0.0 73.6 %copy-start = (bf16[512,2048]{1,0:T(8,128)(2,1)S(1)}, bf16[512,2048]{1,0:T(8,128)(2,1)}, u32[]{:S(2)}) copy-start(bf16[512,2048]{1,0:T(8,128)(2,1)} %refs_4_.5) | copy-start | bytes 6291460
  3.0 10.6 %collective-permute-start.4 = (bf16[16,576]{1,0:T(8,128)(2,1)}, bf16[16,576]{1,0:T(8,128)(2,1)S(1)}, u32[]{:S(2)}, u32[]{:S(2)}) collective-permute-start(bf16[16,576]{1,0:T(8,128)(2,1)} %get-tuple-element.14), channel_id=1, source_target_pairs={{0,1},{1,0},{2,3},{3,2},{4,5},{5,4},{6,7},{7,6},{8,9},{9,8},{10,11... | collective-permute-start | bytes 55304 | tf_op jit(solution)/shard_map/ppermute | solution.py:197
  6.6 30.0 %collective-permute-start = (bf16[16,1536]{1,0:T(8,128)(2,1)}, bf16[16,1536]{1,0:T(8,128)(2,1)}, u32[]{:S(2)}, u32[]{:S(2)}) collective-permute-start(bf16[16,1536]{1,0:T(8,128)(2,1)} %get-tuple-element.13), channel_id=1, source_target_pairs={{0,1},{1,0},{2,3},{3,2},{4,5},{5,4},{6,7},{7,6},{8,9},{9,8},{10,11... | collective-permute-start | bytes 147464 | tf_op jit(solution)/shard_map/ppermute | solution.py:198
  13.7 4.0 %collective-permute-start.5 = (bf16[16,1152]{1,0:T(8,128)(2,1)S(1)}, bf16[16,1152]{1,0:T(8,128)(2,1)S(1)}, u32[]{:S(2)}, u32[]{:S(2)}) collective-permute-start(bf16[16,1152]{1,0:T(8,128)(2,1)S(1)} %concatenate.31), channel_id=1, source_target_pairs={{0,8},{8,0},{16,24},{24,16},{32,40},{40,32},{48,56},{56,48},{64,72... | collective-permute-start | bytes 110600 | tf_op jit(solution)/shard_map/ppermute | solution.py:203
  17.7 8.4 %collective-permute-start.6 = (bf16[32,1152]{1,0:T(8,128)(2,1)S(1)}, bf16[32,1152]{1,0:T(8,128)(2,1)S(1)}, u32[]{:S(2)}, u32[]{:S(2)}) collective-permute-start(bf16[32,1152]{1,0:T(8,128)(2,1)S(1)} %pad_maximum_fusion), channel_id=1, source_target_pairs={{0,16},{8,88},{16,32},{24,104},{32,48},{40,120},{48,64},{56,136},{... | collective-permute-start | bytes 221192 | tf_op jit(solution)/shard_map/ppermute | solution.py:207
  24.0 5.9 %collective-permute-start.7 = (bf16[32,1152]{1,0:T(8,128)(2,1)S(1)}, bf16[32,1152]{1,0:T(8,128)(2,1)S(1)}, u32[]{:S(2)}, u32[]{:S(2)}) collective-permute-start(bf16[32,1152]{1,0:T(8,128)(2,1)S(1)} %pad_maximum_fusion), channel_id=1, source_target_pairs={{0,32},{8,104},{16,48},{24,120},{32,64},{40,136},{48,80},{56,152},... | collective-permute-start | bytes 221192 | tf_op jit(solution)/shard_map/ppermute | solution.py:207
  25.2 5.2 %collective-permute-start.8 = (bf16[32,1152]{1,0:T(8,128)(2,1)S(1)}, bf16[32,1152]{1,0:T(8,128)(2,1)S(1)}, u32[]{:S(2)}, u32[]{:S(2)}) collective-permute-start(bf16[32,1152]{1,0:T(8,128)(2,1)S(1)} %pad_maximum_fusion), channel_id=1, source_target_pairs={{0,48},{8,120},{16,64},{24,136},{32,80},{40,152},{48,96},{56,168},... | collective-permute-start | bytes 221192 | tf_op jit(solution)/shard_map/ppermute | solution.py:207
  25.6 5.1 %collective-permute-start.9 = (bf16[32,1152]{1,0:T(8,128)(2,1)S(1)}, bf16[32,1152]{1,0:T(8,128)(2,1)S(1)}, u32[]{:S(2)}, u32[]{:S(2)}) collective-permute-start(bf16[32,1152]{1,0:T(8,128)(2,1)S(1)} %pad_maximum_fusion), channel_id=1, source_target_pairs={{0,64},{8,136},{16,80},{24,152},{32,96},{40,168},{48,112},{56,184}... | collective-permute-start | bytes 221192 | tf_op jit(solution)/shard_map/ppermute | solution.py:207
  30.8 14.2 %collective-permute-start.12 = (bf16[144,1152]{1,0:T(8,128)(2,1)S(1)}, bf16[144,1152]{1,0:T(8,128)(2,1)S(1)}, u32[]{:S(2)}, u32[]{:S(2)}) collective-permute-start(bf16[144,1152]{1,0:T(8,128)(2,1)S(1)} %constant_dynamic-update-slice_fusion.2.refs_5_), channel_id=1, source_target_pairs={{0,2},{1,3},{2,4},{3,5},{4,6},{5,7},{6,0},{7,1},{8,10},{9,11},{10,... | collective-permute-start | bytes 995336 | tf_op jit(solution)/shard_map/ppermute | solution.py:215
  32.2 16.0 %collective-permute-start.14 = (bf16[144,1152]{1,0:T(8,128)(2,1)S(1)}, bf16[144,1152]{1,0:T(8,128)(2,1)S(1)}, u32[]{:S(2)}, u32[]{:S(2)}) collective-permute-start(bf16[144,1152]{1,0:T(8,128)(2,1)S(1)} %constant_dynamic-update-slice_fusion.2.refs_5_), channel_id=1, source_target_pairs={{0,6},{1,7},{2,0},{3,1},{4,2},{5,3},{6,4},{7,5},{8,14},{9,15},{10,... | collective-permute-start | bytes 995336 | tf_op jit(solution)/shard_map/ppermute | solution.py:216
  33.7 15.2 %collective-permute-start.10 = (bf16[144,1152]{1,0:T(8,128)(2,1)S(1)}, bf16[144,1152]{1,0:T(8,128)(2,1)S(1)}, u32[]{:S(2)}, u32[]{:S(2)}) collective-permute-start(bf16[144,1152]{1,0:T(8,128)(2,1)S(1)} %constant_dynamic-update-slice_fusion.2.refs_5_), channel_id=1, source_target_pairs={{0,4},{1,5},{2,6},{3,7},{4,0},{5,1},{6,2},{7,3},{8,12},{9,13},{10,... | collective-permute-start | bytes 995336 | tf_op jit(solution)/shard_map/ppermute | solution.py:217
  38.0 17.8 %collective-permute-start.1 = (bf16[32,1536]{1,0:T(8,128)(2,1)}, bf16[32,1536]{1,0:T(8,128)(2,1)}, u32[]{:S(2)}, u32[]{:S(2)}) collective-permute-start(bf16[32,1536]{1,0:T(8,128)(2,1)} %constant_dynamic-update-slice_fusion.own), channel_id=1, source_target_pairs={{0,2},{1,3},{2,4},{3,5},{4,6},{5,7},{6,0},{7,1},{8,10},{9,11},{10,... | collective-permute-start | bytes 294920 | tf_op jit(solution)/shard_map/ppermute | solution.py:210
  38.4 35.2 %collective-permute-start.16 = (bf16[144,1152]{1,0:T(8,128)(2,1)S(1)}, bf16[144,1152]{1,0:T(8,128)(2,1)}, u32[]{:S(2)}, u32[]{:S(2)}) collective-permute-start(bf16[144,1152]{1,0:T(8,128)(2,1)S(1)} %constant_dynamic-update-slice_fusion.2.refs_5_), channel_id=1, source_target_pairs={{0,8},{8,0},{16,24},{24,16},{32,40},{40,32},{48,56},{56,48},{64,72... | collective-permute-start | bytes 995336 | tf_op jit(solution)/shard_map/ppermute | solution.py:275
  45.0 36.7 %collective-permute-start.13 = (bf16[144,1152]{1,0:T(8,128)(2,1)S(1)}, bf16[144,1152]{1,0:T(8,128)(2,1)}, u32[]{:S(2)}, u32[]{:S(2)}) collective-permute-start(bf16[144,1152]{1,0:T(8,128)(2,1)S(1)} %collective-permute-done.12.refs_5_), channel_id=1, source_target_pairs={{0,8},{8,0},{16,24},{24,16},{32,40},{40,32},{48,56},{56,48},{64,72... | collective-permute-start | bytes 995336 | tf_op jit(solution)/shard_map/ppermute | solution.py:277
  48.1 33.6 %collective-permute-start.15 = (bf16[144,1152]{1,0:T(8,128)(2,1)S(1)}, bf16[144,1152]{1,0:T(8,128)(2,1)}, u32[]{:S(2)}, u32[]{:S(2)}) collective-permute-start(bf16[144,1152]{1,0:T(8,128)(2,1)S(1)} %collective-permute-done.14.refs_7_), channel_id=1, source_target_pairs={{0,8},{8,0},{16,24},{24,16},{32,40},{40,32},{48,56},{56,48},{64,72... | collective-permute-start | bytes 995336 | tf_op jit(solution)/shard_map/ppermute | solution.py:278
  48.8 44.7 %collective-permute-start.11 = (bf16[144,1152]{1,0:T(8,128)(2,1)S(1)}, bf16[144,1152]{1,0:T(8,128)(2,1)}, u32[]{:S(2)}, u32[]{:S(2)}) collective-permute-start(bf16[144,1152]{1,0:T(8,128)(2,1)S(1)} %collective-permute-done.10.refs_5_), channel_id=1, source_target_pairs={{0,8},{8,0},{16,24},{24,16},{32,40},{40,32},{48,56},{56,48},{64,72... | collective-permute-start | bytes 995336 | tf_op jit(solution)/shard_map/ppermute | solution.py:281
  55.8 4.7 %collective-permute-start.2 = (bf16[32,1536]{1,0:T(8,128)(2,1)}, bf16[32,1536]{1,0:T(8,128)(2,1)}, u32[]{:S(2)}, u32[]{:S(2)}) collective-permute-start(bf16[32,1536]{1,0:T(8,128)(2,1)} %constant_dynamic-update-slice_fusion.own), channel_id=1, source_target_pairs={{0,6},{1,7},{2,0},{3,1},{4,2},{5,3},{6,4},{7,5},{8,14},{9,15},{10,... | collective-permute-start | bytes 294920 | tf_op jit(solution)/shard_map/ppermute | solution.py:211
  58.2 15.4 %copy-start.5 = (s32[1,576]{1,0:T(1,128)S(1)}, s32[1,576]{1,0:T(1,128)}, u32[]{:S(2)}) copy-start(s32[1,576]{1,0:T(1,128)} %broadcast_in_dim.53.refs_1_) | copy-start | bytes 6916
  58.2 23.5 %copy-start.4 = (s32[1,1152]{1,0:T(1,128)S(1)}, s32[1,1152]{1,0:T(1,128)}, u32[]{:S(2)}) copy-start(s32[1,1152]{1,0:T(1,128)} %broadcast_in_dim.52.refs_1_) | copy-start | bytes 13828
  60.6 5.2 %collective-permute-start.3 = (bf16[32,1536]{1,0:T(8,128)(2,1)}, bf16[32,1536]{1,0:T(8,128)(2,1)S(1)}, u32[]{:S(2)}, u32[]{:S(2)}) collective-permute-start(bf16[32,1536]{1,0:T(8,128)(2,1)} %constant_dynamic-update-slice_fusion.own), channel_id=1, source_target_pairs={{0,4},{1,5},{2,6},{3,7},{4,0},{5,1},{6,2},{7,3},{8,12},{9,13},{10,... | collective-permute-start | bytes 294920 | tf_op jit(solution)/shard_map/ppermute | solution.py:212
  65.7 2.3 %copy-start.2 = (bf16[1536,1536]{1,0:T(8,128)(2,1)S(1)}, bf16[1536,1536]{1,0:T(8,128)(2,1)}, u32[]{:S(2)}) copy-start(bf16[1536,1536]{1,0:T(8,128)(2,1)} %w_ref.1) | copy-start | bytes 14155780
  68.1 0.9 copy-start.3
  69.0 0.6 copy-start.7
  73.6 20.0 %copy-start.1 = (bf16[512,2048]{1,0:T(8,128)(2,1)S(1)}, bf16[512,2048]{1,0:T(8,128)(2,1)}, u32[]{:S(2)}) copy-start(bf16[512,2048]{1,0:T(8,128)(2,1)} %refs_4_.5) | copy-start | bytes 6291460
  73.6 20.0 %copy-start.6 = (s32[1,576]{1,0:T(1,128)S(1)}, s32[1,576]{1,0:T(1,128)}, u32[]{:S(2)}) copy-start(s32[1,576]{1,0:T(1,128)} %broadcast_in_dim.48.refs_1_) | copy-start | bytes 6916

commit v2 on v1

v2 whole, which is shorter than its diff:
```python
import math

import jax
import jax.numpy as jnp
import numpy as np
from jax import lax
from jax.experimental import pallas as pl
from jax.experimental.pallas import tpu as pltpu
from jax.sharding import PartitionSpec as P

KL = 512
RD = 64
ND = 128
VD = 128
LANES = 128
EPSILON = 1e-06
MASKED = -1e30
FLOOR = -1e29
COARSE = (1, 4, 7)
SCORE_SCALE = math.log2(math.e) / math.sqrt(ND + RD)


def scaled(values, gain):
    mean = jnp.mean(values * values, axis=-1, keepdims=True)
    return values * lax.rsqrt(mean + EPSILON) * gain


def norm_q_kernel(rows_ref, gain_ref, out_ref):
    rows = rows_ref[...].astype(jnp.float32)
    out_ref[...] = scaled(rows, gain_ref[...][None, :]).astype(jnp.bfloat16)


def norm_kv_kernel(rows_ref, gain_ref, out_ref):
    latent = rows_ref[:, :KL].astype(jnp.float32)
    out_ref[:, :KL] = scaled(latent, gain_ref[...][None, :]).astype(jnp.bfloat16)
    out_ref[:, KL:] = rows_ref[:, KL:]


def pair_kernel(spot, own_ref, other_ref, out_ref):
    def lay(even, odd):
        out_ref[:, :KL] = even[:, :KL]
        out_ref[:, KL : 2 * KL] = odd[:, :KL]
        out_ref[:, 2 * KL :] = jnp.concatenate([even[:, KL:], odd[:, KL:]], axis=1)

    @pl.when(spot[1] == 0)
    def _():
        lay(own_ref, other_ref)

    @pl.when(spot[1] != 0)
    def _():
        lay(other_ref, own_ref)


def join_kernel(sizes, n_after, *refs):
    outs = refs[len(refs) - len(sizes) :]
    at = 0
    for size, out_ref in zip(sizes, outs):
        row = 0
        for ref in refs[at : at + size]:
            out_ref[row : row + ref.shape[0], :] = ref[...]
            row += ref.shape[0]
        at += size


def join(groups, after=()):
    sizes = [len(g) for g in groups]
    shapes = [
        jax.ShapeDtypeStruct((sum(a.shape[0] for a in g), g[0].shape[1]), g[0].dtype)
        for g in groups
    ]
    arrays = [a for g in groups for a in g]
    vmem = pl.BlockSpec(memory_space=pltpu.VMEM)
    anywhere = pl.BlockSpec(memory_space=pl.ANY)

    def kernel(*refs):
        join_kernel(sizes, len(after), *refs)

    return pl.pallas_call(
        kernel,
        in_specs=[vmem] * len(arrays) + [anywhere] * len(after),
        out_specs=[vmem] * len(groups),
        out_shape=shapes,
    )(*arrays, *after)


def query_kernel(spot, own, after, before, across, cos_ref, sin_ref, w_ref, out_ref, rows_ref):
    y, xh = spot[2], spot[3]
    for shift, ref in ((0, own), (3, after), (1, before), (2, across)):
        for half in range(2):
            place = lax.rem(y + shift, 4) * 32 + lax.rem(xh + half, 2) * 16
            at = pl.multiple_of(place, 16)
            rows_ref[pl.ds(at, 16), :] = ref[16 * half : 16 * half + 16, :]

    lane = lax.broadcasted_iota(jnp.int32, (rows_ref.shape[0], LANES), 1)

    def rotated(rope):
        turned = jnp.where(
            lane < RD // 2, pltpu.roll(rope, LANES - RD // 2, 1), pltpu.roll(rope, RD // 2, 1)
        )
        return rope * cos_ref[...] + turned * sin_ref[...]

    width = 2 * (ND + RD)
    for pair in range(w_ref.shape[1] // width):
        w = w_ref[:, pair * width : (pair + 1) * width]
        made = jnp.dot(rows_ref[...], w, preferred_element_type=jnp.float32)
        out_ref[2 * pair, :, :ND] = made[:, :ND].astype(jnp.bfloat16)
        out_ref[2 * pair, :, ND:] = rotated(made[:, ND : ND + LANES]).astype(jnp.bfloat16)
        second = ND + RD
        out_ref[2 * pair + 1, :, :ND] = made[:, second : second + ND].astype(jnp.bfloat16)
        rope = pltpu.roll(made[:, second + RD : second + RD + LANES], RD, 1)
        out_ref[2 * pair + 1, :, ND:] = rotated(rope).astype(jnp.bfloat16)


def attend_kernel(n_pieces, shifts, first, last, *refs):
    spot, q_ref, table_ref, w_ref = refs[:4]
    pieces = refs[4 : 4 + n_pieces]
    at = 4 + n_pieces
    if not first:
        max_in, sum_in, acc_in = refs[at : at + 3]
        at += 3
    if last:
        (out_ref,) = refs[at : at + 1]
        at += 1
    else:
        max_out, sum_out, acc_out = refs[at : at + 3]
        at += 3
    rows_ref, rope_ref, bias_ref = refs[at:]
    size = pieces[0].shape[0]

    for n, ref in enumerate(pieces):
        low = pl.ds(n * size, size)
        high = pl.ds((n_pieces + n) * size, size)
        rows_ref[low, :] = ref[:, :KL]
        rows_ref[high, :] = ref[:, KL : 2 * KL]
        rope = ref[:, 2 * KL :]
        rope_ref[low, :] = rope
        rope_ref[high, :] = jnp.concatenate([rope[:, RD:], rope[:, :RD]], axis=1)

    chip, core, y, xh = spot[0], spot[1], spot[2], spot[3]
    tok_dev, n_keys = bias_ref.shape
    query_pos = (2 * chip + core) * tok_dev + lax.broadcasted_iota(jnp.int32, (tok_dev, 1), 0)
    query_start = jnp.zeros_like(query_pos)
    for doc in range(4, spot.shape[0]):
        query_start = jnp.where(query_pos >= spot[doc], spot[doc], query_start)
    ys = jnp.where(
        table_ref[2:3, :] == 0, lax.rem(y + shifts[0], 4), lax.rem(y + shifts[-1], 4)
    )
    xs = jnp.where(table_ref[1:2, :] == 0, lax.rem(xh + core, 2), lax.rem(xh + core + 1, 2))
    key_pos = table_ref[0:1, :] + 2 * chip * tok_dev + ys * 32 + xs * 16
    allowed = (key_pos <= query_pos) & (key_pos >= query_start)
    bias_ref[...] = jnp.where(allowed, 0.0, MASKED)

    for head in range(q_ref.shape[0]):
        w = w_ref[:, head * (ND + VD) : (head + 1) * (ND + VD)]
        expanded = jnp.dot(rows_ref[...], w, preferred_element_type=jnp.float32)
        expanded = expanded.astype(jnp.bfloat16)
        keys = jnp.concatenate([expanded[:, :ND], rope_ref[...]], axis=1)
        scores = lax.dot_general(
            q_ref[head], keys, (((1,), (1,)), ((), ())), preferred_element_type=jnp.float32
        )
        scores = scores * SCORE_SCALE + bias_ref[...]
        top = jnp.max(scores, axis=1, keepdims=True)
        if first:
            new_max = jnp.maximum(top, FLOOR)
        else:
            old_max = max_in[head][:, :1]
            new_max = jnp.maximum(top, old_max)
        weights = jnp.exp2(scores - new_max)
        total = jnp.sum(weights, axis=1, keepdims=True)
        mixed = jnp.dot(
            weights.astype(jnp.bfloat16), expanded[:, ND:], preferred_element_type=jnp.float32
        )
        if not first:
            faded = jnp.exp2(old_max - new_max)
            total = total + faded * sum_in[head][:, :1]
            mixed = mixed + faded * acc_in[head]
        if last:
            out_ref[:, head * VD : (head + 1) * VD] = (mixed / total).astype(jnp.bfloat16)
        else:
            max_out[head] = jnp.broadcast_to(new_max, mixed.shape)
            sum_out[head] = jnp.broadcast_to(total, mixed.shape)
            acc_out[head] = mixed


def key_table(slots, rows, tok_dev, n_sources):
    held = np.concatenate([np.arange(rows) - 2 * k * tok_dev for k in slots])
    columns = []
    for parity in range(2):
        for source in range(n_sources):
            for partner in range(2):
                place = held + parity * tok_dev
                columns.append(np.stack([place, 0 * place + partner, 0 * place + source]))
    return np.concatenate(columns, axis=1).astype(np.int32)


def attend(spot, queries, slots, w_kv, pieces, shifts, state, last):
    heads, rows, width = queries.shape
    first = state is None
    table = jnp.asarray(key_table(slots, 16, rows, len(shifts)))
    count = table.shape[1]
    vmem = pl.BlockSpec(memory_space=pltpu.VMEM)
    args = [spot, queries, table, w_kv, *pieces]
    if not first:
        args += list(state)
    if last:
        out_shape = jax.ShapeDtypeStruct((rows, heads * VD), jnp.bfloat16)
        out_specs = vmem
    else:
        out_shape = [jax.ShapeDtypeStruct((heads, rows, VD), jnp.float32)] * 3
        out_specs = [vmem] * 3

    def kernel(*refs):
        attend_kernel(len(pieces), shifts, first, last, *refs)

    return pl.pallas_call(
        kernel,
        in_specs=[pl.BlockSpec(memory_space=pltpu.SMEM)] + [vmem] * (len(args) - 1),
        out_specs=out_specs,
        out_shape=out_shape,
        scratch_shapes=[
            pltpu.VMEM((count, KL), jnp.bfloat16),
            pltpu.VMEM((count, LANES), jnp.bfloat16),
            pltpu.VMEM((rows, count), jnp.float32),
        ],
        compiler_params=pltpu.CompilerParams(vmem_limit_bytes=48 * 2**20),
    )(*args)


def body(q_latent, q_gain, kv_cache, kv_gain, w_query, w_kv, doc_lengths):
    ctx_size, head_size = lax.axis_size("ctx"), lax.axis_size("head")
    chips, ys = ctx_size // 2, head_size // 2
    tok_dev = q_latent.shape[0] * head_size
    heads_here = w_query.shape[1] // (ND + RD)
    ctx, head = lax.axis_index("ctx"), lax.axis_index("head")
    smem, vmem = pl.BlockSpec(memory_space=pltpu.SMEM), pl.BlockSpec(memory_space=pltpu.VMEM)

    swap = [(n, n ^ 1) for n in range(ctx_size)]
    across_x = [(n, n ^ 1) for n in range(head_size)]

    def chip_shift(step):
        return [(2 * n + c, 2 * ((n + step) % chips) + c) for n in range(chips) for c in range(2)]

    def coarse_shift(step):
        return [
            ((2 * n + c) * head_size + h, (2 * ((n + step) % chips) + c) * head_size + (h ^ c))
            for n in range(chips)
            for c in range(2)
            for h in range(head_size)
        ]

    def y_shift(step):
        return [(2 * n + x, 2 * ((n + step) % ys) + x) for n in range(ys) for x in range(2)]

    ends = [doc_lengths[0]]
    for doc in range(1, doc_lengths.shape[0]):
        ends.append(ends[-1] + doc_lengths[doc])
    spot = jnp.stack([ctx // 2, ctx % 2, head // 2, head % 2, *ends])

    kv_rows = pl.pallas_call(
        norm_kv_kernel, out_shape=jax.ShapeDtypeStruct(kv_cache.shape, jnp.bfloat16)
    )(kv_cache, kv_gain)
    kv_other = lax.ppermute(kv_rows, "ctx", swap)
    piece = pl.pallas_call(
        pair_kernel,
        in_specs=[smem, vmem, vmem],
        out_specs=vmem,
        out_shape=jax.ShapeDtypeStruct((kv_rows.shape[0], 2 * kv_rows.shape[1]), jnp.bfloat16),
    )(spot, kv_rows, kv_other)
    coarse = [lax.ppermute(piece, ("ctx", "head"), coarse_shift(step)) for step in COARSE]

    q_rows = pl.pallas_call(
        norm_q_kernel, out_shape=jax.ShapeDtypeStruct(q_latent.shape, jnp.bfloat16)
    )(q_latent, q_gain)
    q_other = lax.ppermute(q_rows, "head", across_x)

    coarse, q_pair = join([coarse, [q_rows, q_other]])
    later = lax.ppermute(coarse, "ctx", chip_shift(1))
    sooner = lax.ppermute(coarse, "ctx", chip_shift(-1))
    q_after = lax.ppermute(q_pair, "head", y_shift(1))
    q_before = lax.ppermute(q_pair, "head", y_shift(-1))
    q_across = lax.ppermute(q_pair, "head", y_shift(2))

    slots = [*COARSE, *[k + 1 for k in COARSE], *[k - 1 for k in COARSE]]
    (held,) = join([[coarse, later, sooner]], after=[q_after, q_before, q_across])
    from_after = lax.ppermute(held, "head", y_shift(1))
    from_before = lax.ppermute(held, "head", y_shift(-1))
    from_across = lax.ppermute(held, "head", y_shift(2))
    own_swapped = lax.ppermute(held, "ctx", swap)

    query_pos = ctx * tok_dev + jnp.arange(tok_dev, dtype=jnp.int32)
    query_start = jnp.zeros_like(query_pos)
    for end in ends:
        query_start = jnp.where(query_pos >= end, end, query_start)
    freq_index = jnp.arange(RD // 2, dtype=jnp.float32)
    frequency = jnp.exp(freq_index * (-2.0 * math.log(10000.0) / RD))
    angles = (query_pos - query_start).astype(jnp.float32)[:, None] * frequency[None, :]
    cosine, sine = jnp.cos(angles), jnp.sin(angles)
    blank = jnp.zeros((tok_dev, LANES - RD), jnp.float32)
    cos_table = jnp.concatenate([cosine, cosine, blank], axis=1)
    sin_table = jnp.concatenate([-sine, sine, blank], axis=1)

    queries = pl.pallas_call(
        query_kernel,
        in_specs=[smem] + [vmem] * 7,
        out_specs=vmem,
        out_shape=jax.ShapeDtypeStruct((heads_here, tok_dev, 2 * LANES), jnp.bfloat16),
        scratch_shapes=[pltpu.VMEM((tok_dev, w_query.shape[0]), jnp.bfloat16)],
        compiler_params=pltpu.CompilerParams(vmem_limit_bytes=48 * 2**20),
    )(spot, q_pair, q_after, q_before, q_across, cos_table, sin_table, w_query)

    state = attend(spot, queries, slots, w_kv, [held, own_swapped], [0], None, False)
    after_swapped = lax.ppermute(from_after, "ctx", swap)
    before_swapped = lax.ppermute(from_before, "ctx", swap)
    near = [from_after, after_swapped, from_before, before_swapped]
    state = attend(spot, queries, slots, w_kv, near, [3, 1], state, False)
    across_swapped = lax.ppermute(from_across, "ctx", swap)
    return attend(spot, queries, slots, w_kv, [from_across, across_swapped], [2], state, True)


def solution(mesh):
    placed = (
        P(("ctx", "head"), None),
        P(),
        P(("ctx", "head"), None),
        P(),
        P(None, "head"),
        P(None, "head"),
        P(),
    )
    return jax.shard_map(
        body, mesh=mesh, in_specs=placed, out_specs=P("ctx", "head"), check_vma=False
    )
```

time: 104 us -> 102 us (0.981)
  waiting for transfers between devices: 10.6 us -> 17.6 us
  other arithmetic: 7.05 us -> 1.06 us
  local copies, waits for them, and re-layouts: 15.7 us -> 11.9 us
  Pallas kernels: 34.8 us -> 36.1 us
    ppermute x1, starting transfers between devices: 6.59 us -> 1.53 us  [body(): own_swapped = lax.ppermute(held, 'ctx', swap)]
    ppermute x6, starting transfers between devices: 13.8 us -> 18.8 us  [the longest x3 12 us: body(): lax.ppermute(piece, ('ctx', 'head'), coarse_shift(step))]
    ppermute x1, waiting for transfers between devices: 0.01 us -> 4.99 us  [body(): from_across = lax.ppermute(held, 'head', y_shift(2))]
    ppermute x1, waiting for transfers between devices: 0.01 us -> 4.78 us  [body(): from_after = lax.ppermute(held, 'head', y_shift(1))]
    broadcast_in_dim x4 -> x0, local copies, waits for them, and re-layouts: 3.91 us -> none  [the longest x3 2.47 us: key_positions(): return jnp.concatenate(halves)[None, :]]
    unnamed x20 -> x44, local copies, waits for them, and re-layouts: 5.32 us -> 9.1 us
    add x2 -> x0, other arithmetic: 3.23 us -> none  [the longest x1 1.88 us: body(): query_start + jnp.where(query_pos >= doc_end, doc_lengths[doc], 0)]
    concatenate x4 -> x0, local copies, waits for them, and re-layouts: 2.9 us -> none  [the longest x1 1.43 us: body(): q_pair = jnp.concatenate([q_rows, q_other], axis=0)]
  transfers between devices with their start and end apart: 17 -> 17, of which waited for: 6 -> 6; matrix products, arithmetic and copies ran while one was open for 17% -> 4% of each run, Pallas kernels for 23% -> 23%
where the time goes in v2:
time: 102 us
  Pallas kernels  36.1 us (35%)
  starting transfers between devices  32.9 us (32%)
  waiting for transfers between devices  17.6 us (17%)
  local copies, waits for them, and re-layouts  11.9 us (12%)
  between operations  2.18 us (2%)
  other arithmetic  1.06 us (1%)
    pallas_call x3, Pallas kernels, attend(): pl.pallas_call(kernel, in_specs=[pl.BlockSpec(memory_space=pltpu.SMEM)] +...  26.5 us
    ppermute x3, starting transfers between devices, body(): lax.ppermute(piece, ('ctx', 'head'), coarse_shift(step))  12 us
    unnamed x44, local copies, waits for them, and re-layouts  9.1 us
    ppermute x1, waiting for transfers between devices, body(): from_across = lax.ppermute(held, 'head', y_shift(2))  4.99 us
    ppermute x1, waiting for transfers between devices, body(): from_after = lax.ppermute(held, 'head', y_shift(1))  4.78 us
    pallas_call x2, Pallas kernels, join(): pl.pallas_call(kernel, in_specs=[vmem] * len(arrays) + [anywhere] * len(a...  3.3 us
    ppermute x1, starting transfers between devices, body(): kv_other = lax.ppermute(kv_rows, 'ctx', swap)  3.24 us
    ppermute x3, waiting for transfers between devices, body(): lax.ppermute(piece, ('ctx', 'head'), coarse_shift(step))  3.18 us
  transfers between devices with their start and end apart: 17, of which 6 were waited for; matrix products, arithmetic and copies ran while one was open for 4% of the time, Pallas kernels for 23%

profile of v2, /device:TPU:1, one launch (start us, length us, event | category | flops | bytes accessed | tf_op | source)
XLA Modules:
  0.0 101.8 jit_solution(5331263436687318639)
XLA Ops:
  0.0 1.6 %shard_map.100.own_ref = bf16[16,576]{1,0:T(8,128)(2,1)} custom-call(bf16[16,576]{1,0:T(8,128)(2,1)} %rows_ref.2, f32[512]{0:T(512)} %gain_ref.2), custom_call_target="tpu_custom_call" | custom-call | tf_op jit(solution)/shard_map/pallas_call | solution.py:259
  1.6 3.2 %collective-permute-start = (bf16[16,576]{1,0:T(8,128)(2,1)}, bf16[16,576]{1,0:T(8,128)(2,1)S(1)}, u32[]{:S(2)}, u32[]{:S(2)}) collective-permute-start(bf16[16,576]{1,0:T(8,128)(2,1)} %shard_map.100.own_ref), channel_id=1, source_target_pairs={{0,8},{8,0},{16,24},{24,16},{32,40},{40,32},{48,56},{56,48},{64,72... | collective-permute-start | bytes 55304 | tf_op jit(solution)/shard_map/ppermute | solution.py:262
  4.8 1.5 %shard_map.102.refs_3_ = bf16[16,1536]{1,0:T(8,128)(2,1)} custom-call(bf16[16,1536]{1,0:T(8,128)(2,1)} %rows_ref.3, f32[1536]{0:T(1024)} %gain_ref.3), custom_call_target="tpu_custom_call" | custom-call | tf_op jit(solution)/shard_map/pallas_call | solution.py:271
  6.3 1.0 collective-permute-start.4
  7.3 1.4 %fusion.3 = (s32[1]{0:T(128)}, s32[1]{0:T(128)}, s32[1]{0:T(128)}) fusion(s32[3]{0:T(128)} %param.16), kind=kLoop, calls=%fused_computation.11 | loop fusion | bytes 24 | tf_op jit(solution)/shard_map/slice | solution.py:256
  10.7 1.3 %stack.27.spot.refs_0_ = s32[7]{0:T(128)} concatenate(s32[1]{0:T(128)} %bitcast, s32[1]{0:T(128)} %bitcast.1, s32[1]{0:T(128)} %bitcast.2, s32[1]{0:T(128)} %bitcast.3, s32[1]{0:T(128)} %get-tuple-element.27, s32[1]{0:T(128)} %bitcast.6, s32[1]{0:T(128)} %bitcast.8), dimensions={0} | concatenate | bytes 56 | tf_op jit(solution)/shard_map/stack | solution.py:257
  12.0 0.0 collective-permute-done.other_ref
  12.0 0.6 copy-done.21
  12.6 1.5 %shard_map.101 = bf16[16,1152]{1,0:T(8,128)(2,1)} custom-call(s32[7]{0:T(128)} %stack.27.spot.refs_0_, bf16[16,576]{1,0:T(8,128)(2,1)} %shard_map.100.own_ref, bf16[16,576]{1,0:T(8,128)(2,1)} %copy-done.21), custom_call_target="tpu_custom_call" | custom-call | tf_op jit(solution)/shard_map/pallas_call | solution.py:263
  14.1 1.6 %collective-permute-start.1 = (bf16[16,1152]{1,0:T(8,128)(2,1)}, bf16[16,1152]{1,0:T(8,128)(2,1)S(1)}, u32[]{:S(2)}, u32[]{:S(2)}) collective-permute-start(bf16[16,1152]{1,0:T(8,128)(2,1)} %shard_map.101), channel_id=1, source_target_pairs={{0,16},{1,17},{2,18},{3,19},{4,20},{5,21},{6,22},{7,23},{8,25},{9,... | collective-permute-start | bytes 110600 | tf_op jit(solution)/shard_map/ppermute | solution.py:269
  15.6 8.5 %collective-permute-start.2 = (bf16[16,1152]{1,0:T(8,128)(2,1)}, bf16[16,1152]{1,0:T(8,128)(2,1)S(1)}, u32[]{:S(2)}, u32[]{:S(2)}) collective-permute-start(bf16[16,1152]{1,0:T(8,128)(2,1)} %shard_map.101), channel_id=1, source_target_pairs={{0,64},{1,65},{2,66},{3,67},{4,68},{5,69},{6,70},{7,71},{8,73},{9,... | collective-permute-start | bytes 110600 | tf_op jit(solution)/shard_map/ppermute | solution.py:269
  24.1 1.9 %collective-permute-start.3 = (bf16[16,1152]{1,0:T(8,128)(2,1)}, bf16[16,1152]{1,0:T(8,128)(2,1)S(1)}, u32[]{:S(2)}, u32[]{:S(2)}) collective-permute-start(bf16[16,1152]{1,0:T(8,128)(2,1)} %shard_map.101), channel_id=1, source_target_pairs={{0,112},{1,113},{2,114},{3,115},{4,116},{5,117},{6,118},{7,119},{8... | collective-permute-start | bytes 110600 | tf_op jit(solution)/shard_map/ppermute | solution.py:269
  26.0 0.0 collective-permute-done.4.refs_4_
  26.0 0.0 collective-permute-done.1.refs_0_
  26.0 0.0 copy-start.18
  26.0 0.0 collective-permute-done.2.refs_1_
  26.1 3.2 %collective-permute-done.3.refs_2_ = bf16[16,1152]{1,0:T(8,128)(2,1)S(1)} collective-permute-done((bf16[16,1152]{1,0:T(8,128)(2,1)}, bf16[16,1152]{1,0:T(8,128)(2,1)S(1)}, u32[]{:S(2)}, u32[]{:S(2)}) %collective-permute-start.3) | collective-permute-done | bytes 36896 | tf_op jit(solution)/shard_map/ppermute | solution.py:269
  29.2 0.0 copy-done.18
  29.3 0.6 copy-done.20
  29.9 1.6 %shard_map.103 = (bf16[48,1152]{1,0:T(8,128)(2,1)}, bf16[32,1536]{1,0:T(8,128)(2,1)}) custom-call(bf16[16,1152]{1,0:T(8,128)(2,1)} %copy-done.18, bf16[16,1152]{1,0:T(8,128)(2,1)} %copy-done.19, bf16[16,1152]{1,0:T(8,128)(2,1)} %copy-done.20, bf16[16,1536]{1,0:T(8,128)(2,1)} %shard_map.102.refs_3_, bf16[16,1536]{1,0:T(8,128)(2,1)} %copy-done.17), custom_call_target="tpu_custom_call" | custom-call | tf_op jit(solution)/shard_map/pallas_call | solution.py:78
  31.4 0.7 collective-permute-start.8
  32.1 2.8 %collective-permute-start.9 = (bf16[48,1152]{1,0:T(8,128)(2,1)}, bf16[48,1152]{1,0:T(8,128)(2,1)S(1)}, u32[]{:S(2)}, u32[]{:S(2)}) collective-permute-start(bf16[48,1152]{1,0:T(8,128)(2,1)} %get-tuple-element.14.refs_0_), channel_id=1, source_target_pairs={{0,240},{8,248},{16,0},{24,8},{32,16},{40,24},{48,32},{56,40},{64,... | collective-permute-start | bytes 331784 | tf_op jit(solution)/shard_map/ppermute | solution.py:278
  35.0 1.3 %collective-permute-start.5 = (bf16[32,1536]{1,0:T(8,128)(2,1)}, bf16[32,1536]{1,0:T(8,128)(2,1)S(1)}, u32[]{:S(2)}, u32[]{:S(2)}) collective-permute-start(bf16[32,1536]{1,0:T(8,128)(2,1)} %get-tuple-element.13.own), channel_id=1, source_target_pairs={{0,2},{1,3},{2,4},{3,5},{4,6},{5,7},{6,0},{7,1},{8,10},{9,11},{10,... | collective-permute-start | bytes 294920 | tf_op jit(solution)/shard_map/ppermute | solution.py:279
  36.3 1.4 %collective-permute-start.6 = (bf16[32,1536]{1,0:T(8,128)(2,1)}, bf16[32,1536]{1,0:T(8,128)(2,1)S(1)}, u32[]{:S(2)}, u32[]{:S(2)}) collective-permute-start(bf16[32,1536]{1,0:T(8,128)(2,1)} %get-tuple-element.13.own), channel_id=1, source_target_pairs={{0,6},{1,7},{2,0},{3,1},{4,2},{5,3},{6,4},{7,5},{8,14},{9,15},{10,... | collective-permute-start | bytes 294920 | tf_op jit(solution)/shard_map/ppermute | solution.py:280
  37.7 1.6 %collective-permute-start.7 = (bf16[32,1536]{1,0:T(8,128)(2,1)}, bf16[32,1536]{1,0:T(8,128)(2,1)S(1)}, u32[]{:S(2)}, u32[]{:S(2)}) collective-permute-start(bf16[32,1536]{1,0:T(8,128)(2,1)} %get-tuple-element.13.own), channel_id=1, source_target_pairs={{0,4},{1,5},{2,6},{3,7},{4,0},{5,1},{6,2},{7,3},{8,12},{9,13},{10,... | collective-permute-start | bytes 294920 | tf_op jit(solution)/shard_map/ppermute | solution.py:281
  39.4 1.3 %collective-permute-done.5.after.refs_3_ = bf16[32,1536]{1,0:T(8,128)(2,1)S(1)} collective-permute-done((bf16[32,1536]{1,0:T(8,128)(2,1)}, bf16[32,1536]{1,0:T(8,128)(2,1)S(1)}, u32[]{:S(2)}, u32[]{:S(2)}) %collective-permute-start.5) | collective-permute-done | bytes 98336 | tf_op jit(solution)/shard_map/ppermute | solution.py:279
  40.6 0.6 collective-permute-done.6.before.refs_4_
  41.2 2.8 %collective-permute-done.7.across.refs_5_ = bf16[32,1536]{1,0:T(8,128)(2,1)S(1)} collective-permute-done((bf16[32,1536]{1,0:T(8,128)(2,1)}, bf16[32,1536]{1,0:T(8,128)(2,1)S(1)}, u32[]{:S(2)}, u32[]{:S(2)}) %collective-permute-start.7) | collective-permute-done | bytes 98336 | tf_op jit(solution)/shard_map/ppermute | solution.py:281
  44.0 0.0 collective-permute-done.8.refs_1_
  44.0 0.0 collective-permute-done.9.refs_2_
  44.0 0.6 copy-done.8
  44.6 0.0 copy-done.15
  44.7 0.6 copy-done.16
  45.3 1.8 %shard_map.105.refs_4_ = bf16[144,1152]{1,0:T(8,128)(2,1)} custom-call(bf16[48,1152]{1,0:T(8,128)(2,1)} %get-tuple-element.14.refs_0_, bf16[48,1152]{1,0:T(8,128)(2,1)} %copy-done.15, bf16[48,1152]{1,0:T(8,128)(2,1)} %copy-done.16, bf16[32,1536]{1,0:T(8,128)(2,1)} %copy-done.4, bf16[32,1536]{1,0:T(8,128)(2,1)} %copy-done.6, bf16[32,1536]{1,0:T(8,128)(2,1)} %copy-done.8), custom_call_target="tpu_custom_call" | custom-call | tf_op jit(solution)/shard_map/pallas_call | solution.py:78
  47.1 1.4 %collective-permute-start.12 = (bf16[144,1152]{1,0:T(8,128)(2,1)}, bf16[144,1152]{1,0:T(8,128)(2,1)S(1)}, u32[]{:S(2)}, u32[]{:S(2)}) collective-permute-start(bf16[144,1152]{1,0:T(8,128)(2,1)} %shard_map.105.refs_4_), channel_id=1, source_target_pairs={{0,2},{1,3},{2,4},{3,5},{4,6},{5,7},{6,0},{7,1},{8,10},{9,11},{10,... | collective-permute-start | bytes 995336 | tf_op jit(solution)/shard_map/ppermute | solution.py:285
  48.4 1.3 %collective-permute-start.14 = (bf16[144,1152]{1,0:T(8,128)(2,1)}, bf16[144,1152]{1,0:T(8,128)(2,1)S(1)}, u32[]{:S(2)}, u32[]{:S(2)}) collective-permute-start(bf16[144,1152]{1,0:T(8,128)(2,1)} %shard_map.105.refs_4_), channel_id=1, source_target_pairs={{0,6},{1,7},{2,0},{3,1},{4,2},{5,3},{6,4},{7,5},{8,14},{9,15},{10,... | collective-permute-start | bytes 995336 | tf_op jit(solution)/shard_map/ppermute | solution.py:286
  49.8 0.5 collective-permute-start.10
  50.2 0.6 fusion.2
  50.9 1.5 %collective-permute-start.16 = (bf16[144,1152]{1,0:T(8,128)(2,1)}, bf16[144,1152]{1,0:T(8,128)(2,1)S(1)}, u32[]{:S(2)}, u32[]{:S(2)}) collective-permute-start(bf16[144,1152]{1,0:T(8,128)(2,1)} %shard_map.105.refs_4_), channel_id=1, source_target_pairs={{0,8},{8,0},{16,24},{24,16},{32,40},{40,32},{48,56},{56,48},{64,72... | collective-permute-start | bytes 995336 | tf_op jit(solution)/shard_map/ppermute | solution.py:288
  52.4 4.8 %collective-permute-done.12.refs_4_ = bf16[144,1152]{1,0:T(8,128)(2,1)S(1)} collective-permute-done((bf16[144,1152]{1,0:T(8,128)(2,1)}, bf16[144,1152]{1,0:T(8,128)(2,1)S(1)}, u32[]{:S(2)}, u32[]{:S(2)}) %collective-permute-start.12) | collective-permute-done | bytes 331808 | tf_op jit(solution)/shard_map/ppermute | solution.py:285
  57.2 1.9 %collective-permute-start.13 = (bf16[144,1152]{1,0:T(8,128)(2,1)S(1)}, bf16[144,1152]{1,0:T(8,128)(2,1)S(1)}, u32[]{:S(2)}, u32[]{:S(2)}) collective-permute-start(bf16[144,1152]{1,0:T(8,128)(2,1)S(1)} %collective-permute-done.12.refs_4_), channel_id=1, source_target_pairs={{0,8},{8,0},{16,24},{24,16},{32,40},{40,32},{48,56},{56,48},{64,72... | collective-permute-start | bytes 995336 | tf_op jit(solution)/shard_map/ppermute | solution.py:312
  59.1 0.0 collective-permute-done.14.refs_6_
  59.1 0.9 collective-permute-start.15
  60.0 5.0 %collective-permute-done.10.refs_4_ = bf16[144,1152]{1,0:T(8,128)(2,1)S(1)} collective-permute-done((bf16[144,1152]{1,0:T(8,128)(2,1)}, bf16[144,1152]{1,0:T(8,128)(2,1)S(1)}, u32[]{:S(2)}, u32[]{:S(2)}) %collective-permute-start.10) | collective-permute-done | bytes 331808 | tf_op jit(solution)/shard_map/ppermute | solution.py:287
  65.0 1.2 %collective-permute-start.11 = (bf16[144,1152]{1,0:T(8,128)(2,1)S(1)}, bf16[144,1152]{1,0:T(8,128)(2,1)S(1)}, u32[]{:S(2)}, u32[]{:S(2)}) collective-permute-start(bf16[144,1152]{1,0:T(8,128)(2,1)S(1)} %collective-permute-done.10.refs_4_), channel_id=1, source_target_pairs={{0,8},{8,0},{16,24},{24,16},{32,40},{40,32},{48,56},{56,48},{64,72... | collective-permute-start | bytes 995336 | tf_op jit(solution)/shard_map/ppermute | solution.py:316
  66.2 0.3 fusion
  66.6 0.1 pad.5.clone
  66.6 0.1 maximum_maximum_fusion.1
  66.7 0.0 copy-start.2
  66.8 2.3 %copy-done.2 = bf16[1536,1536]{1,0:T(8,128)(2,1)S(1)} copy-done((bf16[1536,1536]{1,0:T(8,128)(2,1)S(1)}, bf16[1536,1536]{1,0:T(8,128)(2,1)}, u32[]{:S(2)}) %copy-start.2) | copy-done | bytes 4718616
  69.1 0.9 copy-done.5
  70.0 0.9 copy-done.7
  70.9 0.9 copy-done.9
  71.8 0.9 copy-done.10
  72.7 0.7 copy-done.13
  73.3 1.8 %shard_map.104.refs_1_ = bf16[8,128,256]{2,1,0:T(8,128)(2,1)S(1)} custom-call(s32[7]{0:T(128)S(1)} %copy-done.13, bf16[32,1536]{1,0:T(8,128)(2,1)S(1)} %copy-done.10, bf16[32,1536]{1,0:T(8,128)(2,1)S(1)} %copy-done.5, bf16[32,1536]{1,0:T(8,128)(2,1)S(1)} %copy-done.7, bf16[32,1536]{1,0:T(8,128)(2,1)S(1)} %copy-done.9, ...), custom_call_target="tpu_custom_call" | custom-call | tf_op jit(solution)/shard_map/pallas_call | solution.py:302
  75.1 0.0 copy-start.1
  75.1 0.0 collective-permute-done.16.refs_5_
  75.1 6.7 %shard_map.106 = (f32[8,128,128]{2,1,0:T(8,128)S(1)}, f32[8,128,128]{2,1,0:T(8,128)S(1)}, f32[8,128,128]{2,1,0:T(8,128)S(1)}) custom-call(s32[7]{0:T(128)S(1)} %copy-done.13, bf16[8,128,256]{2,1,0:T(8,128)(2,1)S(1)} %shard_map.104.refs_1_, s32[3,576]{1,0:T(4,128)S(1)} %copy-done.11, bf16[512,2048]{1,0:T(8,128)(2,1)S(1)} %copy-done, ...), custom_call_target="tpu_custom_call" | custom-call | tf_op jit(solution)/shard_map/pallas_call | solution.py:215
  81.9 0.0 collective-permute-done.13.refs_5_
  81.9 0.0 collective-permute-done.15.refs_7_
  81.9 11.7 %shard_map.107 = (f32[8,128,128]{2,1,0:T(8,128)S(1)}, f32[8,128,128]{2,1,0:T(8,128)S(1)}, f32[8,128,128]{2,1,0:T(8,128)S(1)}) custom-call(s32[7]{0:T(128)S(1)} %copy-done.14, bf16[8,128,256]{2,1,0:T(8,128)(2,1)S(1)} %shard_map.104.refs_1_, s32[3,1152]{1,0:T(4,128)S(1)} %copy-done.12, bf16[512,2048]{1,0:T(8,128)(2,1)} %refs_3_.5, ...), custom_call_target="tpu_custom_call" | custom-call | tf_op jit(solution)/shard_map/pallas_call | solution.py:215
  93.6 0.0 collective-permute-done.11.refs_5_
  93.7 8.1 %shard_map.108 = bf16[128,1024]{1,0:T(8,128)(2,1)} custom-call(s32[7]{0:T(128)S(1)} %copy-done.14, bf16[8,128,256]{2,1,0:T(8,128)(2,1)S(1)} %shard_map.104.refs_1_, s32[3,576]{1,0:T(4,128)S(1)} %copy-done.11, bf16[512,2048]{1,0:T(8,128)(2,1)S(1)} %copy-done.1, bf16[144,1152]{1,0:T(8,128)(2,1)S(1)} %collective-permute-done.10.refs_4_, ...), custom_call_target="tpu_custom_call" | custom-call | tf_op jit(solution)/shard_map/pallas_call | solution.py:215
  (31 shorter events, 0.1 us)
Async XLA Ops:
  0.0 75.1 %copy-start = (bf16[512,2048]{1,0:T(8,128)(2,1)S(1)}, bf16[512,2048]{1,0:T(8,128)(2,1)}, u32[]{:S(2)}) copy-start(bf16[512,2048]{1,0:T(8,128)(2,1)} %refs_3_.5) | copy-start | bytes 6291460
  1.6 10.4 %collective-permute-start = (bf16[16,576]{1,0:T(8,128)(2,1)}, bf16[16,576]{1,0:T(8,128)(2,1)S(1)}, u32[]{:S(2)}, u32[]{:S(2)}) collective-permute-start(bf16[16,576]{1,0:T(8,128)(2,1)} %shard_map.100.own_ref), channel_id=1, source_target_pairs={{0,8},{8,0},{16,24},{24,16},{32,40},{40,32},{48,56},{56,48},{64,72... | collective-permute-start | bytes 55304 | tf_op jit(solution)/shard_map/ppermute | solution.py:262
  6.3 19.7 %collective-permute-start.4 = (bf16[16,1536]{1,0:T(8,128)(2,1)}, bf16[16,1536]{1,0:T(8,128)(2,1)S(1)}, u32[]{:S(2)}, u32[]{:S(2)}) collective-permute-start(bf16[16,1536]{1,0:T(8,128)(2,1)} %shard_map.102.refs_3_), channel_id=1, source_target_pairs={{0,1},{1,0},{2,3},{3,2},{4,5},{5,4},{6,7},{7,6},{8,9},{9,8},{10,11... | collective-permute-start | bytes 147464 | tf_op jit(solution)/shard_map/ppermute | solution.py:274
  12.0 0.6 copy-start.21
  14.1 12.0 %collective-permute-start.1 = (bf16[16,1152]{1,0:T(8,128)(2,1)}, bf16[16,1152]{1,0:T(8,128)(2,1)S(1)}, u32[]{:S(2)}, u32[]{:S(2)}) collective-permute-start(bf16[16,1152]{1,0:T(8,128)(2,1)} %shard_map.101), channel_id=1, source_target_pairs={{0,16},{1,17},{2,18},{3,19},{4,20},{5,21},{6,22},{7,23},{8,25},{9,... | collective-permute-start | bytes 110600 | tf_op jit(solution)/shard_map/ppermute | solution.py:269
  15.6 10.4 %collective-permute-start.2 = (bf16[16,1152]{1,0:T(8,128)(2,1)}, bf16[16,1152]{1,0:T(8,128)(2,1)S(1)}, u32[]{:S(2)}, u32[]{:S(2)}) collective-permute-start(bf16[16,1152]{1,0:T(8,128)(2,1)} %shard_map.101), channel_id=1, source_target_pairs={{0,64},{1,65},{2,66},{3,67},{4,68},{5,69},{6,70},{7,71},{8,73},{9,... | collective-permute-start | bytes 110600 | tf_op jit(solution)/shard_map/ppermute | solution.py:269
  24.1 5.1 %collective-permute-start.3 = (bf16[16,1152]{1,0:T(8,128)(2,1)}, bf16[16,1152]{1,0:T(8,128)(2,1)S(1)}, u32[]{:S(2)}, u32[]{:S(2)}) collective-permute-start(bf16[16,1152]{1,0:T(8,128)(2,1)} %shard_map.101), channel_id=1, source_target_pairs={{0,112},{1,113},{2,114},{3,115},{4,116},{5,117},{6,118},{7,119},{8... | collective-permute-start | bytes 110600 | tf_op jit(solution)/shard_map/ppermute | solution.py:269
  26.0 3.2 %copy-start.17 = (bf16[16,1536]{1,0:T(8,128)(2,1)}, bf16[16,1536]{1,0:T(8,128)(2,1)S(1)}, u32[]{:S(2)}) copy-start(bf16[16,1536]{1,0:T(8,128)(2,1)S(1)} %collective-permute-done.4.refs_4_) | copy-start | bytes 147460
  26.0 3.2 %copy-start.18 = (bf16[16,1152]{1,0:T(8,128)(2,1)}, bf16[16,1152]{1,0:T(8,128)(2,1)S(1)}, u32[]{:S(2)}) copy-start(bf16[16,1152]{1,0:T(8,128)(2,1)S(1)} %collective-permute-done.1.refs_0_) | copy-start | bytes 110596
  26.0 3.2 %copy-start.19 = (bf16[16,1152]{1,0:T(8,128)(2,1)}, bf16[16,1152]{1,0:T(8,128)(2,1)S(1)}, u32[]{:S(2)}) copy-start(bf16[16,1152]{1,0:T(8,128)(2,1)S(1)} %collective-permute-done.2.refs_1_) | copy-start | bytes 110596
  29.2 0.6 copy-start.20
  31.4 12.6 %collective-permute-start.8 = (bf16[48,1152]{1,0:T(8,128)(2,1)}, bf16[48,1152]{1,0:T(8,128)(2,1)S(1)}, u32[]{:S(2)}, u32[]{:S(2)}) collective-permute-start(bf16[48,1152]{1,0:T(8,128)(2,1)} %get-tuple-element.14.refs_0_), channel_id=1, source_target_pairs={{0,16},{8,24},{16,32},{24,40},{32,48},{40,56},{48,64},{56,72},{64,... | collective-permute-start | bytes 331784 | tf_op jit(solution)/shard_map/ppermute | solution.py:277
  32.1 11.9 %collective-permute-start.9 = (bf16[48,1152]{1,0:T(8,128)(2,1)}, bf16[48,1152]{1,0:T(8,128)(2,1)S(1)}, u32[]{:S(2)}, u32[]{:S(2)}) collective-permute-start(bf16[48,1152]{1,0:T(8,128)(2,1)} %get-tuple-element.14.refs_0_), channel_id=1, source_target_pairs={{0,240},{8,248},{16,0},{24,8},{32,16},{40,24},{48,32},{56,40},{64,... | collective-permute-start | bytes 331784 | tf_op jit(solution)/shard_map/ppermute | solution.py:278
  35.0 5.6 %collective-permute-start.5 = (bf16[32,1536]{1,0:T(8,128)(2,1)}, bf16[32,1536]{1,0:T(8,128)(2,1)S(1)}, u32[]{:S(2)}, u32[]{:S(2)}) collective-permute-start(bf16[32,1536]{1,0:T(8,128)(2,1)} %get-tuple-element.13.own), channel_id=1, source_target_pairs={{0,2},{1,3},{2,4},{3,5},{4,6},{5,7},{6,0},{7,1},{8,10},{9,11},{10,... | collective-permute-start | bytes 294920 | tf_op jit(solution)/shard_map/ppermute | solution.py:279
  36.3 5.0 %collective-permute-start.6 = (bf16[32,1536]{1,0:T(8,128)(2,1)}, bf16[32,1536]{1,0:T(8,128)(2,1)S(1)}, u32[]{:S(2)}, u32[]{:S(2)}) collective-permute-start(bf16[32,1536]{1,0:T(8,128)(2,1)} %get-tuple-element.13.own), channel_id=1, source_target_pairs={{0,6},{1,7},{2,0},{3,1},{4,2},{5,3},{6,4},{7,5},{8,14},{9,15},{10,... | collective-permute-start | bytes 294920 | tf_op jit(solution)/shard_map/ppermute | solution.py:280
  37.7 6.3 %collective-permute-start.7 = (bf16[32,1536]{1,0:T(8,128)(2,1)}, bf16[32,1536]{1,0:T(8,128)(2,1)S(1)}, u32[]{:S(2)}, u32[]{:S(2)}) collective-permute-start(bf16[32,1536]{1,0:T(8,128)(2,1)} %get-tuple-element.13.own), channel_id=1, source_target_pairs={{0,4},{1,5},{2,6},{3,7},{4,0},{5,1},{6,2},{7,3},{8,12},{9,13},{10,... | collective-permute-start | bytes 294920 | tf_op jit(solution)/shard_map/ppermute | solution.py:281
  40.6 3.4 %copy-start.4 = (bf16[32,1536]{1,0:T(8,128)(2,1)}, bf16[32,1536]{1,0:T(8,128)(2,1)S(1)}, u32[]{:S(2)}) copy-start(bf16[32,1536]{1,0:T(8,128)(2,1)S(1)} %collective-permute-done.5.after.refs_3_) | copy-start | bytes 294916
  41.2 2.8 %copy-start.6 = (bf16[32,1536]{1,0:T(8,128)(2,1)}, bf16[32,1536]{1,0:T(8,128)(2,1)S(1)}, u32[]{:S(2)}) copy-start(bf16[32,1536]{1,0:T(8,128)(2,1)S(1)} %collective-permute-done.6.before.refs_4_) | copy-start | bytes 294916
  44.0 0.6 copy-start.8
  44.0 0.7 copy-start.15
  44.7 0.6 copy-start.16
  47.1 10.1 %collective-permute-start.12 = (bf16[144,1152]{1,0:T(8,128)(2,1)}, bf16[144,1152]{1,0:T(8,128)(2,1)S(1)}, u32[]{:S(2)}, u32[]{:S(2)}) collective-permute-start(bf16[144,1152]{1,0:T(8,128)(2,1)} %shard_map.105.refs_4_), channel_id=1, source_target_pairs={{0,2},{1,3},{2,4},{3,5},{4,6},{5,7},{6,0},{7,1},{8,10},{9,11},{10,... | collective-permute-start | bytes 995336 | tf_op jit(solution)/shard_map/ppermute | solution.py:285
  48.4 10.7 %collective-permute-start.14 = (bf16[144,1152]{1,0:T(8,128)(2,1)}, bf16[144,1152]{1,0:T(8,128)(2,1)S(1)}, u32[]{:S(2)}, u32[]{:S(2)}) collective-permute-start(bf16[144,1152]{1,0:T(8,128)(2,1)} %shard_map.105.refs_4_), channel_id=1, source_target_pairs={{0,6},{1,7},{2,0},{3,1},{4,2},{5,3},{6,4},{7,5},{8,14},{9,15},{10,... | collective-permute-start | bytes 995336 | tf_op jit(solution)/shard_map/ppermute | solution.py:286
  49.8 15.2 %collective-permute-start.10 = (bf16[144,1152]{1,0:T(8,128)(2,1)}, bf16[144,1152]{1,0:T(8,128)(2,1)S(1)}, u32[]{:S(2)}, u32[]{:S(2)}) collective-permute-start(bf16[144,1152]{1,0:T(8,128)(2,1)} %shard_map.105.refs_4_), channel_id=1, source_target_pairs={{0,4},{1,5},{2,6},{3,7},{4,0},{5,1},{6,2},{7,3},{8,12},{9,13},{10,... | collective-permute-start | bytes 995336 | tf_op jit(solution)/shard_map/ppermute | solution.py:287
  50.9 24.2 %collective-permute-start.16 = (bf16[144,1152]{1,0:T(8,128)(2,1)}, bf16[144,1152]{1,0:T(8,128)(2,1)S(1)}, u32[]{:S(2)}, u32[]{:S(2)}) collective-permute-start(bf16[144,1152]{1,0:T(8,128)(2,1)} %shard_map.105.refs_4_), channel_id=1, source_target_pairs={{0,8},{8,0},{16,24},{24,16},{32,40},{40,32},{48,56},{56,48},{64,72... | collective-permute-start | bytes 995336 | tf_op jit(solution)/shard_map/ppermute | solution.py:288
  57.2 24.7 %collective-permute-start.13 = (bf16[144,1152]{1,0:T(8,128)(2,1)S(1)}, bf16[144,1152]{1,0:T(8,128)(2,1)S(1)}, u32[]{:S(2)}, u32[]{:S(2)}) collective-permute-start(bf16[144,1152]{1,0:T(8,128)(2,1)S(1)} %collective-permute-done.12.refs_4_), channel_id=1, source_target_pairs={{0,8},{8,0},{16,24},{24,16},{32,40},{40,32},{48,56},{56,48},{64,72... | collective-permute-start | bytes 995336 | tf_op jit(solution)/shard_map/ppermute | solution.py:312
  59.1 22.8 %collective-permute-start.15 = (bf16[144,1152]{1,0:T(8,128)(2,1)S(1)}, bf16[144,1152]{1,0:T(8,128)(2,1)S(1)}, u32[]{:S(2)}, u32[]{:S(2)}) collective-permute-start(bf16[144,1152]{1,0:T(8,128)(2,1)S(1)} %collective-permute-done.14.refs_6_), channel_id=1, source_target_pairs={{0,8},{8,0},{16,24},{24,16},{32,40},{40,32},{48,56},{56,48},{64,72... | collective-permute-start | bytes 995336 | tf_op jit(solution)/shard_map/ppermute | solution.py:313
  65.0 28.6 %collective-permute-start.11 = (bf16[144,1152]{1,0:T(8,128)(2,1)S(1)}, bf16[144,1152]{1,0:T(8,128)(2,1)S(1)}, u32[]{:S(2)}, u32[]{:S(2)}) collective-permute-start(bf16[144,1152]{1,0:T(8,128)(2,1)S(1)} %collective-permute-done.10.refs_4_), channel_id=1, source_target_pairs={{0,8},{8,0},{16,24},{24,16},{32,40},{40,32},{48,56},{56,48},{64,72... | collective-permute-start | bytes 995336 | tf_op jit(solution)/shard_map/ppermute | solution.py:316
  66.7 2.3 %copy-start.2 = (bf16[1536,1536]{1,0:T(8,128)(2,1)S(1)}, bf16[1536,1536]{1,0:T(8,128)(2,1)}, u32[]{:S(2)}) copy-start(bf16[1536,1536]{1,0:T(8,128)(2,1)} %w_ref.1) | copy-start | bytes 14155780
  69.1 0.9 copy-start.5
  70.0 0.9 copy-start.7
  70.9 0.9 copy-start.9
  71.8 0.9 copy-start.10
  72.7 0.7 copy-start.13
  73.3 1.8 %copy-start.3 = (bf16[144,1152]{1,0:T(8,128)(2,1)S(1)}, bf16[144,1152]{1,0:T(8,128)(2,1)}, u32[]{:S(2)}) copy-start(bf16[144,1152]{1,0:T(8,128)(2,1)} %shard_map.105.refs_4_) | copy-start | bytes 995332
  73.3 1.8 %copy-start.11 = (s32[3,576]{1,0:T(4,128)S(1)}, s32[3,576]{1,0:T(4,128)}, u32[]{:S(2)}) copy-start(s32[3,576]{1,0:T(4,128)} %constant.55.clone.refs_2_) | copy-start | bytes 20740
  73.3 8.6 %copy-start.12 = (s32[3,1152]{1,0:T(4,128)S(1)}, s32[3,1152]{1,0:T(4,128)}, u32[]{:S(2)}) copy-start(s32[3,1152]{1,0:T(4,128)} %constant.56.clone.refs_2_) | copy-start | bytes 41476
  73.3 8.6 %copy-start.14 = (s32[7]{0:T(128)S(1)}, s32[7]{0:T(128)}, u32[]{:S(2)}) copy-start(s32[7]{0:T(128)} %stack.27.spot.refs_0_) | copy-start | bytes 88
  75.1 18.6 %copy-start.1 = (bf16[512,2048]{1,0:T(8,128)(2,1)S(1)}, bf16[512,2048]{1,0:T(8,128)(2,1)}, u32[]{:S(2)}) copy-start(bf16[512,2048]{1,0:T(8,128)(2,1)} %refs_3_.5) | copy-start | bytes 6291460

commit v3 on v2

v3 whole, which is shorter than its diff:
```python
import math

import jax
import jax.numpy as jnp
import numpy as np
from jax import lax
from jax.experimental import pallas as pl
from jax.experimental.pallas import tpu as pltpu
from jax.sharding import PartitionSpec as P

KL = 512
RD = 64
ND = 128
VD = 128
LANES = 128
EPSILON = 1e-06
MASKED = -1e30
FLOOR = -1e29
COARSE = (1, 4, 7)
SCORE_SCALE = math.log2(math.e) / math.sqrt(ND + RD)


SMALL = pltpu.CompilerParams(vmem_limit_bytes=12 * 2**20)


def fast(array):
    return pltpu.with_memory_space_constraint(array, pltpu.VMEM)


def slow(array):
    return pltpu.with_memory_space_constraint(array, pltpu.HBM)


def here():
    ctx, head = lax.axis_index("ctx"), lax.axis_index("head")
    return ctx // 2, lax.rem(ctx, 2), head // 2, lax.rem(head, 2)


def scaled(values, gain):
    mean = jnp.mean(values * values, axis=-1, keepdims=True)
    return values * lax.rsqrt(mean + EPSILON) * gain


def norm_q_kernel(rows_ref, gain_ref, out_ref):
    rows = rows_ref[...].astype(jnp.float32)
    out_ref[...] = scaled(rows, gain_ref[...][None, :]).astype(jnp.bfloat16)


def norm_kv_kernel(rows_ref, gain_ref, out_ref):
    latent = rows_ref[:, :KL].astype(jnp.float32)
    out_ref[:, :KL] = scaled(latent, gain_ref[...][None, :]).astype(jnp.bfloat16)
    out_ref[:, KL:] = rows_ref[:, KL:]


def pair_kernel(own_ref, other_ref, out_ref):
    def lay(even, odd):
        out_ref[:, :KL] = even[:, :KL]
        out_ref[:, KL : 2 * KL] = odd[:, :KL]
        out_ref[:, 2 * KL :] = jnp.concatenate([even[:, KL:], odd[:, KL:]], axis=1)

    core = here()[1]

    @pl.when(core == 0)
    def _():
        lay(own_ref, other_ref)

    @pl.when(core != 0)
    def _():
        lay(other_ref, own_ref)


def join_kernel(sizes, n_after, *refs):
    outs = refs[len(refs) - len(sizes) :]
    at = 0
    for size, out_ref in zip(sizes, outs):
        row = 0
        for ref in refs[at : at + size]:
            out_ref[row : row + ref.shape[0], :] = ref[...]
            row += ref.shape[0]
        at += size


def join(groups, after=()):
    sizes = [len(g) for g in groups]
    shapes = [
        pltpu.VMEM((sum(a.shape[0] for a in g), g[0].shape[1]), g[0].dtype)
        for g in groups
    ]
    arrays = [a for g in groups for a in g]
    vmem = pl.BlockSpec(memory_space=pltpu.VMEM)

    def kernel(*refs):
        join_kernel(sizes, len(after), *refs)

    return pl.pallas_call(
        kernel,
        in_specs=[vmem] * (len(arrays) + len(after)),
        out_specs=[vmem] * len(groups),
        out_shape=shapes,
        compiler_params=SMALL,
    )(*[fast(a) for a in (*arrays, *after)])


def document_start(position, lengths):
    start, end = jnp.zeros_like(position), 0
    for doc in range(lengths.shape[0]):
        end = end + lengths[doc]
        start = jnp.where(position >= end, end, start)
    return start


def query_kernel(lengths, own, after, before, across, w_ref, out_ref, rows_ref):
    chip, core, y, xh = here()
    for shift, ref in ((0, own), (3, after), (1, before), (2, across)):
        for half in range(2):
            place = lax.rem(y + shift, 4) * 32 + lax.rem(xh + half, 2) * 16
            at = pl.multiple_of(place, 16)
            rows_ref[pl.ds(at, 16), :] = ref[16 * half : 16 * half + 16, :]

    shape = (rows_ref.shape[0], LANES)
    lane = lax.broadcasted_iota(jnp.int32, shape, 1)
    position = (2 * chip + core) * shape[0] + lax.broadcasted_iota(jnp.int32, shape, 0)
    offset = (position - document_start(position, lengths)).astype(jnp.float32)
    freq_index = lax.rem(lane, RD // 2).astype(jnp.float32)
    angles = offset * jnp.exp(freq_index * (-2.0 * math.log(10000.0) / RD))
    cosine = jnp.where(lane < RD, jnp.cos(angles), 0.0)
    sine = jnp.sin(angles)
    sine = jnp.where(lane < RD // 2, -sine, jnp.where(lane < RD, sine, 0.0))

    def rotated(rope):
        turned = jnp.where(
            lane < RD // 2, pltpu.roll(rope, LANES - RD // 2, 1), pltpu.roll(rope, RD // 2, 1)
        )
        return rope * cosine + turned * sine

    width = 2 * (ND + RD)
    for pair in range(w_ref.shape[1] // width):
        w = w_ref[:, pair * width : (pair + 1) * width]
        made = jnp.dot(rows_ref[...], w, preferred_element_type=jnp.float32)
        out_ref[2 * pair, :, :ND] = made[:, :ND].astype(jnp.bfloat16)
        out_ref[2 * pair, :, ND:] = rotated(made[:, ND : ND + LANES]).astype(jnp.bfloat16)
        second = ND + RD
        out_ref[2 * pair + 1, :, :ND] = made[:, second : second + ND].astype(jnp.bfloat16)
        rope = pltpu.roll(made[:, second + RD : second + RD + LANES], RD, 1)
        out_ref[2 * pair + 1, :, ND:] = rotated(rope).astype(jnp.bfloat16)


def attend_kernel(n_pieces, turn, first, last, *refs):
    lengths, q_ref, table_ref, w_ref = refs[:4]
    pieces = refs[4 : 4 + n_pieces]
    at = 4 + n_pieces
    if not first:
        max_in, sum_in, acc_in = refs[at : at + 3]
        at += 3
    if last:
        (out_ref,) = refs[at : at + 1]
        at += 1
    else:
        max_out, sum_out, acc_out = refs[at : at + 3]
        at += 3
    rows_ref, rope_ref, bias_ref = refs[at:]
    size = pieces[0].shape[0]

    for n, ref in enumerate(pieces):
        low = pl.ds(n * size, size)
        high = pl.ds((n_pieces + n) * size, size)
        rows_ref[low, :] = ref[:, :KL]
        rows_ref[high, :] = ref[:, KL : 2 * KL]
        rope = ref[:, 2 * KL :]
        rope_ref[low, :] = rope
        rope_ref[high, :] = jnp.concatenate([rope[:, RD:], rope[:, :RD]], axis=1)

    chip, core, y, xh = here()
    tok_dev, n_keys = bias_ref.shape
    query_pos = (2 * chip + core) * tok_dev + lax.broadcasted_iota(jnp.int32, (tok_dev, 1), 0)
    query_start = document_start(query_pos, lengths)
    ys = lax.rem(y + jnp.where(lax.rem(table_ref[1:2, :] + core, 2) == 0, 4 - turn, 4 + turn), 4)
    ys = lax.rem(ys + table_ref[2:3, :], 4)
    xs = lax.rem(xh + core + table_ref[1:2, :], 2)
    key_pos = table_ref[0:1, :] + 2 * chip * tok_dev + ys * 32 + xs * 16
    allowed = (key_pos <= query_pos) & (key_pos >= query_start)
    bias_ref[...] = jnp.where(allowed, 0.0, MASKED)

    for head in range(q_ref.shape[0]):
        w = w_ref[:, head * (ND + VD) : (head + 1) * (ND + VD)]
        expanded = jnp.dot(rows_ref[...], w, preferred_element_type=jnp.float32)
        expanded = expanded.astype(jnp.bfloat16)
        keys = jnp.concatenate([expanded[:, :ND], rope_ref[...]], axis=1)
        scores = lax.dot_general(
            q_ref[head], keys, (((1,), (1,)), ((), ())), preferred_element_type=jnp.float32
        )
        scores = scores * SCORE_SCALE + bias_ref[...]
        top = jnp.max(scores, axis=1, keepdims=True)
        if first:
            new_max = jnp.maximum(top, FLOOR)
        else:
            old_max = max_in[head][:, :1]
            new_max = jnp.maximum(top, old_max)
        weights = jnp.exp2(scores - new_max)
        total = jnp.sum(weights, axis=1, keepdims=True)
        mixed = jnp.dot(
            weights.astype(jnp.bfloat16), expanded[:, ND:], preferred_element_type=jnp.float32
        )
        if not first:
            faded = jnp.exp2(old_max - new_max)
            total = total + faded * sum_in[head][:, :1]
            mixed = mixed + faded * acc_in[head]
        if last:
            out_ref[:, head * VD : (head + 1) * VD] = (mixed / total).astype(jnp.bfloat16)
        else:
            max_out[head] = jnp.broadcast_to(new_max, mixed.shape)
            sum_out[head] = jnp.broadcast_to(total, mixed.shape)
            acc_out[head] = mixed


def key_table(slots, rows, tok_dev, partners):
    coarse = len(slots) // 3
    held = []
    for part in range(3):
        for turn in (0, 2):
            for k in slots[part * coarse : (part + 1) * coarse]:
                held += [(row - 2 * k * tok_dev, turn) for row in range(rows)]
    columns = [
        (place + parity * tok_dev, partner, turn)
        for parity in range(2)
        for partner in partners
        for place, turn in held
    ]
    return np.array(columns, np.int32).T


def attend(doc_lengths, queries, slots, w_kv, pieces, turn, partners, state, last):
    heads, rows, width = queries.shape
    first = state is None
    table = jnp.asarray(key_table(slots, 16, rows, partners))
    count = table.shape[1]
    vmem = pl.BlockSpec(memory_space=pltpu.VMEM)
    args = [queries, table, w_kv, *pieces]
    if not first:
        args += list(state)
    args = [slow(doc_lengths), *[fast(a) for a in args]]
    if last:
        out_shape = jax.ShapeDtypeStruct((rows, heads * VD), jnp.bfloat16)
        out_specs = vmem
    else:
        out_shape = [pltpu.VMEM((heads, rows, VD), jnp.float32)] * 3
        out_specs = [vmem] * 3

    def kernel(*refs):
        attend_kernel(len(pieces), turn, first, last, *refs)

    return pl.pallas_call(
        kernel,
        in_specs=[pl.BlockSpec(memory_space=pltpu.SMEM)] + [vmem] * (len(args) - 1),
        out_specs=out_specs,
        out_shape=out_shape,
        scratch_shapes=[
            pltpu.VMEM((count, KL), jnp.bfloat16),
            pltpu.VMEM((count, LANES), jnp.bfloat16),
            pltpu.VMEM((rows, count), jnp.float32),
        ],
        compiler_params=SMALL,
    )(*args)


def body(q_latent, q_gain, kv_cache, kv_gain, w_query, w_kv, doc_lengths):
    ctx_size, head_size = lax.axis_size("ctx"), lax.axis_size("head")
    chips, ys = ctx_size // 2, head_size // 2
    tok_dev = q_latent.shape[0] * head_size
    heads_here = w_query.shape[1] // (ND + RD)
    ctx, head = lax.axis_index("ctx"), lax.axis_index("head")
    vmem = pl.BlockSpec(memory_space=pltpu.VMEM)

    swap = [(n, n ^ 1) for n in range(ctx_size)]
    across_x = [(n, n ^ 1) for n in range(head_size)]

    def chip_shift(step):
        return [(2 * n + c, 2 * ((n + step) % chips) + c) for n in range(chips) for c in range(2)]

    def coarse_shift(step, turn):
        return [
            (
                (2 * n + c) * head_size + h,
                (2 * ((n + step) % chips) + c) * head_size + ((h + 2 * turn) % head_size ^ c),
            )
            for n in range(chips)
            for c in range(2)
            for h in range(head_size)
        ]

    apart = [
        ((2 * n + c) * head_size + h, (2 * n + c) * head_size + (h + 2 - 4 * c) % head_size)
        for n in range(chips)
        for c in range(2)
        for h in range(head_size)
    ]

    def y_shift(step):
        return [(2 * n + x, 2 * ((n + step) % ys) + x) for n in range(ys) for x in range(2)]

    kv_rows = pl.pallas_call(
        norm_kv_kernel,
        out_shape=pltpu.VMEM(kv_cache.shape, jnp.bfloat16),
        compiler_params=SMALL,

    )(slow(kv_cache), slow(kv_gain))
    q_rows = pl.pallas_call(
        norm_q_kernel,
        out_shape=pltpu.VMEM(q_latent.shape, jnp.bfloat16),
        compiler_params=SMALL,

    )(slow(q_latent), slow(q_gain))
    q_other = lax.ppermute(q_rows, "head", across_x)
    kv_other = lax.ppermute(kv_rows, "ctx", swap)
    piece = pl.pallas_call(
        pair_kernel,
        in_specs=[vmem, vmem],
        out_specs=vmem,
        out_shape=pltpu.VMEM((kv_rows.shape[0], 2 * kv_rows.shape[1]), jnp.bfloat16),
        compiler_params=SMALL,
    )(fast(kv_rows), fast(kv_other))
    coarse = [
        lax.ppermute(piece, ("ctx", "head"), coarse_shift(step, turn))
        for turn in (0, 2)
        for step in COARSE
    ]

    coarse, q_pair = join([coarse, [q_rows, q_other]])
    later = lax.ppermute(coarse, "ctx", chip_shift(1))
    sooner = lax.ppermute(coarse, "ctx", chip_shift(-1))
    q_after = lax.ppermute(q_pair, "head", y_shift(1))
    q_before = lax.ppermute(q_pair, "head", y_shift(-1))
    q_across = lax.ppermute(q_pair, "head", y_shift(2))

    slots = [*COARSE, *[k + 1 for k in COARSE], *[k - 1 for k in COARSE]]
    (held,) = join([[coarse, later, sooner]], after=[q_after, q_before, q_across])
    received = lax.ppermute(held, ("ctx", "head"), apart)
    own_swapped = lax.ppermute(held, "ctx", swap)

    queries = pl.pallas_call(
        query_kernel,
        in_specs=[pl.BlockSpec(memory_space=pltpu.SMEM)] + [vmem] * 5,
        out_specs=vmem,
        out_shape=pltpu.VMEM((heads_here, tok_dev, 2 * LANES), jnp.bfloat16),
        scratch_shapes=[pltpu.VMEM((tok_dev, w_query.shape[0]), jnp.bfloat16)],
        compiler_params=SMALL,
    )(slow(doc_lengths), *[fast(a) for a in (q_pair, q_after, q_before, q_across, w_query)])

    def attend_to(pieces, turn, partners, state, last=False):
        return attend(doc_lengths, queries, slots, w_kv, pieces, turn, partners, state, last)

    state = attend_to([held, own_swapped], 0, [0, 1], None)
    received, state = lax.optimization_barrier((received, state))
    swapped = lax.ppermute(received, "ctx", swap)
    state = attend_to([received], 1, [0], state)
    return attend_to([swapped], 1, [1], state, last=True)


def solution(mesh):
    placed = (
        P(("ctx", "head"), None),
        P(),
        P(("ctx", "head"), None),
        P(),
        P(None, "head"),
        P(None, "head"),
        P(),
    )
    return jax.shard_map(
        body, mesh=mesh, in_specs=placed, out_specs=P("ctx", "head"), check_vma=False
    )
```

time: 102 us -> 76.8 us (0.75)
  local copies, waits for them, and re-layouts: 11.9 us -> 2.35 us
  Pallas kernels: 36.1 us -> 29.6 us
  waiting for transfers between devices: 17.6 us -> 11.9 us
  between operations: 2.18 us -> 0.14 us
  other arithmetic: 1.06 us -> 0 us
    ppermute x9 -> x8, waiting for transfers between devices: 13 us -> 6.11 us  [the longest x6 6.11 us: body(): lax.ppermute(piece, ('ctx', 'head'), coarse_shift(step, turn))]
    unnamed x44 -> x10, local copies, waits for them, and re-layouts: 9.1 us -> 2.35 us
    pallas_call x6, Pallas kernels: 9.6 us -> 3.95 us  [the longest x1 1.93 us: body(): pl.pallas_call(query_kernel, in_specs=[pl.BlockSpec(memory_space=pltpu.SM...]
    ppermute x9 -> x8, starting transfers between devices: 19.1 us -> 23.1 us  [the longest x6 22.5 us: body(): lax.ppermute(piece, ('ctx', 'head'), coarse_shift(step, turn))]
    ppermute x1, starting transfers between devices: 2.84 us -> 0.08 us  [body(): sooner = lax.ppermute(coarse, 'ctx', chip_shift(-1))]
    ppermute x1, starting transfers between devices: 1.64 us -> 0.06 us  [body(): q_across = lax.ppermute(q_pair, 'head', y_shift(2))]
    slice x1 -> x0, local copies, waits for them, and re-layouts: 1.41 us -> none  [body(): ends.append(ends[-1] + doc_lengths[doc])]
    another operation x1 -> x0, local copies, waits for them, and re-layouts: 1.3 us -> none  [body(): spot = jnp.stack([ctx // 2, ctx % 2, head // 2, head % 2, *ends])]
  transfers between devices with their start and end apart: 17 -> 16, of which waited for: 6 -> 5; matrix products, arithmetic and copies ran while one was open for 4% -> 0% of each run, Pallas kernels for 23% -> 26%
where the time goes in v3:
time: 76.8 us; the launch traced here: 76.6 us
  starting transfers between devices  32.6 us (42%)
  Pallas kernels  29.6 us (39%)
  waiting for transfers between devices  11.9 us (15%)
  local copies, waits for them, and re-layouts  2.35 us (3%)
    pallas_call x3, Pallas kernels, attend(): pl.pallas_call(kernel, in_specs=[pl.BlockSpec(memory_space=pltpu.SMEM)] +...  25.7 us
    ppermute x6, starting transfers between devices, body(): lax.ppermute(piece, ('ctx', 'head'), coarse_shift(step, turn))  22.5 us
    ppermute x6, waiting for transfers between devices, body(): lax.ppermute(piece, ('ctx', 'head'), coarse_shift(step, turn))  6.11 us
    ppermute x1, starting transfers between devices, body(): kv_other = lax.ppermute(kv_rows, 'ctx', swap)  3.33 us
    ppermute x1, waiting for transfers between devices, body(): q_across = lax.ppermute(q_pair, 'head', y_shift(2))  3.25 us
    ppermute x1, starting transfers between devices, body(): q_before = lax.ppermute(q_pair, 'head', y_shift(-1))  2.73 us
    unnamed x10, local copies, waits for them, and re-layouts  2.35 us
    ppermute x1, waiting for transfers between devices, body(): q_after = lax.ppermute(q_pair, 'head', y_shift(1))  2.04 us
  transfers between devices with their start and end apart: 16, of which 5 were waited for; matrix products, arithmetic and copies ran while one was open for 0% of the time, Pallas kernels for 26%

profile of v3, /device:TPU:1, one launch (start us, length us, event | category | flops | bytes accessed | tf_op | source)
XLA Modules:
  0.0 76.6 jit_solution(4194365600355472173)
XLA Ops:
  0.0 0.0 copy-start.2
  0.0 0.0 copy-start
  0.0 1.0 %shard_map.100.own_ref = bf16[16,576]{1,0:T(8,128)(2,1)S(1)} custom-call(bf16[16,576]{1,0:T(8,128)(2,1)} %rows_ref.2, f32[512]{0:T(512)} %gain_ref.2), custom_call_target="tpu_custom_call" | custom-call | tf_op jit(solution)/shard_map/pallas_call | solution.py:301
  1.0 3.3 %collective-permute-start = (bf16[16,576]{1,0:T(8,128)(2,1)S(1)}, bf16[16,576]{1,0:T(8,128)(2,1)S(1)}, u32[]{:S(2)}, u32[]{:S(2)}) collective-permute-start(bf16[16,576]{1,0:T(8,128)(2,1)S(1)} %shard_map.100.own_ref), channel_id=1, source_target_pairs={{0,8},{8,0},{16,24},{24,16},{32,40},{40,32},{48,56},{56,48},{64,72... | collective-permute-start | bytes 55304 | tf_op jit(solution)/shard_map/ppermute | solution.py:314
  4.3 0.9 %shard_map.102.refs_6_ = bf16[16,1536]{1,0:T(8,128)(2,1)S(1)} custom-call(bf16[16,1536]{1,0:T(8,128)(2,1)} %rows_ref.3, f32[1536]{0:T(1024)} %gain_ref.3), custom_call_target="tpu_custom_call" | custom-call | tf_op jit(solution)/shard_map/pallas_call | solution.py:307
  5.2 1.1 %collective-permute-start.7 = (bf16[16,1536]{1,0:T(8,128)(2,1)S(1)}, bf16[16,1536]{1,0:T(8,128)(2,1)S(1)}, u32[]{:S(2)}, u32[]{:S(2)}) collective-permute-start(bf16[16,1536]{1,0:T(8,128)(2,1)S(1)} %shard_map.102.refs_6_), channel_id=1, source_target_pairs={{0,1},{1,0},{2,3},{3,2},{4,5},{5,4},{6,7},{7,6},{8,9},{9,8},{10,11... | collective-permute-start | bytes 147464 | tf_op jit(solution)/shard_map/ppermute | solution.py:313
  6.3 0.0 collective-permute-done.other_ref
  6.3 0.1 shard_map.101
  6.4 8.2 %collective-permute-start.6 = (bf16[16,1152]{1,0:T(8,128)(2,1)S(1)}, bf16[16,1152]{1,0:T(8,128)(2,1)S(1)}, u32[]{:S(2)}, u32[]{:S(2)}) collective-permute-start(bf16[16,1152]{1,0:T(8,128)(2,1)S(1)} %shard_map.101), channel_id=1, source_target_pairs={{0,116},{1,117},{2,118},{3,119},{4,112},{5,113},{6,114},{7,115},{8... | collective-permute-start | bytes 110600 | tf_op jit(solution)/shard_map/ppermute | solution.py:323
  14.5 2.5 %collective-permute-start.5 = (bf16[16,1152]{1,0:T(8,128)(2,1)S(1)}, bf16[16,1152]{1,0:T(8,128)(2,1)S(1)}, u32[]{:S(2)}, u32[]{:S(2)}) collective-permute-start(bf16[16,1152]{1,0:T(8,128)(2,1)S(1)} %shard_map.101), channel_id=1, source_target_pairs={{0,68},{1,69},{2,70},{3,71},{4,64},{5,65},{6,66},{7,67},{8,77},{9,... | collective-permute-start | bytes 110600 | tf_op jit(solution)/shard_map/ppermute | solution.py:323
  17.1 5.7 %collective-permute-start.4 = (bf16[16,1152]{1,0:T(8,128)(2,1)S(1)}, bf16[16,1152]{1,0:T(8,128)(2,1)S(1)}, u32[]{:S(2)}, u32[]{:S(2)}) collective-permute-start(bf16[16,1152]{1,0:T(8,128)(2,1)S(1)} %shard_map.101), channel_id=1, source_target_pairs={{0,20},{1,21},{2,22},{3,23},{4,16},{5,17},{6,18},{7,19},{8,29},{9,... | collective-permute-start | bytes 110600 | tf_op jit(solution)/shard_map/ppermute | solution.py:323
  22.8 2.0 %collective-permute-start.3 = (bf16[16,1152]{1,0:T(8,128)(2,1)S(1)}, bf16[16,1152]{1,0:T(8,128)(2,1)S(1)}, u32[]{:S(2)}, u32[]{:S(2)}) collective-permute-start(bf16[16,1152]{1,0:T(8,128)(2,1)S(1)} %shard_map.101), channel_id=1, source_target_pairs={{0,112},{1,113},{2,114},{3,115},{4,116},{5,117},{6,118},{7,119},{8... | collective-permute-start | bytes 110600 | tf_op jit(solution)/shard_map/ppermute | solution.py:323
  24.8 0.0 collective-permute-done.7.refs_7_
  24.8 4.2 %collective-permute-start.2 = (bf16[16,1152]{1,0:T(8,128)(2,1)S(1)}, bf16[16,1152]{1,0:T(8,128)(2,1)S(1)}, u32[]{:S(2)}, u32[]{:S(2)}) collective-permute-start(bf16[16,1152]{1,0:T(8,128)(2,1)S(1)} %shard_map.101), channel_id=1, source_target_pairs={{0,64},{1,65},{2,66},{3,67},{4,68},{5,69},{6,70},{7,71},{8,73},{9,... | collective-permute-start | bytes 110600 | tf_op jit(solution)/shard_map/ppermute | solution.py:323
  28.9 0.0 collective-permute-done.6.refs_5_
  28.9 0.0 collective-permute-start.1
  28.9 0.0 collective-permute-done.5.refs_4_
  28.9 0.0 collective-permute-done.4.refs_3_
  28.9 0.0 collective-permute-done.3.refs_2_
  28.9 4.8 %collective-permute-done.2.refs_1_ = bf16[16,1152]{1,0:T(8,128)(2,1)S(1)} collective-permute-done((bf16[16,1152]{1,0:T(8,128)(2,1)S(1)}, bf16[16,1152]{1,0:T(8,128)(2,1)S(1)}, u32[]{:S(2)}, u32[]{:S(2)}) %collective-permute-start.2) | collective-permute-done | bytes 36896 | tf_op jit(solution)/shard_map/ppermute | solution.py:323
  33.8 1.3 %collective-permute-done.1.refs_0_ = bf16[16,1152]{1,0:T(8,128)(2,1)S(1)} collective-permute-done((bf16[16,1152]{1,0:T(8,128)(2,1)S(1)}, bf16[16,1152]{1,0:T(8,128)(2,1)S(1)}, u32[]{:S(2)}, u32[]{:S(2)}) %collective-permute-start.1) | collective-permute-done | bytes 36896 | tf_op jit(solution)/shard_map/ppermute | solution.py:323
  35.1 0.1 collective-permute-start.12
  35.2 1.5 %collective-permute-start.11 = (bf16[96,1152]{1,0:T(8,128)(2,1)S(1)}, bf16[96,1152]{1,0:T(8,128)(2,1)S(1)}, u32[]{:S(2)}, u32[]{:S(2)}) collective-permute-start(bf16[96,1152]{1,0:T(8,128)(2,1)S(1)} %get-tuple-element.18.refs_0_), channel_id=1, source_target_pairs={{0,16},{8,24},{16,32},{24,40},{32,48},{40,56},{48,64},{56,72},{64,... | collective-permute-start | bytes 663560 | tf_op jit(solution)/shard_map/ppermute | solution.py:329
  36.6 0.1 collective-permute-start.10
  36.7 2.7 %collective-permute-start.9 = (bf16[32,1536]{1,0:T(8,128)(2,1)S(1)}, bf16[32,1536]{1,0:T(8,128)(2,1)S(1)}, u32[]{:S(2)}, u32[]{:S(2)}) collective-permute-start(bf16[32,1536]{1,0:T(8,128)(2,1)S(1)} %get-tuple-element.17.own), channel_id=1, source_target_pairs={{0,6},{1,7},{2,0},{3,1},{4,2},{5,3},{6,4},{7,5},{8,14},{9,15},{10,... | collective-permute-start | bytes 294920 | tf_op jit(solution)/shard_map/ppermute | solution.py:332
  39.4 0.0 collective-permute-start.8
  39.4 3.2 %collective-permute-done.10.across.refs_5_ = bf16[32,1536]{1,0:T(8,128)(2,1)S(1)} collective-permute-done((bf16[32,1536]{1,0:T(8,128)(2,1)S(1)}, bf16[32,1536]{1,0:T(8,128)(2,1)S(1)}, u32[]{:S(2)}, u32[]{:S(2)}) %collective-permute-start.10) | collective-permute-done | bytes 98336 | tf_op jit(solution)/shard_map/ppermute | solution.py:333
  42.7 0.5 collective-permute-done.9.before.refs_4_
  43.1 2.0 %collective-permute-done.8.after.refs_3_ = bf16[32,1536]{1,0:T(8,128)(2,1)S(1)} collective-permute-done((bf16[32,1536]{1,0:T(8,128)(2,1)S(1)}, bf16[32,1536]{1,0:T(8,128)(2,1)S(1)}, u32[]{:S(2)}, u32[]{:S(2)}) %collective-permute-start.8) | collective-permute-done | bytes 98336 | tf_op jit(solution)/shard_map/ppermute | solution.py:331
  45.2 0.0 collective-permute-done.12.refs_2_
  45.2 0.0 collective-permute-done.11.refs_1_
  45.2 0.0 copy-start.4
  45.2 0.1 shard_map.105.refs_4_
  45.2 0.8 collective-permute-start.14
  46.0 0.2 collective-permute-start.13
  46.2 0.0 copy-start.1
  46.2 2.3 %copy-done.1 = bf16[1536,1536]{1,0:T(8,128)(2,1)S(1)} copy-done((bf16[1536,1536]{1,0:T(8,128)(2,1)S(1)}, bf16[1536,1536]{1,0:T(8,128)(2,1)}, u32[]{:S(2)}) %copy-start.1) | copy-done | bytes 4718616
  48.5 1.9 %shard_map.104.refs_1_ = bf16[8,128,256]{2,1,0:T(8,128)(2,1)S(1)} custom-call(s32[3]{0:T(128)} %refs_0_.5, bf16[32,1536]{1,0:T(8,128)(2,1)S(1)} %get-tuple-element.17.own, bf16[32,1536]{1,0:T(8,128)(2,1)S(1)} %collective-permute-done.8.after.refs_3_, bf16[32,1536]{1,0:T(8,128)(2,1)S(1)} %collective-permute-done.9.before.refs_4_, ...), custom_call_target="tpu_custom_call" | custom-call | tf_op jit(solution)/shard_map/pallas_call | solution.py:340
  50.5 0.0 copy-start.3
  50.5 0.0 collective-permute-done.14.refs_5_
  50.5 0.0 copy-done.2
  50.5 0.0 copy-done
  50.5 9.9 %shard_map.106 = (f32[8,128,128]{2,1,0:T(8,128)S(1)}, f32[8,128,128]{2,1,0:T(8,128)S(1)}, f32[8,128,128]{2,1,0:T(8,128)S(1)}) custom-call(s32[3]{0:T(128)} %refs_0_.5, bf16[8,128,256]{2,1,0:T(8,128)(2,1)S(1)} %shard_map.104.refs_1_, s32[3,1152]{1,0:T(4,128)S(1)} %copy-done.2, bf16[512,2048]{1,0:T(8,128)(2,1)S(1)} %copy-done, ...), custom_call_target="tpu_custom_call" | custom-call | tf_op jit(solution)/shard_map/pallas_call | solution.py:252
  60.4 0.0 collective-permute-done.13.refs_4_
  60.4 0.4 collective-permute-start.15
  60.8 0.0 copy-done.4
  60.8 7.5 %shard_map.107 = (f32[8,128,128]{2,1,0:T(8,128)S(1)}, f32[8,128,128]{2,1,0:T(8,128)S(1)}, f32[8,128,128]{2,1,0:T(8,128)S(1)}) custom-call(s32[3]{0:T(128)} %refs_0_.5, bf16[8,128,256]{2,1,0:T(8,128)(2,1)S(1)} %shard_map.104.refs_1_, s32[3,576]{1,0:T(4,128)S(1)} %copy-done.4, bf16[512,2048]{1,0:T(8,128)(2,1)S(1)} %copy-done, ...), custom_call_target="tpu_custom_call" | custom-call | tf_op jit(solution)/shard_map/pallas_call | solution.py:252
  68.3 0.0 collective-permute-done.15.refs_4_
  68.3 0.0 copy-done.3
  68.3 8.3 %shard_map.108 = bf16[128,1024]{1,0:T(8,128)(2,1)} custom-call(s32[3]{0:T(128)} %refs_0_.5, bf16[8,128,256]{2,1,0:T(8,128)(2,1)S(1)} %shard_map.104.refs_1_, s32[3,576]{1,0:T(4,128)S(1)} %copy-done.3, bf16[512,2048]{1,0:T(8,128)(2,1)S(1)} %copy-done, bf16[288,1152]{1,0:T(8,128)(2,1)S(1)} %collective-permute-done.15.refs_4_, ...), custom_call_target="tpu_custom_call" | custom-call | tf_op jit(solution)/shard_map/pallas_call | solution.py:252
  (1 shorter events, 0.0 us)
Async XLA Ops:
  0.0 50.5 %copy-start.2 = (s32[3,1152]{1,0:T(4,128)S(1)}, s32[3,1152]{1,0:T(4,128)}, u32[]{:S(2)}) copy-start(s32[3,1152]{1,0:T(4,128)} %constant.6.clone.refs_2_) | copy-start | bytes 41476
  0.0 50.5 %copy-start = (bf16[512,2048]{1,0:T(8,128)(2,1)S(1)}, bf16[512,2048]{1,0:T(8,128)(2,1)}, u32[]{:S(2)}) copy-start(bf16[512,2048]{1,0:T(8,128)(2,1)} %refs_3_.5) | copy-start | bytes 6291460
  1.0 5.3 %collective-permute-start = (bf16[16,576]{1,0:T(8,128)(2,1)S(1)}, bf16[16,576]{1,0:T(8,128)(2,1)S(1)}, u32[]{:S(2)}, u32[]{:S(2)}) collective-permute-start(bf16[16,576]{1,0:T(8,128)(2,1)S(1)} %shard_map.100.own_ref), channel_id=1, source_target_pairs={{0,8},{8,0},{16,24},{24,16},{32,40},{40,32},{48,56},{56,48},{64,72... | collective-permute-start | bytes 55304 | tf_op jit(solution)/shard_map/ppermute | solution.py:314
  5.2 19.5 %collective-permute-start.7 = (bf16[16,1536]{1,0:T(8,128)(2,1)S(1)}, bf16[16,1536]{1,0:T(8,128)(2,1)S(1)}, u32[]{:S(2)}, u32[]{:S(2)}) collective-permute-start(bf16[16,1536]{1,0:T(8,128)(2,1)S(1)} %shard_map.102.refs_6_), channel_id=1, source_target_pairs={{0,1},{1,0},{2,3},{3,2},{4,5},{5,4},{6,7},{7,6},{8,9},{9,8},{10,11... | collective-permute-start | bytes 147464 | tf_op jit(solution)/shard_map/ppermute | solution.py:313
  6.4 22.5 %collective-permute-start.6 = (bf16[16,1152]{1,0:T(8,128)(2,1)S(1)}, bf16[16,1152]{1,0:T(8,128)(2,1)S(1)}, u32[]{:S(2)}, u32[]{:S(2)}) collective-permute-start(bf16[16,1152]{1,0:T(8,128)(2,1)S(1)} %shard_map.101), channel_id=1, source_target_pairs={{0,116},{1,117},{2,118},{3,119},{4,112},{5,113},{6,114},{7,115},{8... | collective-permute-start | bytes 110600 | tf_op jit(solution)/shard_map/ppermute | solution.py:323
  14.5 14.4 %collective-permute-start.5 = (bf16[16,1152]{1,0:T(8,128)(2,1)S(1)}, bf16[16,1152]{1,0:T(8,128)(2,1)S(1)}, u32[]{:S(2)}, u32[]{:S(2)}) collective-permute-start(bf16[16,1152]{1,0:T(8,128)(2,1)S(1)} %shard_map.101), channel_id=1, source_target_pairs={{0,68},{1,69},{2,70},{3,71},{4,64},{5,65},{6,66},{7,67},{8,77},{9,... | collective-permute-start | bytes 110600 | tf_op jit(solution)/shard_map/ppermute | solution.py:323
  17.1 11.9 %collective-permute-start.4 = (bf16[16,1152]{1,0:T(8,128)(2,1)S(1)}, bf16[16,1152]{1,0:T(8,128)(2,1)S(1)}, u32[]{:S(2)}, u32[]{:S(2)}) collective-permute-start(bf16[16,1152]{1,0:T(8,128)(2,1)S(1)} %shard_map.101), channel_id=1, source_target_pairs={{0,20},{1,21},{2,22},{3,23},{4,16},{5,17},{6,18},{7,19},{8,29},{9,... | collective-permute-start | bytes 110600 | tf_op jit(solution)/shard_map/ppermute | solution.py:323
  22.8 6.1 %collective-permute-start.3 = (bf16[16,1152]{1,0:T(8,128)(2,1)S(1)}, bf16[16,1152]{1,0:T(8,128)(2,1)S(1)}, u32[]{:S(2)}, u32[]{:S(2)}) collective-permute-start(bf16[16,1152]{1,0:T(8,128)(2,1)S(1)} %shard_map.101), channel_id=1, source_target_pairs={{0,112},{1,113},{2,114},{3,115},{4,116},{5,117},{6,118},{7,119},{8... | collective-permute-start | bytes 110600 | tf_op jit(solution)/shard_map/ppermute | solution.py:323
  24.8 9.0 %collective-permute-start.2 = (bf16[16,1152]{1,0:T(8,128)(2,1)S(1)}, bf16[16,1152]{1,0:T(8,128)(2,1)S(1)}, u32[]{:S(2)}, u32[]{:S(2)}) collective-permute-start(bf16[16,1152]{1,0:T(8,128)(2,1)S(1)} %shard_map.101), channel_id=1, source_target_pairs={{0,64},{1,65},{2,66},{3,67},{4,68},{5,69},{6,70},{7,71},{8,73},{9,... | collective-permute-start | bytes 110600 | tf_op jit(solution)/shard_map/ppermute | solution.py:323
  28.9 6.1 %collective-permute-start.1 = (bf16[16,1152]{1,0:T(8,128)(2,1)S(1)}, bf16[16,1152]{1,0:T(8,128)(2,1)S(1)}, u32[]{:S(2)}, u32[]{:S(2)}) collective-permute-start(bf16[16,1152]{1,0:T(8,128)(2,1)S(1)} %shard_map.101), channel_id=1, source_target_pairs={{0,16},{1,17},{2,18},{3,19},{4,20},{5,21},{6,22},{7,23},{8,25},{9,... | collective-permute-start | bytes 110600 | tf_op jit(solution)/shard_map/ppermute | solution.py:323
  35.1 10.1 %collective-permute-start.12 = (bf16[96,1152]{1,0:T(8,128)(2,1)S(1)}, bf16[96,1152]{1,0:T(8,128)(2,1)S(1)}, u32[]{:S(2)}, u32[]{:S(2)}) collective-permute-start(bf16[96,1152]{1,0:T(8,128)(2,1)S(1)} %get-tuple-element.18.refs_0_), channel_id=1, source_target_pairs={{0,240},{8,248},{16,0},{24,8},{32,16},{40,24},{48,32},{56,40},{64,... | collective-permute-start | bytes 663560 | tf_op jit(solution)/shard_map/ppermute | solution.py:330
  35.2 10.0 %collective-permute-start.11 = (bf16[96,1152]{1,0:T(8,128)(2,1)S(1)}, bf16[96,1152]{1,0:T(8,128)(2,1)S(1)}, u32[]{:S(2)}, u32[]{:S(2)}) collective-permute-start(bf16[96,1152]{1,0:T(8,128)(2,1)S(1)} %get-tuple-element.18.refs_0_), channel_id=1, source_target_pairs={{0,16},{8,24},{16,32},{24,40},{32,48},{40,56},{48,64},{56,72},{64,... | collective-permute-start | bytes 663560 | tf_op jit(solution)/shard_map/ppermute | solution.py:329
  36.6 6.0 %collective-permute-start.10 = (bf16[32,1536]{1,0:T(8,128)(2,1)S(1)}, bf16[32,1536]{1,0:T(8,128)(2,1)S(1)}, u32[]{:S(2)}, u32[]{:S(2)}) collective-permute-start(bf16[32,1536]{1,0:T(8,128)(2,1)S(1)} %get-tuple-element.17.own), channel_id=1, source_target_pairs={{0,4},{1,5},{2,6},{3,7},{4,0},{5,1},{6,2},{7,3},{8,12},{9,13},{10,... | collective-permute-start | bytes 294920 | tf_op jit(solution)/shard_map/ppermute | solution.py:333
  36.7 6.4 %collective-permute-start.9 = (bf16[32,1536]{1,0:T(8,128)(2,1)S(1)}, bf16[32,1536]{1,0:T(8,128)(2,1)S(1)}, u32[]{:S(2)}, u32[]{:S(2)}) collective-permute-start(bf16[32,1536]{1,0:T(8,128)(2,1)S(1)} %get-tuple-element.17.own), channel_id=1, source_target_pairs={{0,6},{1,7},{2,0},{3,1},{4,2},{5,3},{6,4},{7,5},{8,14},{9,15},{10,... | collective-permute-start | bytes 294920 | tf_op jit(solution)/shard_map/ppermute | solution.py:332
  39.4 5.8 %collective-permute-start.8 = (bf16[32,1536]{1,0:T(8,128)(2,1)S(1)}, bf16[32,1536]{1,0:T(8,128)(2,1)S(1)}, u32[]{:S(2)}, u32[]{:S(2)}) collective-permute-start(bf16[32,1536]{1,0:T(8,128)(2,1)S(1)} %get-tuple-element.17.own), channel_id=1, source_target_pairs={{0,2},{1,3},{2,4},{3,5},{4,6},{5,7},{6,0},{7,1},{8,10},{9,11},{10,... | collective-permute-start | bytes 294920 | tf_op jit(solution)/shard_map/ppermute | solution.py:331
  45.2 15.6 %copy-start.4 = (s32[3,576]{1,0:T(4,128)S(1)}, s32[3,576]{1,0:T(4,128)}, u32[]{:S(2)}) copy-start(s32[3,576]{1,0:T(4,128)} %constant.7.clone.refs_2_) | copy-start | bytes 20740
  45.2 5.2 %collective-permute-start.14 = (bf16[288,1152]{1,0:T(8,128)(2,1)S(1)}, bf16[288,1152]{1,0:T(8,128)(2,1)S(1)}, u32[]{:S(2)}, u32[]{:S(2)}) collective-permute-start(bf16[288,1152]{1,0:T(8,128)(2,1)S(1)} %shard_map.105.refs_4_), channel_id=1, source_target_pairs={{0,8},{8,0},{16,24},{24,16},{32,40},{40,32},{48,56},{56,48},{64,72... | collective-permute-start | bytes 1990664 | tf_op jit(solution)/shard_map/ppermute | solution.py:338
  46.0 14.4 %collective-permute-start.13 = (bf16[288,1152]{1,0:T(8,128)(2,1)S(1)}, bf16[288,1152]{1,0:T(8,128)(2,1)S(1)}, u32[]{:S(2)}, u32[]{:S(2)}) collective-permute-start(bf16[288,1152]{1,0:T(8,128)(2,1)S(1)} %shard_map.105.refs_4_), channel_id=1, source_target_pairs={{0,2},{1,3},{2,4},{3,5},{4,6},{5,7},{6,0},{7,1},{8,14},{9,15},{10,... | collective-permute-start | bytes 1990664 | tf_op jit(solution)/shard_map/ppermute | solution.py:337
  46.2 2.3 %copy-start.1 = (bf16[1536,1536]{1,0:T(8,128)(2,1)S(1)}, bf16[1536,1536]{1,0:T(8,128)(2,1)}, u32[]{:S(2)}) copy-start(bf16[1536,1536]{1,0:T(8,128)(2,1)} %w_ref.1) | copy-start | bytes 14155780
  50.5 17.9 %copy-start.3 = (s32[3,576]{1,0:T(4,128)S(1)}, s32[3,576]{1,0:T(4,128)}, u32[]{:S(2)}) copy-start(s32[3,576]{1,0:T(4,128)} %constant.8.clone.refs_2_) | copy-start | bytes 20740
  60.4 7.9 %collective-permute-start.15 = (bf16[288,1152]{1,0:T(8,128)(2,1)S(1)}, bf16[288,1152]{1,0:T(8,128)(2,1)S(1)}, u32[]{:S(2)}, u32[]{:S(2)}) collective-permute-start(bf16[288,1152]{1,0:T(8,128)(2,1)S(1)} %collective-permute-done.13.refs_4_), channel_id=1, source_target_pairs={{0,8},{8,0},{16,24},{24,16},{32,40},{40,32},{48,56},{56,48},{64,72... | collective-permute-start | bytes 1990664 | tf_op jit(solution)/shard_map/ppermute | solution.py:354

commit v4 on v3

--- a/solution.py
+++ b/solution.py
@@ -41,32 +41,31 @@
     return values * lax.rsqrt(mean + EPSILON) * gain
 
 
-def norm_q_kernel(rows_ref, gain_ref, out_ref):
-    rows = rows_ref[...].astype(jnp.float32)
-    out_ref[...] = scaled(rows, gain_ref[...][None, :]).astype(jnp.bfloat16)
-
-
-def norm_kv_kernel(rows_ref, gain_ref, out_ref):
-    latent = rows_ref[:, :KL].astype(jnp.float32)
-    out_ref[:, :KL] = scaled(latent, gain_ref[...][None, :]).astype(jnp.bfloat16)
-    out_ref[:, KL:] = rows_ref[:, KL:]
+def norm_kernel(q_ref, q_gain_ref, kv_ref, kv_gain_ref, out_ref):
+    latent = kv_ref[:, :KL].astype(jnp.float32)
+    out_ref[:, :KL] = scaled(latent, kv_gain_ref[...][None, :]).astype(jnp.bfloat16)
+    rows = q_ref[...].astype(jnp.float32)
+    q_end = KL + rows.shape[1]
+    out_ref[:, KL:q_end] = scaled(rows, q_gain_ref[...][None, :]).astype(jnp.bfloat16)
+    out_ref[:, q_end:] = kv_ref[:, KL:]
 
 
 def pair_kernel(own_ref, other_ref, out_ref):
-    def lay(even, odd):
-        out_ref[:, :KL] = even[:, :KL]
-        out_ref[:, KL : 2 * KL] = odd[:, :KL]
-        out_ref[:, 2 * KL :] = jnp.concatenate([even[:, KL:], odd[:, KL:]], axis=1)
-
-    core = here()[1]
-
-    @pl.when(core == 0)
-    def _():
-        lay(own_ref, other_ref)
-
-    @pl.when(core != 0)
-    def _():
-        lay(other_ref, own_ref)
+    q_end = own_ref.shape[1] - RD
+    q_size = q_end - KL
+    at = 2 * (KL + RD)
+    for n, ref in enumerate((own_ref, other_ref)):
+        out_ref[:, n * KL : (n + 1) * KL] = ref[:, :KL]
+        out_ref[:, at + n * q_size : at + (n + 1) * q_size] = ref[:, KL:q_end]
+    rope = jnp.concatenate([own_ref[:, q_end:], other_ref[:, q_end:]], axis=1)
+    out_ref[:, 2 * KL : at] = rope
+
+
+def part_kernel(own_ref, got_ref, kv_ref, q_ref):
+    size, width = own_ref.shape[0], kv_ref.shape[1]
+    for n, ref in enumerate((own_ref, got_ref)):
+        kv_ref[n * size : (n + 1) * size, :] = ref[:, :width]
+        q_ref[n * size : (n + 1) * size, :] = ref[:, width:]
 
 
 def join_kernel(sizes, n_after, *refs):
@@ -109,13 +108,16 @@
     return start
 
 
-def query_kernel(lengths, own, after, before, across, w_ref, out_ref, rows_ref):
+def query_kernel(lengths, own, got, w_ref, out_ref, rows_ref):
     chip, core, y, xh = here()
-    for shift, ref in ((0, own), (3, after), (1, before), (2, across)):
-        for half in range(2):
-            place = lax.rem(y + shift, 4) * 32 + lax.rem(xh + half, 2) * 16
+    width = rows_ref.shape[1]
+    for base, ref in ((y, own), (y + jnp.where(core == 0, 3, 1), got)):
+        for n in range(4):
+            turn, half = n // 2, n % 2
+            place = lax.rem(base + 2 * turn, 4) * 32 + lax.rem(xh + half, 2) * 16
             at = pl.multiple_of(place, 16)
-            rows_ref[pl.ds(at, 16), :] = ref[16 * half : 16 * half + 16, :]
+            rows = ref[16 * turn : 16 * turn + 16, half * width : (half + 1) * width]
+            rows_ref[pl.ds(at, 16), :] = rows
 
     shape = (rows_ref.shape[0], LANES)
     lane = lax.broadcasted_iota(jnp.int32, shape, 1)
@@ -176,8 +178,9 @@
     query_start = document_start(query_pos, lengths)
     ys = lax.rem(y + jnp.where(lax.rem(table_ref[1:2, :] + core, 2) == 0, 4 - turn, 4 + turn), 4)
     ys = lax.rem(ys + table_ref[2:3, :], 4)
-    xs = lax.rem(xh + core + table_ref[1:2, :], 2)
-    key_pos = table_ref[0:1, :] + 2 * chip * tok_dev + ys * 32 + xs * 16
+    xs = lax.rem(xh + table_ref[3:4, :], 2)
+    parity = lax.rem(core + table_ref[1:2, :], 2)
+    key_pos = table_ref[0:1, :] + (2 * chip + parity) * tok_dev + ys * 32 + xs * 16
     allowed = (key_pos <= query_pos) & (key_pos >= query_start)
     bias_ref[...] = jnp.where(allowed, 0.0, MASKED)
 
@@ -217,12 +220,12 @@
     coarse = len(slots) // 3
     held = []
     for part in range(3):
-        for turn in (0, 2):
-            for k in slots[part * coarse : (part + 1) * coarse]:
+        for k in slots[part * coarse : (part + 1) * coarse]:
+            for turn in (0, 2):
                 held += [(row - 2 * k * tok_dev, turn) for row in range(rows)]
     columns = [
-        (place + parity * tok_dev, partner, turn)
-        for parity in range(2)
+        (place, partner, turn, half)
+        for half in range(2)
         for partner in partners
         for place, turn in held
     ]
@@ -277,17 +280,6 @@
     def chip_shift(step):
         return [(2 * n + c, 2 * ((n + step) % chips) + c) for n in range(chips) for c in range(2)]
 
-    def coarse_shift(step, turn):
-        return [
-            (
-                (2 * n + c) * head_size + h,
-                (2 * ((n + step) % chips) + c) * head_size + ((h + 2 * turn) % head_size ^ c),
-            )
-            for n in range(chips)
-            for c in range(2)
-            for h in range(head_size)
-        ]
-
     apart = [
         ((2 * n + c) * head_size + h, (2 * n + c) * head_size + (h + 2 - 4 * c) % head_size)
         for n in range(chips)
@@ -295,56 +287,54 @@
         for h in range(head_size)
     ]
 
-    def y_shift(step):
-        return [(2 * n + x, 2 * ((n + step) % ys) + x) for n in range(ys) for x in range(2)]
-
-    kv_rows = pl.pallas_call(
-        norm_kv_kernel,
-        out_shape=pltpu.VMEM(kv_cache.shape, jnp.bfloat16),
-        compiler_params=SMALL,
-
-    )(slow(kv_cache), slow(kv_gain))
-    q_rows = pl.pallas_call(
-        norm_q_kernel,
-        out_shape=pltpu.VMEM(q_latent.shape, jnp.bfloat16),
-        compiler_params=SMALL,
-
-    )(slow(q_latent), slow(q_gain))
-    q_other = lax.ppermute(q_rows, "head", across_x)
-    kv_other = lax.ppermute(kv_rows, "ctx", swap)
-    piece = pl.pallas_call(
+    across_y = [(n, (n + ys) % head_size) for n in range(head_size)]
+
+    size, q_width = q_latent.shape
+    kv_width = kv_cache.shape[1]
+    rows = pl.pallas_call(
+        norm_kernel,
+        out_shape=pltpu.VMEM((size, q_width + kv_width), jnp.bfloat16),
+        compiler_params=SMALL,
+    )(*[slow(a) for a in (q_latent, q_gain, kv_cache, kv_gain)])
+    other = lax.ppermute(rows, "head", across_x)
+    both = pl.pallas_call(
         pair_kernel,
-        in_specs=[vmem, vmem],
+        in_specs=[vmem] * 2,
         out_specs=vmem,
-        out_shape=pltpu.VMEM((kv_rows.shape[0], 2 * kv_rows.shape[1]), jnp.bfloat16),
-        compiler_params=SMALL,
-    )(fast(kv_rows), fast(kv_other))
-    coarse = [
-        lax.ppermute(piece, ("ctx", "head"), coarse_shift(step, turn))
-        for turn in (0, 2)
-        for step in COARSE
-    ]
-
-    coarse, q_pair = join([coarse, [q_rows, q_other]])
+        out_shape=pltpu.VMEM((size, 2 * rows.shape[1]), jnp.bfloat16),
+        compiler_params=SMALL,
+    )(fast(rows), fast(other))
+    opposite = lax.ppermute(both, "head", across_y)
+    piece, q_set = pl.pallas_call(
+        part_kernel,
+        in_specs=[vmem] * 2,
+        out_specs=[vmem] * 2,
+        out_shape=[
+            pltpu.VMEM((2 * size, 2 * kv_width), jnp.bfloat16),
+            pltpu.VMEM((2 * size, 2 * q_width), jnp.bfloat16),
+        ],
+        compiler_params=SMALL,
+    )(fast(both), fast(opposite))
+    coarse = [lax.ppermute(piece, "ctx", chip_shift(step)) for step in COARSE]
+    (coarse,) = join([coarse])
     later = lax.ppermute(coarse, "ctx", chip_shift(1))
     sooner = lax.ppermute(coarse, "ctx", chip_shift(-1))
-    q_after = lax.ppermute(q_pair, "head", y_shift(1))
-    q_before = lax.ppermute(q_pair, "head", y_shift(-1))
-    q_across = lax.ppermute(q_pair, "head", y_shift(2))
+    q_set, coarse = lax.optimization_barrier((q_set, coarse))
+    q_got = lax.ppermute(q_set, ("ctx", "head"), apart)
 
     slots = [*COARSE, *[k + 1 for k in COARSE], *[k - 1 for k in COARSE]]
-    (held,) = join([[coarse, later, sooner]], after=[q_after, q_before, q_across])
+    (held,) = join([[coarse, later, sooner]], after=[q_got])
     received = lax.ppermute(held, ("ctx", "head"), apart)
     own_swapped = lax.ppermute(held, "ctx", swap)
 
     queries = pl.pallas_call(
         query_kernel,
-        in_specs=[pl.BlockSpec(memory_space=pltpu.SMEM)] + [vmem] * 5,
+        in_specs=[pl.BlockSpec(memory_space=pltpu.SMEM)] + [vmem] * 3,
         out_specs=vmem,
         out_shape=pltpu.VMEM((heads_here, tok_dev, 2 * LANES), jnp.bfloat16),
         scratch_shapes=[pltpu.VMEM((tok_dev, w_query.shape[0]), jnp.bfloat16)],
         compiler_params=SMALL,
-    )(slow(doc_lengths), *[fast(a) for a in (q_pair, q_after, q_before, q_across, w_query)])
+    )(slow(doc_lengths), *[fast(a) for a in (q_set, q_got, w_query)])
 
     def attend_to(pieces, turn, partners, state, last=False):
         return attend(doc_lengths, queries, slots, w_kv, pieces, turn, partners, state, last)

time: 76.8 us -> 73.1 us (0.952)
  starting transfers between devices: 32.6 us -> 29.3 us
  Pallas kernels: 29.6 us -> 28.8 us
    ppermute x11 -> x6, starting transfers between devices: 29.7 us -> 19 us  [the longest x3 9.43 us: body(): coarse = [lax.ppermute(piece, 'ctx', chip_shift(step)) for step in COARSE]]
    ppermute x1, starting transfers between devices: 0.76 us -> 5.75 us  [body(): own_swapped = lax.ppermute(held, 'ctx', swap)]
    ppermute x1, starting transfers between devices: 0.2 us -> 2.72 us  [body(): received = lax.ppermute(held, ('ctx', 'head'), apart)]
    pallas_call x3, Pallas kernels: 1.95 us -> 1.17 us  [the longest x1 1.08 us: body(): pl.pallas_call(norm_kernel, out_shape=pltpu.VMEM((size, q_width + kv_widt...]
    ppermute x11 -> x6, waiting for transfers between devices: 11.9 us -> 12 us  [the longest x3 5.25 us: body(): coarse = [lax.ppermute(piece, 'ctx', chip_shift(step)) for step in COARSE]]
  transfers between devices with their start and end apart: 16 -> 11, of which waited for: 5 -> 6; matrix products, arithmetic and copies ran while one was open for 0% -> 0% of each run, Pallas kernels for 26% -> 26%
where the time goes in v4:
time: 73.1 us; the launch traced here: 72.9 us
  starting transfers between devices  29.3 us (40%)
  Pallas kernels  28.8 us (39%)
  waiting for transfers between devices  12.3 us (17%)
  local copies, waits for them, and re-layouts  2.35 us (3%)
    pallas_call x3, Pallas kernels, attend(): pl.pallas_call(kernel, in_specs=[pl.BlockSpec(memory_space=pltpu.SMEM)] +...  25.7 us
    ppermute x3, starting transfers between devices, body(): coarse = [lax.ppermute(piece, 'ctx', chip_shift(step)) for step in COARSE]  9.43 us
    ppermute x1, starting transfers between devices, body(): own_swapped = lax.ppermute(held, 'ctx', swap)  5.75 us
    ppermute x3, waiting for transfers between devices, body(): coarse = [lax.ppermute(piece, 'ctx', chip_shift(step)) for step in COARSE]  5.25 us
    ppermute x1, starting transfers between devices, body(): other = lax.ppermute(rows, 'head', across_x)  3.66 us
    ppermute x1, starting transfers between devices, body(): opposite = lax.ppermute(both, 'head', across_y)  3.16 us
    ppermute x1, starting transfers between devices, body(): q_got = lax.ppermute(q_set, ('ctx', 'head'), apart)  2.73 us
    ppermute x1, starting transfers between devices, body(): received = lax.ppermute(held, ('ctx', 'head'), apart)  2.72 us
  transfers between devices with their start and end apart: 11, of which 6 were waited for; matrix products, arithmetic and copies ran while one was open for 0% of the time, Pallas kernels for 26%

profile of v4, /device:TPU:1, one launch (start us, length us, event | category | flops | bytes accessed | tf_op | source)
XLA Modules:
  0.0 72.9 jit_solution(6299988466411543135)
XLA Ops:
  0.0 0.0 copy-start.2
  0.0 0.0 copy-start
  0.0 1.1 %shard_map.100.own_ref = bf16[16,2112]{1,0:T(8,128)(2,1)S(1)} custom-call(bf16[16,1536]{1,0:T(8,128)(2,1)} %q_ref.1, f32[1536]{0:T(1024)} %q_gain_ref.1, bf16[16,576]{1,0:T(8,128)(2,1)} %kv_ref.1, f32[512]{0:T(512)} %kv_gain_ref.1), custom_call_target="tpu_custom_call" | custom-call | tf_op jit(solution)/shard_map/pallas_call | solution.py:294
  1.1 3.7 %collective-permute-start = (bf16[16,2112]{1,0:T(8,128)(2,1)S(1)}, bf16[16,2112]{1,0:T(8,128)(2,1)S(1)}, u32[]{:S(2)}, u32[]{:S(2)}) collective-permute-start(bf16[16,2112]{1,0:T(8,128)(2,1)S(1)} %shard_map.100.own_ref), channel_id=1, source_target_pairs={{0,1},{1,0},{2,3},{3,2},{4,5},{5,4},{6,7},{7,6},{8,9},{9,8},{10,11... | collective-permute-start | bytes 202760 | tf_op jit(solution)/shard_map/ppermute | solution.py:299
  4.7 1.7 %collective-permute-done.other_ref = bf16[16,2112]{1,0:T(8,128)(2,1)S(1)} collective-permute-done((bf16[16,2112]{1,0:T(8,128)(2,1)S(1)}, bf16[16,2112]{1,0:T(8,128)(2,1)S(1)}, u32[]{:S(2)}, u32[]{:S(2)}) %collective-permute-start) | collective-permute-done | bytes 67616 | tf_op jit(solution)/shard_map/ppermute | solution.py:299
  6.4 0.1 shard_map.101.own_ref
  6.5 3.2 %collective-permute-start.1 = (bf16[16,4224]{1,0:T(8,128)(2,1)S(1)}, bf16[16,4224]{1,0:T(8,128)(2,1)S(1)}, u32[]{:S(2)}, u32[]{:S(2)}) collective-permute-start(bf16[16,4224]{1,0:T(8,128)(2,1)S(1)} %shard_map.101.own_ref), channel_id=1, source_target_pairs={{0,4},{1,5},{2,6},{3,7},{4,0},{5,1},{6,2},{7,3},{8,12},{9,13},{10,... | collective-permute-start | bytes 405512 | tf_op jit(solution)/shard_map/ppermute | solution.py:307
  9.7 2.4 %collective-permute-done.1.got_ref = bf16[16,4224]{1,0:T(8,128)(2,1)S(1)} collective-permute-done((bf16[16,4224]{1,0:T(8,128)(2,1)S(1)}, bf16[16,4224]{1,0:T(8,128)(2,1)S(1)}, u32[]{:S(2)}, u32[]{:S(2)}) %collective-permute-start.1) | collective-permute-done | bytes 135200 | tf_op jit(solution)/shard_map/ppermute | solution.py:307
  12.1 5.7 %collective-permute-start.4 = (bf16[32,1152]{1,0:T(8,128)(2,1)S(1)}, bf16[32,1152]{1,0:T(8,128)(2,1)S(1)}, u32[]{:S(2)}, u32[]{:S(2)}) collective-permute-start(bf16[32,1152]{1,0:T(8,128)(2,1)S(1)} %get-tuple-element.20), channel_id=1, source_target_pairs={{0,112},{8,120},{16,128},{24,136},{32,144},{40,152},{48,160},{56,1... | collective-permute-start | bytes 221192 | tf_op jit(solution)/shard_map/ppermute | solution.py:318
  17.8 2.1 %collective-permute-start.3 = (bf16[32,1152]{1,0:T(8,128)(2,1)S(1)}, bf16[32,1152]{1,0:T(8,128)(2,1)S(1)}, u32[]{:S(2)}, u32[]{:S(2)}) collective-permute-start(bf16[32,1152]{1,0:T(8,128)(2,1)S(1)} %get-tuple-element.20), channel_id=1, source_target_pairs={{0,64},{8,72},{16,80},{24,88},{32,96},{40,104},{48,112},{56,120},{... | collective-permute-start | bytes 221192 | tf_op jit(solution)/shard_map/ppermute | solution.py:318
  19.9 1.6 %collective-permute-start.2 = (bf16[32,1152]{1,0:T(8,128)(2,1)S(1)}, bf16[32,1152]{1,0:T(8,128)(2,1)S(1)}, u32[]{:S(2)}, u32[]{:S(2)}) collective-permute-start(bf16[32,1152]{1,0:T(8,128)(2,1)S(1)} %get-tuple-element.20), channel_id=1, source_target_pairs={{0,16},{8,24},{16,32},{24,40},{32,48},{40,56},{48,64},{56,72},{64,... | collective-permute-start | bytes 221192 | tf_op jit(solution)/shard_map/ppermute | solution.py:318
  21.5 0.0 collective-permute-done.4.refs_2_
  21.5 4.5 %collective-permute-done.3.refs_1_ = bf16[32,1152]{1,0:T(8,128)(2,1)S(1)} collective-permute-done((bf16[32,1152]{1,0:T(8,128)(2,1)S(1)}, bf16[32,1152]{1,0:T(8,128)(2,1)S(1)}, u32[]{:S(2)}, u32[]{:S(2)}) %collective-permute-start.3) | collective-permute-done | bytes 73760 | tf_op jit(solution)/shard_map/ppermute | solution.py:318
  26.0 0.8 %collective-permute-done.2.refs_0_ = bf16[32,1152]{1,0:T(8,128)(2,1)S(1)} collective-permute-done((bf16[32,1152]{1,0:T(8,128)(2,1)S(1)}, bf16[32,1152]{1,0:T(8,128)(2,1)S(1)}, u32[]{:S(2)}, u32[]{:S(2)}) %collective-permute-start.2) | collective-permute-done | bytes 73760 | tf_op jit(solution)/shard_map/ppermute | solution.py:318
  26.8 0.3 collective-permute-start.7
  27.1 1.2 %collective-permute-start.6 = (bf16[96,1152]{1,0:T(8,128)(2,1)S(1)}, bf16[96,1152]{1,0:T(8,128)(2,1)S(1)}, u32[]{:S(2)}, u32[]{:S(2)}) collective-permute-start(bf16[96,1152]{1,0:T(8,128)(2,1)S(1)} %shard_map.103.refs_0_), channel_id=1, source_target_pairs={{0,16},{8,24},{16,32},{24,40},{32,48},{40,56},{48,64},{56,72},{64,... | collective-permute-start | bytes 663560 | tf_op jit(solution)/shard_map/ppermute | solution.py:320
  28.4 2.7 %collective-permute-start.5 = (bf16[32,3072]{1,0:T(8,128)(2,1)S(1)}, bf16[32,3072]{1,0:T(8,128)(2,1)S(1)}, u32[]{:S(2)}, u32[]{:S(2)}) collective-permute-start(bf16[32,3072]{1,0:T(8,128)(2,1)S(1)} %get-tuple-element.21.own), channel_id=1, source_target_pairs={{0,2},{1,3},{2,4},{3,5},{4,6},{5,7},{6,0},{7,1},{8,14},{9,15},{10,... | collective-permute-start | bytes 589832 | tf_op jit(solution)/shard_map/ppermute | solution.py:323
  31.1 2.6 %collective-permute-done.5.got.refs_3_ = bf16[32,3072]{1,0:T(8,128)(2,1)S(1)} collective-permute-done((bf16[32,3072]{1,0:T(8,128)(2,1)S(1)}, bf16[32,3072]{1,0:T(8,128)(2,1)S(1)}, u32[]{:S(2)}, u32[]{:S(2)}) %collective-permute-start.5) | collective-permute-done | bytes 196640 | tf_op jit(solution)/shard_map/ppermute | solution.py:323
  33.7 0.0 collective-permute-done.7.refs_2_
  33.7 0.3 collective-permute-done.6.refs_1_
  34.0 0.0 copy-start.4
  34.1 5.8 %collective-permute-start.9 = (bf16[288,1152]{1,0:T(8,128)(2,1)S(1)}, bf16[288,1152]{1,0:T(8,128)(2,1)S(1)}, u32[]{:S(2)}, u32[]{:S(2)}) collective-permute-start(bf16[288,1152]{1,0:T(8,128)(2,1)S(1)} %shard_map.105.refs_4_), channel_id=1, source_target_pairs={{0,8},{8,0},{16,24},{24,16},{32,40},{40,32},{48,56},{56,48},{64,72... | collective-permute-start | bytes 1990664 | tf_op jit(solution)/shard_map/ppermute | solution.py:328
  39.9 2.7 %collective-permute-start.8 = (bf16[288,1152]{1,0:T(8,128)(2,1)S(1)}, bf16[288,1152]{1,0:T(8,128)(2,1)S(1)}, u32[]{:S(2)}, u32[]{:S(2)}) collective-permute-start(bf16[288,1152]{1,0:T(8,128)(2,1)S(1)} %shard_map.105.refs_4_), channel_id=1, source_target_pairs={{0,2},{1,3},{2,4},{3,5},{4,6},{5,7},{6,0},{7,1},{8,14},{9,15},{10,... | collective-permute-start | bytes 1990664 | tf_op jit(solution)/shard_map/ppermute | solution.py:327
  42.6 0.0 copy-start.1
  42.6 2.3 %copy-done.1 = bf16[1536,1536]{1,0:T(8,128)(2,1)S(1)} copy-done((bf16[1536,1536]{1,0:T(8,128)(2,1)S(1)}, bf16[1536,1536]{1,0:T(8,128)(2,1)}, u32[]{:S(2)}) %copy-start.1) | copy-done | bytes 4718616
  44.9 1.9 %shard_map.104.refs_1_ = bf16[8,128,256]{2,1,0:T(8,128)(2,1)S(1)} custom-call(s32[3]{0:T(128)} %refs_0_.5, bf16[32,3072]{1,0:T(8,128)(2,1)S(1)} %get-tuple-element.21.own, bf16[32,3072]{1,0:T(8,128)(2,1)S(1)} %collective-permute-done.5.got.refs_3_, bf16[1536,1536]{1,0:T(8,128)(2,1)S(1)} %copy-done.1), custom_call_target="tpu_custom_call" | custom-call | tf_op jit(solution)/shard_map/pallas_call | solution.py:330
  46.9 0.0 copy-start.3
  46.9 0.0 collective-permute-done.9.refs_5_
  46.9 0.0 copy-done.2
  46.9 0.0 copy-done
  46.9 9.8 %shard_map.106 = (f32[8,128,128]{2,1,0:T(8,128)S(1)}, f32[8,128,128]{2,1,0:T(8,128)S(1)}, f32[8,128,128]{2,1,0:T(8,128)S(1)}) custom-call(s32[3]{0:T(128)} %refs_0_.5, bf16[8,128,256]{2,1,0:T(8,128)(2,1)S(1)} %shard_map.104.refs_1_, s32[4,1152]{1,0:T(4,128)S(1)} %copy-done.2, bf16[512,2048]{1,0:T(8,128)(2,1)S(1)} %copy-done, ...), custom_call_target="tpu_custom_call" | custom-call | tf_op jit(solution)/shard_map/pallas_call | solution.py:255
  56.7 0.0 collective-permute-done.8.refs_4_
  56.8 0.3 collective-permute-start.10
  57.1 0.0 copy-done.4
  57.1 7.5 %shard_map.107 = (f32[8,128,128]{2,1,0:T(8,128)S(1)}, f32[8,128,128]{2,1,0:T(8,128)S(1)}, f32[8,128,128]{2,1,0:T(8,128)S(1)}) custom-call(s32[3]{0:T(128)} %refs_0_.5, bf16[8,128,256]{2,1,0:T(8,128)(2,1)S(1)} %shard_map.104.refs_1_, s32[4,576]{1,0:T(4,128)S(1)} %copy-done.4, bf16[512,2048]{1,0:T(8,128)(2,1)S(1)} %copy-done, ...), custom_call_target="tpu_custom_call" | custom-call | tf_op jit(solution)/shard_map/pallas_call | solution.py:255
  64.6 0.0 collective-permute-done.10.refs_4_
  64.6 0.0 copy-done.3
  64.6 8.3 %shard_map.108 = bf16[128,1024]{1,0:T(8,128)(2,1)} custom-call(s32[3]{0:T(128)} %refs_0_.5, bf16[8,128,256]{2,1,0:T(8,128)(2,1)S(1)} %shard_map.104.refs_1_, s32[4,576]{1,0:T(4,128)S(1)} %copy-done.3, bf16[512,2048]{1,0:T(8,128)(2,1)S(1)} %copy-done, bf16[288,1152]{1,0:T(8,128)(2,1)S(1)} %collective-permute-done.10.refs_4_, ...), custom_call_target="tpu_custom_call" | custom-call | tf_op jit(solution)/shard_map/pallas_call | solution.py:255
  (3 shorter events, 0.1 us)
Async XLA Ops:
  0.0 46.9 %copy-start.2 = (s32[4,1152]{1,0:T(4,128)S(1)}, s32[4,1152]{1,0:T(4,128)}, u32[]{:S(2)}) copy-start(s32[4,1152]{1,0:T(4,128)} %constant.6.clone.refs_2_) | copy-start | bytes 55300
  0.0 46.9 %copy-start = (bf16[512,2048]{1,0:T(8,128)(2,1)S(1)}, bf16[512,2048]{1,0:T(8,128)(2,1)}, u32[]{:S(2)}) copy-start(bf16[512,2048]{1,0:T(8,128)(2,1)} %refs_3_.5) | copy-start | bytes 6291460
  1.1 5.4 %collective-permute-start = (bf16[16,2112]{1,0:T(8,128)(2,1)S(1)}, bf16[16,2112]{1,0:T(8,128)(2,1)S(1)}, u32[]{:S(2)}, u32[]{:S(2)}) collective-permute-start(bf16[16,2112]{1,0:T(8,128)(2,1)S(1)} %shard_map.100.own_ref), channel_id=1, source_target_pairs={{0,1},{1,0},{2,3},{3,2},{4,5},{5,4},{6,7},{7,6},{8,9},{9,8},{10,11... | collective-permute-start | bytes 202760 | tf_op jit(solution)/shard_map/ppermute | solution.py:299
  6.5 5.6 %collective-permute-start.1 = (bf16[16,4224]{1,0:T(8,128)(2,1)S(1)}, bf16[16,4224]{1,0:T(8,128)(2,1)S(1)}, u32[]{:S(2)}, u32[]{:S(2)}) collective-permute-start(bf16[16,4224]{1,0:T(8,128)(2,1)S(1)} %shard_map.101.own_ref), channel_id=1, source_target_pairs={{0,4},{1,5},{2,6},{3,7},{4,0},{5,1},{6,2},{7,3},{8,12},{9,13},{10,... | collective-permute-start | bytes 405512 | tf_op jit(solution)/shard_map/ppermute | solution.py:307
  12.1 9.4 %collective-permute-start.4 = (bf16[32,1152]{1,0:T(8,128)(2,1)S(1)}, bf16[32,1152]{1,0:T(8,128)(2,1)S(1)}, u32[]{:S(2)}, u32[]{:S(2)}) collective-permute-start(bf16[32,1152]{1,0:T(8,128)(2,1)S(1)} %get-tuple-element.20), channel_id=1, source_target_pairs={{0,112},{8,120},{16,128},{24,136},{32,144},{40,152},{48,160},{56,1... | collective-permute-start | bytes 221192 | tf_op jit(solution)/shard_map/ppermute | solution.py:318
  17.8 8.2 %collective-permute-start.3 = (bf16[32,1152]{1,0:T(8,128)(2,1)S(1)}, bf16[32,1152]{1,0:T(8,128)(2,1)S(1)}, u32[]{:S(2)}, u32[]{:S(2)}) collective-permute-start(bf16[32,1152]{1,0:T(8,128)(2,1)S(1)} %get-tuple-element.20), channel_id=1, source_target_pairs={{0,64},{8,72},{16,80},{24,88},{32,96},{40,104},{48,112},{56,120},{... | collective-permute-start | bytes 221192 | tf_op jit(solution)/shard_map/ppermute | solution.py:318
  19.9 6.9 %collective-permute-start.2 = (bf16[32,1152]{1,0:T(8,128)(2,1)S(1)}, bf16[32,1152]{1,0:T(8,128)(2,1)S(1)}, u32[]{:S(2)}, u32[]{:S(2)}) collective-permute-start(bf16[32,1152]{1,0:T(8,128)(2,1)S(1)} %get-tuple-element.20), channel_id=1, source_target_pairs={{0,16},{8,24},{16,32},{24,40},{32,48},{40,56},{48,64},{56,72},{64,... | collective-permute-start | bytes 221192 | tf_op jit(solution)/shard_map/ppermute | solution.py:318
  26.8 6.9 %collective-permute-start.7 = (bf16[96,1152]{1,0:T(8,128)(2,1)S(1)}, bf16[96,1152]{1,0:T(8,128)(2,1)S(1)}, u32[]{:S(2)}, u32[]{:S(2)}) collective-permute-start(bf16[96,1152]{1,0:T(8,128)(2,1)S(1)} %shard_map.103.refs_0_), channel_id=1, source_target_pairs={{0,240},{8,248},{16,0},{24,8},{32,16},{40,24},{48,32},{56,40},{64,... | collective-permute-start | bytes 663560 | tf_op jit(solution)/shard_map/ppermute | solution.py:321
  27.1 6.9 %collective-permute-start.6 = (bf16[96,1152]{1,0:T(8,128)(2,1)S(1)}, bf16[96,1152]{1,0:T(8,128)(2,1)S(1)}, u32[]{:S(2)}, u32[]{:S(2)}) collective-permute-start(bf16[96,1152]{1,0:T(8,128)(2,1)S(1)} %shard_map.103.refs_0_), channel_id=1, source_target_pairs={{0,16},{8,24},{16,32},{24,40},{32,48},{40,56},{48,64},{56,72},{64,... | collective-permute-start | bytes 663560 | tf_op jit(solution)/shard_map/ppermute | solution.py:320
  28.4 5.3 %collective-permute-start.5 = (bf16[32,3072]{1,0:T(8,128)(2,1)S(1)}, bf16[32,3072]{1,0:T(8,128)(2,1)S(1)}, u32[]{:S(2)}, u32[]{:S(2)}) collective-permute-start(bf16[32,3072]{1,0:T(8,128)(2,1)S(1)} %get-tuple-element.21.own), channel_id=1, source_target_pairs={{0,2},{1,3},{2,4},{3,5},{4,6},{5,7},{6,0},{7,1},{8,14},{9,15},{10,... | collective-permute-start | bytes 589832 | tf_op jit(solution)/shard_map/ppermute | solution.py:323
  34.0 23.0 %copy-start.4 = (s32[4,576]{1,0:T(4,128)S(1)}, s32[4,576]{1,0:T(4,128)}, u32[]{:S(2)}) copy-start(s32[4,576]{1,0:T(4,128)} %constant.7.clone.refs_2_) | copy-start | bytes 27652
  34.1 12.8 %collective-permute-start.9 = (bf16[288,1152]{1,0:T(8,128)(2,1)S(1)}, bf16[288,1152]{1,0:T(8,128)(2,1)S(1)}, u32[]{:S(2)}, u32[]{:S(2)}) collective-permute-start(bf16[288,1152]{1,0:T(8,128)(2,1)S(1)} %shard_map.105.refs_4_), channel_id=1, source_target_pairs={{0,8},{8,0},{16,24},{24,16},{32,40},{40,32},{48,56},{56,48},{64,72... | collective-permute-start | bytes 1990664 | tf_op jit(solution)/shard_map/ppermute | solution.py:328
  39.9 16.9 %collective-permute-start.8 = (bf16[288,1152]{1,0:T(8,128)(2,1)S(1)}, bf16[288,1152]{1,0:T(8,128)(2,1)S(1)}, u32[]{:S(2)}, u32[]{:S(2)}) collective-permute-start(bf16[288,1152]{1,0:T(8,128)(2,1)S(1)} %shard_map.105.refs_4_), channel_id=1, source_target_pairs={{0,2},{1,3},{2,4},{3,5},{4,6},{5,7},{6,0},{7,1},{8,14},{9,15},{10,... | collective-permute-start | bytes 1990664 | tf_op jit(solution)/shard_map/ppermute | solution.py:327
  42.6 2.3 %copy-start.1 = (bf16[1536,1536]{1,0:T(8,128)(2,1)S(1)}, bf16[1536,1536]{1,0:T(8,128)(2,1)}, u32[]{:S(2)}) copy-start(bf16[1536,1536]{1,0:T(8,128)(2,1)} %w_ref.1) | copy-start | bytes 14155780
  46.9 17.8 %copy-start.3 = (s32[4,576]{1,0:T(4,128)S(1)}, s32[4,576]{1,0:T(4,128)}, u32[]{:S(2)}) copy-start(s32[4,576]{1,0:T(4,128)} %constant.8.clone.refs_2_) | copy-start | bytes 27652
  56.8 7.9 %collective-permute-start.10 = (bf16[288,1152]{1,0:T(8,128)(2,1)S(1)}, bf16[288,1152]{1,0:T(8,128)(2,1)S(1)}, u32[]{:S(2)}, u32[]{:S(2)}) collective-permute-start(bf16[288,1152]{1,0:T(8,128)(2,1)S(1)} %collective-permute-done.8.refs_4_), channel_id=1, source_target_pairs={{0,8},{8,0},{16,24},{24,16},{32,40},{40,32},{48,56},{56,48},{64,72... | collective-permute-start | bytes 1990664 | tf_op jit(solution)/shard_map/ppermute | solution.py:344

commit v5 on v4

--- a/solution.py
+++ b/solution.py
@@ -21,6 +21,7 @@
 
 
 SMALL = pltpu.CompilerParams(vmem_limit_bytes=12 * 2**20)
+LARGE = pltpu.CompilerParams(vmem_limit_bytes=28 * 2**20)
 
 
 def fast(array):
@@ -68,6 +69,15 @@
         q_ref[n * size : (n + 1) * size, :] = ref[:, width:]
 
 
+def bundle_kernel(n_parts, *refs):
+    *parts, q_ref, coarse_ref, bundle_ref = refs
+    size, width = parts[0].shape
+    for n, ref in enumerate(parts):
+        coarse_ref[n * size : (n + 1) * size, :] = ref[...]
+        bundle_ref[:, n * width : (n + 1) * width] = ref[...]
+    bundle_ref[:, n_parts * width :] = q_ref[...]
+
+
 def join_kernel(sizes, n_after, *refs):
     outs = refs[len(refs) - len(sizes) :]
     at = 0
@@ -108,15 +118,22 @@
     return start
 
 
-def query_kernel(lengths, own, got, w_ref, out_ref, rows_ref):
+def query_kernel(q_at, lengths, own, got, w_hbm, out_ref, rows_ref, w_ref, arrived):
+    fetches = []
+    pairs, _, pair_width = w_ref.shape
+    for n in range(pairs):
+        columns = w_hbm.at[:, n * pair_width : (n + 1) * pair_width]
+        fetches.append(pltpu.make_async_copy(columns, w_ref.at[n], arrived.at[n]))
+        fetches[-1].start()
     chip, core, y, xh = here()
     width = rows_ref.shape[1]
-    for base, ref in ((y, own), (y + jnp.where(core == 0, 3, 1), got)):
+    for base, ref, lane_at in ((y, own, 0), (y + jnp.where(core == 0, 3, 1), got, q_at)):
         for n in range(4):
             turn, half = n // 2, n % 2
             place = lax.rem(base + 2 * turn, 4) * 32 + lax.rem(xh + half, 2) * 16
             at = pl.multiple_of(place, 16)
-            rows = ref[16 * turn : 16 * turn + 16, half * width : (half + 1) * width]
+            lanes = slice(lane_at + half * width, lane_at + (half + 1) * width)
+            rows = ref[16 * turn : 16 * turn + 16, lanes]
             rows_ref[pl.ds(at, 16), :] = rows
 
     shape = (rows_ref.shape[0], LANES)
@@ -135,10 +152,9 @@
         )
         return rope * cosine + turned * sine
 
-    width = 2 * (ND + RD)
-    for pair in range(w_ref.shape[1] // width):
-        w = w_ref[:, pair * width : (pair + 1) * width]
-        made = jnp.dot(rows_ref[...], w, preferred_element_type=jnp.float32)
+    for pair in range(pairs):
+        fetches[pair].wait()
+        made = jnp.dot(rows_ref[...], w_ref[pair], preferred_element_type=jnp.float32)
         out_ref[2 * pair, :, :ND] = made[:, :ND].astype(jnp.bfloat16)
         out_ref[2 * pair, :, ND:] = rotated(made[:, ND : ND + LANES]).astype(jnp.bfloat16)
         second = ND + RD
@@ -147,10 +163,10 @@
         out_ref[2 * pair + 1, :, ND:] = rotated(rope).astype(jnp.bfloat16)
 
 
-def attend_kernel(n_pieces, turn, first, last, *refs):
+def attend_kernel(views, group, first, last, *refs):
     lengths, q_ref, table_ref, w_ref = refs[:4]
-    pieces = refs[4 : 4 + n_pieces]
-    at = 4 + n_pieces
+    at = 4 + 1 + max(view[0] for view in views)
+    pieces = refs[4:at]
     if not first:
         max_in, sum_in, acc_in = refs[at : at + 3]
         at += 3
@@ -160,82 +176,104 @@
     else:
         max_out, sum_out, acc_out = refs[at : at + 3]
         at += 3
-    rows_ref, rope_ref, bias_ref = refs[at:]
-    size = pieces[0].shape[0]
-
-    for n, ref in enumerate(pieces):
-        low = pl.ds(n * size, size)
-        high = pl.ds((n_pieces + n) * size, size)
-        rows_ref[low, :] = ref[:, :KL]
-        rows_ref[high, :] = ref[:, KL : 2 * KL]
-        rope = ref[:, 2 * KL :]
-        rope_ref[low, :] = rope
-        rope_ref[high, :] = jnp.concatenate([rope[:, RD:], rope[:, :RD]], axis=1)
+    rows_ref, rope_ref, bias_ref, made_ref, score_ref, weight_ref = refs[at:]
+    heads = q_ref.shape[0]
+    tok_dev, n_keys = bias_ref.shape
+
+    row = 0
+    for piece, lane_at, *_ in views:
+        ref = pieces[piece]
+        size = ref.shape[0]
+        rope = ref[:, lane_at + 2 * KL : lane_at + 2 * (KL + RD)]
+        turned = jnp.concatenate([rope[:, RD:], rope[:, :RD]], axis=1)
+        for half in range(2):
+            to = slice(row + half * (n_keys // 2), row + half * (n_keys // 2) + size)
+            rows_ref[to, :] = ref[:, lane_at + half * KL : lane_at + (half + 1) * KL]
+            rope_ref[to, :] = turned if half else rope
+        row += size
 
     chip, core, y, xh = here()
-    tok_dev, n_keys = bias_ref.shape
     query_pos = (2 * chip + core) * tok_dev + lax.broadcasted_iota(jnp.int32, (tok_dev, 1), 0)
     query_start = document_start(query_pos, lengths)
-    ys = lax.rem(y + jnp.where(lax.rem(table_ref[1:2, :] + core, 2) == 0, 4 - turn, 4 + turn), 4)
-    ys = lax.rem(ys + table_ref[2:3, :], 4)
-    xs = lax.rem(xh + table_ref[3:4, :], 2)
-    parity = lax.rem(core + table_ref[1:2, :], 2)
-    key_pos = table_ref[0:1, :] + (2 * chip + parity) * tok_dev + ys * 32 + xs * 16
+    place, partner, turn, half, across = [table_ref[n : n + 1, :] for n in range(5)]
+    holder = lax.rem(core + partner, 2)
+    ys = lax.rem(y + turn + across * (3 - 2 * holder), 4)
+    xs = lax.rem(xh + half, 2)
+    key_pos = place + (2 * chip + holder) * tok_dev + ys * 32 + xs * 16
     allowed = (key_pos <= query_pos) & (key_pos >= query_start)
     bias_ref[...] = jnp.where(allowed, 0.0, MASKED)
 
-    for head in range(q_ref.shape[0]):
-        w = w_ref[:, head * (ND + VD) : (head + 1) * (ND + VD)]
-        expanded = jnp.dot(rows_ref[...], w, preferred_element_type=jnp.float32)
-        expanded = expanded.astype(jnp.bfloat16)
-        keys = jnp.concatenate([expanded[:, :ND], rope_ref[...]], axis=1)
+    def expand(head):
+        columns = slice(head * (ND + VD), (head + 1) * (ND + VD))
+        made = jnp.dot(rows_ref[...], w_ref[:, columns], preferred_element_type=jnp.float32)
+        made_ref[:, columns] = made.astype(jnp.bfloat16)
+
+    def score(head):
+        at = head * (ND + VD)
+        keys = jnp.concatenate([made_ref[:, at : at + ND], rope_ref[...]], axis=1)
         scores = lax.dot_general(
             q_ref[head], keys, (((1,), (1,)), ((), ())), preferred_element_type=jnp.float32
         )
-        scores = scores * SCORE_SCALE + bias_ref[...]
+        score_ref[head] = scores * SCORE_SCALE + bias_ref[...]
+
+    def weigh(head):
+        scores = score_ref[head]
         top = jnp.max(scores, axis=1, keepdims=True)
-        if first:
-            new_max = jnp.maximum(top, FLOOR)
-        else:
-            old_max = max_in[head][:, :1]
-            new_max = jnp.maximum(top, old_max)
+        old_max = FLOOR if first else max_in[head][:, :1]
+        new_max = jnp.maximum(top, old_max)
         weights = jnp.exp2(scores - new_max)
         total = jnp.sum(weights, axis=1, keepdims=True)
-        mixed = jnp.dot(
-            weights.astype(jnp.bfloat16), expanded[:, ND:], preferred_element_type=jnp.float32
-        )
+        weight_ref[head] = weights.astype(jnp.bfloat16)
+        if first:
+            return new_max, total, None
+        faded = jnp.exp2(old_max - new_max)
+        return new_max, total + faded * sum_in[head][:, :1], faded
+
+    def mix(head, new_max, total, faded):
+        at = head * (ND + VD) + ND
+        values = made_ref[:, at : at + VD]
+        mixed = jnp.dot(weight_ref[head], values, preferred_element_type=jnp.float32)
         if not first:
-            faded = jnp.exp2(old_max - new_max)
-            total = total + faded * sum_in[head][:, :1]
             mixed = mixed + faded * acc_in[head]
         if last:
-            out_ref[:, head * VD : (head + 1) * VD] = (mixed / total).astype(jnp.bfloat16)
+            out_ref[:, head * VD : (head + 1) * VD] = (mixed * (1.0 / total)).astype(jnp.bfloat16)
         else:
             max_out[head] = jnp.broadcast_to(new_max, mixed.shape)
             sum_out[head] = jnp.broadcast_to(total, mixed.shape)
             acc_out[head] = mixed
 
-
-def key_table(slots, rows, tok_dev, partners):
-    coarse = len(slots) // 3
-    held = []
-    for part in range(3):
-        for k in slots[part * coarse : (part + 1) * coarse]:
-            for turn in (0, 2):
-                held += [(row - 2 * k * tok_dev, turn) for row in range(rows)]
-    columns = [
-        (place, partner, turn, half)
-        for half in range(2)
-        for partner in partners
-        for place, turn in held
-    ]
+    groups = [range(low, low + group) for low in range(0, heads, group)]
+    found = {}
+    for step in range(len(groups) + 3):
+        if step < len(groups):
+            for head in groups[step]:
+                expand(head)
+        if 0 <= step - 1 < len(groups):
+            for head in groups[step - 1]:
+                score(head)
+        if 0 <= step - 2 < len(groups):
+            for head in groups[step - 2]:
+                found[head] = weigh(head)
+        if 0 <= step - 3:
+            for head in groups[step - 3]:
+                mix(head, *found[head])
+
+
+def key_table(views, rows, tok_dev):
+    columns = []
+    for half in range(2):
+        for _, _, partner, across, slots in views:
+            for k in slots:
+                for turn in (0, 2):
+                    place = [row - 2 * k * tok_dev for row in range(rows)]
+                    columns += [(p, partner, turn, half, across) for p in place]
     return np.array(columns, np.int32).T
 
 
-def attend(doc_lengths, queries, slots, w_kv, pieces, turn, partners, state, last):
+def attend(doc_lengths, queries, w_kv, pieces, views, group, state, last):
     heads, rows, width = queries.shape
     first = state is None
-    table = jnp.asarray(key_table(slots, 16, rows, partners))
+    table = jnp.asarray(key_table(views, 16, rows))
     count = table.shape[1]
     vmem = pl.BlockSpec(memory_space=pltpu.VMEM)
     args = [queries, table, w_kv, *pieces]
@@ -250,7 +288,7 @@
         out_specs = [vmem] * 3
 
     def kernel(*refs):
-        attend_kernel(len(pieces), turn, first, last, *refs)
+        attend_kernel(views, group, first, last, *refs)
 
     return pl.pallas_call(
         kernel,
@@ -261,8 +299,11 @@
             pltpu.VMEM((count, KL), jnp.bfloat16),
             pltpu.VMEM((count, LANES), jnp.bfloat16),
             pltpu.VMEM((rows, count), jnp.float32),
+            pltpu.VMEM((count, w_kv.shape[1]), jnp.bfloat16),
+            pltpu.VMEM((heads, rows, count), jnp.float32),
+            pltpu.VMEM((heads, rows, count), jnp.bfloat16),
         ],
-        compiler_params=SMALL,
+        compiler_params=LARGE,
     )(*args)
 
 
@@ -316,34 +357,62 @@
         compiler_params=SMALL,
     )(fast(both), fast(opposite))
     coarse = [lax.ppermute(piece, "ctx", chip_shift(step)) for step in COARSE]
-    (coarse,) = join([coarse])
+    set_shape = coarse[0].shape
+    q_at = len(COARSE) * set_shape[1]
+    coarse, bundle = pl.pallas_call(
+        lambda *refs: bundle_kernel(len(COARSE), *refs),
+        in_specs=[vmem] * (len(COARSE) + 1),
+        out_specs=[vmem] * 2,
+        out_shape=[
+            pltpu.VMEM((len(COARSE) * set_shape[0], set_shape[1]), jnp.bfloat16),
+            pltpu.VMEM((set_shape[0], q_at + q_set.shape[1]), jnp.bfloat16),
+        ],
+        compiler_params=SMALL,
+    )(*[fast(a) for a in (*coarse, q_set)])
     later = lax.ppermute(coarse, "ctx", chip_shift(1))
     sooner = lax.ppermute(coarse, "ctx", chip_shift(-1))
-    q_set, coarse = lax.optimization_barrier((q_set, coarse))
-    q_got = lax.ppermute(q_set, ("ctx", "head"), apart)
-
-    slots = [*COARSE, *[k + 1 for k in COARSE], *[k - 1 for k in COARSE]]
-    (held,) = join([[coarse, later, sooner]], after=[q_got])
-    received = lax.ppermute(held, ("ctx", "head"), apart)
-    own_swapped = lax.ppermute(held, "ctx", swap)
-
+    got = lax.ppermute(bundle, ("ctx", "head"), apart)
+    coarse_swapped = lax.ppermute(coarse, "ctx", swap)
+
+    (near,) = join([[later, sooner]])
+    received = lax.ppermute(near, ("ctx", "head"), apart)
+    near_swapped = lax.ppermute(near, "ctx", swap)
+    got_swapped = lax.ppermute(got, "ctx", swap)
+
+    pairs = heads_here // 2
     queries = pl.pallas_call(
-        query_kernel,
-        in_specs=[pl.BlockSpec(memory_space=pltpu.SMEM)] + [vmem] * 3,
+        lambda *refs: query_kernel(q_at, *refs),
+        in_specs=[
+            pl.BlockSpec(memory_space=pltpu.SMEM),
+            vmem,
+            vmem,
+            pl.BlockSpec(memory_space=pl.ANY),
+        ],
         out_specs=vmem,
         out_shape=pltpu.VMEM((heads_here, tok_dev, 2 * LANES), jnp.bfloat16),
-        scratch_shapes=[pltpu.VMEM((tok_dev, w_query.shape[0]), jnp.bfloat16)],
-        compiler_params=SMALL,
-    )(slow(doc_lengths), *[fast(a) for a in (q_set, q_got, w_query)])
-
-    def attend_to(pieces, turn, partners, state, last=False):
-        return attend(doc_lengths, queries, slots, w_kv, pieces, turn, partners, state, last)
-
-    state = attend_to([held, own_swapped], 0, [0, 1], None)
+        scratch_shapes=[
+            pltpu.VMEM((tok_dev, w_query.shape[0]), jnp.bfloat16),
+            pltpu.VMEM((pairs, w_query.shape[0], w_query.shape[1] // pairs), jnp.bfloat16),
+            pltpu.SemaphoreType.DMA((pairs,)),
+        ],
+        compiler_params=SMALL,
+    )(slow(doc_lengths), fast(q_set), fast(got), slow(w_query))
+
+    def attend_to(pieces, views, group, state, last=False):
+        return attend(doc_lengths, queries, w_kv, pieces, views, group, state, last)
+
+    near_slots = [*[k + 1 for k in COARSE], *[k - 1 for k in COARSE]]
+    views = [(0, 0, 0, 0, COARSE), (1, 0, 0, 0, near_slots)]
+    views += [(2, 0, 1, 0, COARSE), (3, 0, 1, 0, near_slots)]
+    for partner in range(2):
+        for n, k in enumerate(COARSE):
+            views.append((4 + partner, n * set_shape[1], partner, 1, [k]))
+    pieces = [coarse, near, coarse_swapped, near_swapped, got, got_swapped]
+    state = attend_to(pieces, views, 2, None)
     received, state = lax.optimization_barrier((received, state))
     swapped = lax.ppermute(received, "ctx", swap)
-    state = attend_to([received], 1, [0], state)
-    return attend_to([swapped], 1, [1], state, last=True)
+    state = attend_to([received], [(0, 0, 0, 1, near_slots)], 1, state)
+    return attend_to([swapped], [(0, 0, 1, 1, near_slots)], 1, state, last=True)
 
 
 def solution(mesh):

time: 73.1 us -> 63.5 us (0.87)
  Pallas kernels: 28.8 us -> 20.7 us
  waiting for transfers between devices: 12.3 us -> 15.1 us
  local copies, waits for them, and re-layouts: 2.35 us -> 0.02 us
  starting transfers between devices: 29.3 us -> 27.4 us
    pallas_call x3, Pallas kernels: 25.7 us -> 15.2 us  [attend(): pl.pallas_call(kernel, in_specs=[pl.BlockSpec(memory_space=pltpu.SMEM)] +...]
    ppermute x1, waiting for transfers between devices: 0.01 us -> 3.32 us  [body(): sooner = lax.ppermute(coarse, 'ctx', chip_shift(-1))]
    ppermute x3 -> x5, waiting for transfers between devices: 2.62 us -> 0.01 us  [the longest x1 0.01 us: body(): got_swapped = lax.ppermute(got, 'ctx', swap)]
    pallas_call x1 -> x2, Pallas kernels: 1.94 us -> 4.31 us  [the longest x1 4.26 us: body(): pl.pallas_call(lambda *refs: query_kernel(q_at, *refs), in_specs=[pl.Bloc...]
    unnamed x10 -> x8, local copies, waits for them, and re-layouts: 2.35 us -> 0.02 us
    ppermute x3 -> x5, starting transfers between devices: 11.2 us -> 9.08 us  [the longest x1 4.43 us: body(): near_swapped = lax.ppermute(near, 'ctx', swap)]
    ppermute x1, waiting for transfers between devices: 0.33 us -> 2.37 us  [body(): later = lax.ppermute(coarse, 'ctx', chip_shift(1))]
  transfers between devices with their start and end apart: 11 -> 13, of which waited for: 6 -> 6; matrix products, arithmetic and copies ran while one was open for 0% -> 0% of each run, Pallas kernels for 26% -> 24%
where the time goes in v5:
time: 63.5 us; the launch traced here: 63.4 us
  starting transfers between devices  27.4 us (43%)
  Pallas kernels  20.7 us (33%)
  waiting for transfers between devices  15.1 us (24%)
    pallas_call x3, Pallas kernels, attend(): pl.pallas_call(kernel, in_specs=[pl.BlockSpec(memory_space=pltpu.SMEM)] +...  15.2 us
    ppermute x3, starting transfers between devices, body(): coarse = [lax.ppermute(piece, 'ctx', chip_shift(step)) for step in COARSE]  9.43 us
    ppermute x3, waiting for transfers between devices, body(): coarse = [lax.ppermute(piece, 'ctx', chip_shift(step)) for step in COARSE]  5.25 us
    ppermute x1, starting transfers between devices, body(): near_swapped = lax.ppermute(near, 'ctx', swap)  4.43 us
    pallas_call x1, Pallas kernels, body(): pl.pallas_call(lambda *refs: query_kernel(q_at, *refs), in_specs=[pl.Bloc...  4.26 us
    ppermute x1, starting transfers between devices, body(): other = lax.ppermute(rows, 'head', across_x)  3.66 us
    ppermute x1, waiting for transfers between devices, body(): sooner = lax.ppermute(coarse, 'ctx', chip_shift(-1))  3.32 us
    ppermute x1, starting transfers between devices, body(): opposite = lax.ppermute(both, 'head', across_y)  3.16 us
  transfers between devices with their start and end apart: 13, of which 6 were waited for; matrix products, arithmetic and copies ran while one was open for 0% of the time, Pallas kernels for 24%

profile of v5, /device:TPU:1, one launch (start us, length us, event | category | flops | bytes accessed | tf_op | source)
XLA Modules:
  0.0 63.4 jit_solution(13419752217144087320)
XLA Ops:
  0.0 0.0 copy-start.1
  0.0 0.0 copy-start
  0.0 1.1 %shard_map.100.own_ref = bf16[16,2112]{1,0:T(8,128)(2,1)S(1)} custom-call(bf16[16,1536]{1,0:T(8,128)(2,1)} %q_ref.1, f32[1536]{0:T(1024)} %q_gain_ref.1, bf16[16,576]{1,0:T(8,128)(2,1)} %kv_ref.1, f32[512]{0:T(512)} %kv_gain_ref.1), custom_call_target="tpu_custom_call" | custom-call | tf_op jit(solution)/shard_map/pallas_call | solution.py:335
  1.1 3.7 %collective-permute-start = (bf16[16,2112]{1,0:T(8,128)(2,1)S(1)}, bf16[16,2112]{1,0:T(8,128)(2,1)S(1)}, u32[]{:S(2)}, u32[]{:S(2)}) collective-permute-start(bf16[16,2112]{1,0:T(8,128)(2,1)S(1)} %shard_map.100.own_ref), channel_id=1, source_target_pairs={{0,1},{1,0},{2,3},{3,2},{4,5},{5,4},{6,7},{7,6},{8,9},{9,8},{10,11... | collective-permute-start | bytes 202760 | tf_op jit(solution)/shard_map/ppermute | solution.py:340
  4.7 1.7 %collective-permute-done.other_ref = bf16[16,2112]{1,0:T(8,128)(2,1)S(1)} collective-permute-done((bf16[16,2112]{1,0:T(8,128)(2,1)S(1)}, bf16[16,2112]{1,0:T(8,128)(2,1)S(1)}, u32[]{:S(2)}, u32[]{:S(2)}) %collective-permute-start) | collective-permute-done | bytes 67616 | tf_op jit(solution)/shard_map/ppermute | solution.py:340
  6.4 0.1 shard_map.101.own_ref
  6.5 3.2 %collective-permute-start.1 = (bf16[16,4224]{1,0:T(8,128)(2,1)S(1)}, bf16[16,4224]{1,0:T(8,128)(2,1)S(1)}, u32[]{:S(2)}, u32[]{:S(2)}) collective-permute-start(bf16[16,4224]{1,0:T(8,128)(2,1)S(1)} %shard_map.101.own_ref), channel_id=1, source_target_pairs={{0,4},{1,5},{2,6},{3,7},{4,0},{5,1},{6,2},{7,3},{8,12},{9,13},{10,... | collective-permute-start | bytes 405512 | tf_op jit(solution)/shard_map/ppermute | solution.py:348
  9.7 2.4 %collective-permute-done.1.got_ref = bf16[16,4224]{1,0:T(8,128)(2,1)S(1)} collective-permute-done((bf16[16,4224]{1,0:T(8,128)(2,1)S(1)}, bf16[16,4224]{1,0:T(8,128)(2,1)S(1)}, u32[]{:S(2)}, u32[]{:S(2)}) %collective-permute-start.1) | collective-permute-done | bytes 135200 | tf_op jit(solution)/shard_map/ppermute | solution.py:348
  12.1 5.7 %collective-permute-start.4 = (bf16[32,1152]{1,0:T(8,128)(2,1)S(1)}, bf16[32,1152]{1,0:T(8,128)(2,1)S(1)}, u32[]{:S(2)}, u32[]{:S(2)}) collective-permute-start(bf16[32,1152]{1,0:T(8,128)(2,1)S(1)} %get-tuple-element.20), channel_id=1, source_target_pairs={{0,112},{8,120},{16,128},{24,136},{32,144},{40,152},{48,160},{56,1... | collective-permute-start | bytes 221192 | tf_op jit(solution)/shard_map/ppermute | solution.py:359
  17.8 2.1 %collective-permute-start.3 = (bf16[32,1152]{1,0:T(8,128)(2,1)S(1)}, bf16[32,1152]{1,0:T(8,128)(2,1)S(1)}, u32[]{:S(2)}, u32[]{:S(2)}) collective-permute-start(bf16[32,1152]{1,0:T(8,128)(2,1)S(1)} %get-tuple-element.20), channel_id=1, source_target_pairs={{0,64},{8,72},{16,80},{24,88},{32,96},{40,104},{48,112},{56,120},{... | collective-permute-start | bytes 221192 | tf_op jit(solution)/shard_map/ppermute | solution.py:359
  19.9 1.6 %collective-permute-start.2 = (bf16[32,1152]{1,0:T(8,128)(2,1)S(1)}, bf16[32,1152]{1,0:T(8,128)(2,1)S(1)}, u32[]{:S(2)}, u32[]{:S(2)}) collective-permute-start(bf16[32,1152]{1,0:T(8,128)(2,1)S(1)} %get-tuple-element.20), channel_id=1, source_target_pairs={{0,16},{8,24},{16,32},{24,40},{32,48},{40,56},{48,64},{56,72},{64,... | collective-permute-start | bytes 221192 | tf_op jit(solution)/shard_map/ppermute | solution.py:359
  21.5 0.0 collective-permute-done.4.refs_2_
  21.5 4.5 %collective-permute-done.3.refs_1_ = bf16[32,1152]{1,0:T(8,128)(2,1)S(1)} collective-permute-done((bf16[32,1152]{1,0:T(8,128)(2,1)S(1)}, bf16[32,1152]{1,0:T(8,128)(2,1)S(1)}, u32[]{:S(2)}, u32[]{:S(2)}) %collective-permute-start.3) | collective-permute-done | bytes 73760 | tf_op jit(solution)/shard_map/ppermute | solution.py:359
  26.0 0.8 %collective-permute-done.2.refs_0_ = bf16[32,1152]{1,0:T(8,128)(2,1)S(1)} collective-permute-done((bf16[32,1152]{1,0:T(8,128)(2,1)S(1)}, bf16[32,1152]{1,0:T(8,128)(2,1)S(1)}, u32[]{:S(2)}, u32[]{:S(2)}) %collective-permute-start.2) | collective-permute-done | bytes 73760 | tf_op jit(solution)/shard_map/ppermute | solution.py:359
  26.8 2.8 %collective-permute-start.5 = (bf16[32,6528]{1,0:T(8,128)(2,1)S(1)}, bf16[32,6528]{1,0:T(8,128)(2,1)S(1)}, u32[]{:S(2)}, u32[]{:S(2)}) collective-permute-start(bf16[32,6528]{1,0:T(8,128)(2,1)S(1)} %get-tuple-element.21), channel_id=1, source_target_pairs={{0,2},{1,3},{2,4},{3,5},{4,6},{5,7},{6,0},{7,1},{8,14},{9,15},{10,... | collective-permute-start | bytes 1253384 | tf_op jit(solution)/shard_map/ppermute | solution.py:374
  29.7 0.3 collective-permute-start.7
  29.9 1.2 %collective-permute-start.6 = (bf16[96,1152]{1,0:T(8,128)(2,1)S(1)}, bf16[96,1152]{1,0:T(8,128)(2,1)S(1)}, u32[]{:S(2)}, u32[]{:S(2)}) collective-permute-start(bf16[96,1152]{1,0:T(8,128)(2,1)S(1)} %get-tuple-element.22.refs_4_), channel_id=1, source_target_pairs={{0,16},{8,24},{16,32},{24,40},{32,48},{40,56},{48,64},{56,72},{64,... | collective-permute-start | bytes 663560 | tf_op jit(solution)/shard_map/ppermute | solution.py:372
  31.1 3.3 %collective-permute-done.7.refs_1_ = bf16[96,1152]{1,0:T(8,128)(2,1)S(1)} collective-permute-done((bf16[96,1152]{1,0:T(8,128)(2,1)S(1)}, bf16[96,1152]{1,0:T(8,128)(2,1)S(1)}, u32[]{:S(2)}, u32[]{:S(2)}) %collective-permute-start.7) | collective-permute-done | bytes 221216 | tf_op jit(solution)/shard_map/ppermute | solution.py:373
  34.4 2.4 %collective-permute-done.6.refs_0_ = bf16[96,1152]{1,0:T(8,128)(2,1)S(1)} collective-permute-done((bf16[96,1152]{1,0:T(8,128)(2,1)S(1)}, bf16[96,1152]{1,0:T(8,128)(2,1)S(1)}, u32[]{:S(2)}, u32[]{:S(2)}) %collective-permute-start.6) | collective-permute-done | bytes 221216 | tf_op jit(solution)/shard_map/ppermute | solution.py:372
  36.8 0.0 copy-start.3
  36.9 4.4 %collective-permute-start.10 = (bf16[192,1152]{1,0:T(8,128)(2,1)S(1)}, bf16[192,1152]{1,0:T(8,128)(2,1)S(1)}, u32[]{:S(2)}, u32[]{:S(2)}) collective-permute-start(bf16[192,1152]{1,0:T(8,128)(2,1)S(1)} %shard_map.105.refs_5_), channel_id=1, source_target_pairs={{0,8},{8,0},{16,24},{24,16},{32,40},{40,32},{48,56},{56,48},{64,72... | collective-permute-start | bytes 1327112 | tf_op jit(solution)/shard_map/ppermute | solution.py:379
  41.3 1.3 %collective-permute-start.8 = (bf16[192,1152]{1,0:T(8,128)(2,1)S(1)}, bf16[192,1152]{1,0:T(8,128)(2,1)S(1)}, u32[]{:S(2)}, u32[]{:S(2)}) collective-permute-start(bf16[192,1152]{1,0:T(8,128)(2,1)S(1)} %shard_map.105.refs_5_), channel_id=1, source_target_pairs={{0,2},{1,3},{2,4},{3,5},{4,6},{5,7},{6,0},{7,1},{8,14},{9,15},{10,... | collective-permute-start | bytes 1327112 | tf_op jit(solution)/shard_map/ppermute | solution.py:378
  42.6 0.0 collective-permute-done.5.refs_2_.refs_8_
  42.6 0.3 collective-permute-start.11
  43.0 0.2 collective-permute-start.9
  43.1 4.3 %shard_map.104.refs_1_ = bf16[8,128,256]{2,1,0:T(8,128)(2,1)S(1)} custom-call(s32[3]{0:T(128)} %refs_0_.7, bf16[32,3072]{1,0:T(8,128)(2,1)S(1)} %get-tuple-element.19.refs_3_.refs_1_, bf16[32,6528]{1,0:T(8,128)(2,1)S(1)} %collective-permute-done.5.refs_2_.refs_8_, bf16[1536,1536]{1,0:T(8,128)(2,1)} %refs_3_.4), custom_call_target="tpu_custom_call" | custom-call | tf_op jit(solution)/shard_map/pallas_call | solution.py:383
  47.4 0.0 copy-start.2
  47.4 0.0 collective-permute-done.9.refs_6_
  47.4 0.0 collective-permute-done.10.refs_7_
  47.4 0.0 collective-permute-done.11.refs_9_
  47.4 0.0 copy-done.1
  47.5 0.0 copy-done
  47.5 7.9 %shard_map.106 = (f32[8,128,128]{2,1,0:T(8,128)S(1)}, f32[8,128,128]{2,1,0:T(8,128)S(1)}, f32[8,128,128]{2,1,0:T(8,128)S(1)}) custom-call(s32[3]{0:T(128)} %refs_0_.7, bf16[8,128,256]{2,1,0:T(8,128)(2,1)S(1)} %shard_map.104.refs_1_, s32[5,1536]{1,0:T(8,128)S(1)} %copy-done.1, bf16[512,2048]{1,0:T(8,128)(2,1)S(1)} %copy-done, ...), custom_call_target="tpu_custom_call" | custom-call | tf_op jit(solution)/shard_map/pallas_call | solution.py:293
  55.4 0.0 collective-permute-done.8.refs_4_
  55.4 0.6 %collective-permute-start.12 = (bf16[192,1152]{1,0:T(8,128)(2,1)S(1)}, bf16[192,1152]{1,0:T(8,128)(2,1)S(1)}, u32[]{:S(2)}, u32[]{:S(2)}) collective-permute-start(bf16[192,1152]{1,0:T(8,128)(2,1)S(1)} %collective-permute-done.8.refs_4_), channel_id=1, source_target_pairs={{0,8},{8,0},{16,24},{24,16},{32,40},{40,32},{48,56},{56,48},{64,72... | collective-permute-start | bytes 1327112 | tf_op jit(solution)/shard_map/ppermute | solution.py:413
  56.0 0.0 copy-done.3
  56.0 3.3 %shard_map.107 = (f32[8,128,128]{2,1,0:T(8,128)S(1)}, f32[8,128,128]{2,1,0:T(8,128)S(1)}, f32[8,128,128]{2,1,0:T(8,128)S(1)}) custom-call(s32[3]{0:T(128)} %refs_0_.7, bf16[8,128,256]{2,1,0:T(8,128)(2,1)S(1)} %shard_map.104.refs_1_, s32[5,384]{1,0:T(8,128)S(1)} %copy-done.3, bf16[512,2048]{1,0:T(8,128)(2,1)S(1)} %copy-done, ...), custom_call_target="tpu_custom_call" | custom-call | tf_op jit(solution)/shard_map/pallas_call | solution.py:293
  59.3 0.0 collective-permute-done.12.refs_4_
  59.3 0.0 copy-done.2
  59.3 4.0 %shard_map.108 = bf16[128,1024]{1,0:T(8,128)(2,1)} custom-call(s32[3]{0:T(128)} %refs_0_.7, bf16[8,128,256]{2,1,0:T(8,128)(2,1)S(1)} %shard_map.104.refs_1_, s32[5,384]{1,0:T(8,128)S(1)} %copy-done.2, bf16[512,2048]{1,0:T(8,128)(2,1)S(1)} %copy-done, bf16[192,1152]{1,0:T(8,128)(2,1)S(1)} %collective-permute-done.12.refs_4_, ...), custom_call_target="tpu_custom_call" | custom-call | tf_op jit(solution)/shard_map/pallas_call | solution.py:293
  (3 shorter events, 0.1 us)
Async XLA Ops:
  0.0 47.4 %copy-start.1 = (s32[5,1536]{1,0:T(8,128)S(1)}, s32[5,1536]{1,0:T(8,128)}, u32[]{:S(2)}) copy-start(s32[5,1536]{1,0:T(8,128)} %constant.6.clone.refs_2_) | copy-start | bytes 92164
  0.0 47.5 %copy-start = (bf16[512,2048]{1,0:T(8,128)(2,1)S(1)}, bf16[512,2048]{1,0:T(8,128)(2,1)}, u32[]{:S(2)}) copy-start(bf16[512,2048]{1,0:T(8,128)(2,1)} %refs_3_.7) | copy-start | bytes 6291460
  1.1 5.4 %collective-permute-start = (bf16[16,2112]{1,0:T(8,128)(2,1)S(1)}, bf16[16,2112]{1,0:T(8,128)(2,1)S(1)}, u32[]{:S(2)}, u32[]{:S(2)}) collective-permute-start(bf16[16,2112]{1,0:T(8,128)(2,1)S(1)} %shard_map.100.own_ref), channel_id=1, source_target_pairs={{0,1},{1,0},{2,3},{3,2},{4,5},{5,4},{6,7},{7,6},{8,9},{9,8},{10,11... | collective-permute-start | bytes 202760 | tf_op jit(solution)/shard_map/ppermute | solution.py:340
  6.5 5.6 %collective-permute-start.1 = (bf16[16,4224]{1,0:T(8,128)(2,1)S(1)}, bf16[16,4224]{1,0:T(8,128)(2,1)S(1)}, u32[]{:S(2)}, u32[]{:S(2)}) collective-permute-start(bf16[16,4224]{1,0:T(8,128)(2,1)S(1)} %shard_map.101.own_ref), channel_id=1, source_target_pairs={{0,4},{1,5},{2,6},{3,7},{4,0},{5,1},{6,2},{7,3},{8,12},{9,13},{10,... | collective-permute-start | bytes 405512 | tf_op jit(solution)/shard_map/ppermute | solution.py:348
  12.1 9.4 %collective-permute-start.4 = (bf16[32,1152]{1,0:T(8,128)(2,1)S(1)}, bf16[32,1152]{1,0:T(8,128)(2,1)S(1)}, u32[]{:S(2)}, u32[]{:S(2)}) collective-permute-start(bf16[32,1152]{1,0:T(8,128)(2,1)S(1)} %get-tuple-element.20), channel_id=1, source_target_pairs={{0,112},{8,120},{16,128},{24,136},{32,144},{40,152},{48,160},{56,1... | collective-permute-start | bytes 221192 | tf_op jit(solution)/shard_map/ppermute | solution.py:359
  17.8 8.2 %collective-permute-start.3 = (bf16[32,1152]{1,0:T(8,128)(2,1)S(1)}, bf16[32,1152]{1,0:T(8,128)(2,1)S(1)}, u32[]{:S(2)}, u32[]{:S(2)}) collective-permute-start(bf16[32,1152]{1,0:T(8,128)(2,1)S(1)} %get-tuple-element.20), channel_id=1, source_target_pairs={{0,64},{8,72},{16,80},{24,88},{32,96},{40,104},{48,112},{56,120},{... | collective-permute-start | bytes 221192 | tf_op jit(solution)/shard_map/ppermute | solution.py:359
  19.9 6.9 %collective-permute-start.2 = (bf16[32,1152]{1,0:T(8,128)(2,1)S(1)}, bf16[32,1152]{1,0:T(8,128)(2,1)S(1)}, u32[]{:S(2)}, u32[]{:S(2)}) collective-permute-start(bf16[32,1152]{1,0:T(8,128)(2,1)S(1)} %get-tuple-element.20), channel_id=1, source_target_pairs={{0,16},{8,24},{16,32},{24,40},{32,48},{40,56},{48,64},{56,72},{64,... | collective-permute-start | bytes 221192 | tf_op jit(solution)/shard_map/ppermute | solution.py:359
  26.8 15.8 %collective-permute-start.5 = (bf16[32,6528]{1,0:T(8,128)(2,1)S(1)}, bf16[32,6528]{1,0:T(8,128)(2,1)S(1)}, u32[]{:S(2)}, u32[]{:S(2)}) collective-permute-start(bf16[32,6528]{1,0:T(8,128)(2,1)S(1)} %get-tuple-element.21), channel_id=1, source_target_pairs={{0,2},{1,3},{2,4},{3,5},{4,6},{5,7},{6,0},{7,1},{8,14},{9,15},{10,... | collective-permute-start | bytes 1253384 | tf_op jit(solution)/shard_map/ppermute | solution.py:374
  29.7 4.8 %collective-permute-start.7 = (bf16[96,1152]{1,0:T(8,128)(2,1)S(1)}, bf16[96,1152]{1,0:T(8,128)(2,1)S(1)}, u32[]{:S(2)}, u32[]{:S(2)}) collective-permute-start(bf16[96,1152]{1,0:T(8,128)(2,1)S(1)} %get-tuple-element.22.refs_4_), channel_id=1, source_target_pairs={{0,240},{8,248},{16,0},{24,8},{32,16},{40,24},{48,32},{56,40},{64,... | collective-permute-start | bytes 663560 | tf_op jit(solution)/shard_map/ppermute | solution.py:373
  29.9 6.9 %collective-permute-start.6 = (bf16[96,1152]{1,0:T(8,128)(2,1)S(1)}, bf16[96,1152]{1,0:T(8,128)(2,1)S(1)}, u32[]{:S(2)}, u32[]{:S(2)}) collective-permute-start(bf16[96,1152]{1,0:T(8,128)(2,1)S(1)} %get-tuple-element.22.refs_4_), channel_id=1, source_target_pairs={{0,16},{8,24},{16,32},{24,40},{32,48},{40,56},{48,64},{56,72},{64,... | collective-permute-start | bytes 663560 | tf_op jit(solution)/shard_map/ppermute | solution.py:372
  36.8 19.2 %copy-start.3 = (s32[5,384]{1,0:T(8,128)S(1)}, s32[5,384]{1,0:T(8,128)}, u32[]{:S(2)}) copy-start(s32[5,384]{1,0:T(8,128)} %constant.7.clone.refs_2_) | copy-start | bytes 23044
  36.9 10.6 %collective-permute-start.10 = (bf16[192,1152]{1,0:T(8,128)(2,1)S(1)}, bf16[192,1152]{1,0:T(8,128)(2,1)S(1)}, u32[]{:S(2)}, u32[]{:S(2)}) collective-permute-start(bf16[192,1152]{1,0:T(8,128)(2,1)S(1)} %shard_map.105.refs_5_), channel_id=1, source_target_pairs={{0,8},{8,0},{16,24},{24,16},{32,40},{40,32},{48,56},{56,48},{64,72... | collective-permute-start | bytes 1327112 | tf_op jit(solution)/shard_map/ppermute | solution.py:379
  41.3 14.1 %collective-permute-start.8 = (bf16[192,1152]{1,0:T(8,128)(2,1)S(1)}, bf16[192,1152]{1,0:T(8,128)(2,1)S(1)}, u32[]{:S(2)}, u32[]{:S(2)}) collective-permute-start(bf16[192,1152]{1,0:T(8,128)(2,1)S(1)} %shard_map.105.refs_5_), channel_id=1, source_target_pairs={{0,2},{1,3},{2,4},{3,5},{4,6},{5,7},{6,0},{7,1},{8,14},{9,15},{10,... | collective-permute-start | bytes 1327112 | tf_op jit(solution)/shard_map/ppermute | solution.py:378
  42.6 4.8 %collective-permute-start.11 = (bf16[32,6528]{1,0:T(8,128)(2,1)S(1)}, bf16[32,6528]{1,0:T(8,128)(2,1)S(1)}, u32[]{:S(2)}, u32[]{:S(2)}) collective-permute-start(bf16[32,6528]{1,0:T(8,128)(2,1)S(1)} %collective-permute-done.5.refs_2_.refs_8_), channel_id=1, source_target_pairs={{0,8},{8,0},{16,24},{24,16},{32,40},{40,32},{48,56},{56,48},{64,72... | collective-permute-start | bytes 1253384 | tf_op jit(solution)/shard_map/ppermute | solution.py:380
  43.0 4.5 %collective-permute-start.9 = (bf16[96,1152]{1,0:T(8,128)(2,1)S(1)}, bf16[96,1152]{1,0:T(8,128)(2,1)S(1)}, u32[]{:S(2)}, u32[]{:S(2)}) collective-permute-start(bf16[96,1152]{1,0:T(8,128)(2,1)S(1)} %get-tuple-element.22.refs_4_), channel_id=1, source_target_pairs={{0,8},{8,0},{16,24},{24,16},{32,40},{40,32},{48,56},{56,48},{64,72... | collective-permute-start | bytes 663560 | tf_op jit(solution)/shard_map/ppermute | solution.py:375
  47.4 11.9 %copy-start.2 = (s32[5,384]{1,0:T(8,128)S(1)}, s32[5,384]{1,0:T(8,128)}, u32[]{:S(2)}) copy-start(s32[5,384]{1,0:T(8,128)} %constant.8.clone.refs_2_) | copy-start | bytes 23044
  55.4 3.9 %collective-permute-start.12 = (bf16[192,1152]{1,0:T(8,128)(2,1)S(1)}, bf16[192,1152]{1,0:T(8,128)(2,1)S(1)}, u32[]{:S(2)}, u32[]{:S(2)}) collective-permute-start(bf16[192,1152]{1,0:T(8,128)(2,1)S(1)} %collective-permute-done.8.refs_4_), channel_id=1, source_target_pairs={{0,8},{8,0},{16,24},{24,16},{32,40},{40,32},{48,56},{56,48},{64,72... | collective-permute-start | bytes 1327112 | tf_op jit(solution)/shard_map/ppermute | solution.py:413

commit v6 on v5

--- a/solution.py
+++ b/solution.py
@@ -16,7 +16,7 @@
 EPSILON = 1e-06
 MASKED = -1e30
 FLOOR = -1e29
-COARSE = (1, 4, 7)
+COARSE = (4, 1, 7)
 SCORE_SCALE = math.log2(math.e) / math.sqrt(ND + RD)
 
 
@@ -51,7 +51,18 @@
     out_ref[:, q_end:] = kv_ref[:, KL:]
 
 
-def pair_kernel(own_ref, other_ref, out_ref):
+def split_kernel(w_ref, key_ref, value_ref):
+    for head in range(key_ref.shape[0] // ND):
+        at = head * (ND + VD)
+        key_ref[head * ND : (head + 1) * ND, :] = w_ref[:, at : at + ND].T
+        value_ref[:, head * VD : (head + 1) * VD] = w_ref[:, at + ND : at + ND + VD]
+
+
+def fetch_kernel(from_ref, to_ref, arrived):
+    pltpu.async_copy(from_ref, to_ref, arrived).wait()
+
+
+def pair_kernel(own_ref, other_ref, ready_ref, out_ref):
     q_end = own_ref.shape[1] - RD
     q_size = q_end - KL
     at = 2 * (KL + RD)
@@ -62,7 +73,7 @@
     out_ref[:, 2 * KL : at] = rope
 
 
-def part_kernel(own_ref, got_ref, kv_ref, q_ref):
+def part_kernel(own_ref, got_ref, ready_ref, kv_ref, q_ref):
     size, width = own_ref.shape[0], kv_ref.shape[1]
     for n, ref in enumerate((own_ref, got_ref)):
         kv_ref[n * size : (n + 1) * size, :] = ref[:, :width]
@@ -118,13 +129,7 @@
     return start
 
 
-def query_kernel(q_at, lengths, own, got, w_hbm, out_ref, rows_ref, w_ref, arrived):
-    fetches = []
-    pairs, _, pair_width = w_ref.shape
-    for n in range(pairs):
-        columns = w_hbm.at[:, n * pair_width : (n + 1) * pair_width]
-        fetches.append(pltpu.make_async_copy(columns, w_ref.at[n], arrived.at[n]))
-        fetches[-1].start()
+def query_kernel(q_at, lengths, own, got, w_ref, out_ref, rows_ref):
     chip, core, y, xh = here()
     width = rows_ref.shape[1]
     for base, ref, lane_at in ((y, own, 0), (y + jnp.where(core == 0, 3, 1), got, q_at)):
@@ -152,9 +157,10 @@
         )
         return rope * cosine + turned * sine
 
-    for pair in range(pairs):
-        fetches[pair].wait()
-        made = jnp.dot(rows_ref[...], w_ref[pair], preferred_element_type=jnp.float32)
+    pair_width = 2 * (ND + RD)
+    for pair in range(w_ref.shape[1] // pair_width):
+        w = w_ref[:, pair * pair_width : (pair + 1) * pair_width]
+        made = jnp.dot(rows_ref[...], w, preferred_element_type=jnp.float32)
         out_ref[2 * pair, :, :ND] = made[:, :ND].astype(jnp.bfloat16)
         out_ref[2 * pair, :, ND:] = rotated(made[:, ND : ND + LANES]).astype(jnp.bfloat16)
         second = ND + RD
@@ -164,9 +170,9 @@
 
 
 def attend_kernel(views, group, first, last, *refs):
-    lengths, q_ref, table_ref, w_ref = refs[:4]
-    at = 4 + 1 + max(view[0] for view in views)
-    pieces = refs[4:at]
+    lengths, q_ref, table_ref, w_key_ref, w_value_ref = refs[:5]
+    at = 5 + 1 + max(view[0] for view in views)
+    pieces = refs[5:at]
     if not first:
         max_in, sum_in, acc_in = refs[at : at + 3]
         at += 3
@@ -176,7 +182,7 @@
     else:
         max_out, sum_out, acc_out = refs[at : at + 3]
         at += 3
-    rows_ref, rope_ref, bias_ref, made_ref, score_ref, weight_ref = refs[at:]
+    rows_ref, rope_ref, bias_ref, turned_ref, key_ref, value_ref, score_ref, weight_ref = refs[at:]
     heads = q_ref.shape[0]
     tok_dev, n_keys = bias_ref.shape
 
@@ -203,17 +209,20 @@
     allowed = (key_pos <= query_pos) & (key_pos >= query_start)
     bias_ref[...] = jnp.where(allowed, 0.0, MASKED)
 
-    def expand(head):
-        columns = slice(head * (ND + VD), (head + 1) * (ND + VD))
-        made = jnp.dot(rows_ref[...], w_ref[:, columns], preferred_element_type=jnp.float32)
-        made_ref[:, columns] = made.astype(jnp.bfloat16)
+    turned_ref[:KL, :] = rows_ref[...].T
+    turned_ref[KL:, :] = rope_ref[...].T
+
+    def expand(pair):
+        some = slice(pair * 2 * ND, (pair + 1) * 2 * ND)
+        keys = jnp.dot(w_key_ref[some, :], turned_ref[:KL, :], preferred_element_type=jnp.float32)
+        key_ref[some, :] = keys.astype(jnp.bfloat16)
+        values = jnp.dot(rows_ref[...], w_value_ref[:, some], preferred_element_type=jnp.float32)
+        value_ref[:, some] = values.astype(jnp.bfloat16)
 
     def score(head):
-        at = head * (ND + VD)
-        keys = jnp.concatenate([made_ref[:, at : at + ND], rope_ref[...]], axis=1)
-        scores = lax.dot_general(
-            q_ref[head], keys, (((1,), (1,)), ((), ())), preferred_element_type=jnp.float32
-        )
+        keys = [key_ref[head * ND : (head + 1) * ND, :], turned_ref[KL:, :]]
+        keys = jnp.concatenate(keys, axis=0)
+        scores = jnp.dot(q_ref[head], keys, preferred_element_type=jnp.float32)
         score_ref[head] = scores * SCORE_SCALE + bias_ref[...]
 
     def weigh(head):
@@ -230,8 +239,7 @@
         return new_max, total + faded * sum_in[head][:, :1], faded
 
     def mix(head, new_max, total, faded):
-        at = head * (ND + VD) + ND
-        values = made_ref[:, at : at + VD]
+        values = value_ref[:, head * VD : (head + 1) * VD]
         mixed = jnp.dot(weight_ref[head], values, preferred_element_type=jnp.float32)
         if not first:
             mixed = mixed + faded * acc_in[head]
@@ -247,7 +255,8 @@
     for step in range(len(groups) + 3):
         if step < len(groups):
             for head in groups[step]:
-                expand(head)
+                if head % 2 == 0:
+                    expand(head // 2)
         if 0 <= step - 1 < len(groups):
             for head in groups[step - 1]:
                 score(head)
@@ -270,13 +279,13 @@
     return np.array(columns, np.int32).T
 
 
-def attend(doc_lengths, queries, w_kv, pieces, views, group, state, last):
+def attend(doc_lengths, queries, w_key, w_value, pieces, views, group, state, last):
     heads, rows, width = queries.shape
     first = state is None
     table = jnp.asarray(key_table(views, 16, rows))
     count = table.shape[1]
     vmem = pl.BlockSpec(memory_space=pltpu.VMEM)
-    args = [queries, table, w_kv, *pieces]
+    args = [queries, table, w_key, w_value, *pieces]
     if not first:
         args += list(state)
     args = [slow(doc_lengths), *[fast(a) for a in args]]
@@ -299,7 +308,9 @@
             pltpu.VMEM((count, KL), jnp.bfloat16),
             pltpu.VMEM((count, LANES), jnp.bfloat16),
             pltpu.VMEM((rows, count), jnp.float32),
-            pltpu.VMEM((count, w_kv.shape[1]), jnp.bfloat16),
+            pltpu.VMEM((KL + LANES, count), jnp.bfloat16),
+            pltpu.VMEM((heads * ND, count), jnp.bfloat16),
+            pltpu.VMEM((count, heads * VD), jnp.bfloat16),
             pltpu.VMEM((heads, rows, count), jnp.float32),
             pltpu.VMEM((heads, rows, count), jnp.bfloat16),
         ],
@@ -338,24 +349,44 @@
         compiler_params=SMALL,
     )(*[slow(a) for a in (q_latent, q_gain, kv_cache, kv_gain)])
     other = lax.ppermute(rows, "head", across_x)
+    w_kv, rows = lax.optimization_barrier((w_kv, rows))
+    w_key, w_value = pl.pallas_call(
+        split_kernel,
+        in_specs=[vmem],
+        out_specs=[vmem] * 2,
+        out_shape=[
+            pltpu.VMEM((heads_here * ND, KL), jnp.bfloat16),
+            pltpu.VMEM((KL, heads_here * VD), jnp.bfloat16),
+        ],
+        compiler_params=SMALL,
+    )(fast(w_kv))
     both = pl.pallas_call(
         pair_kernel,
-        in_specs=[vmem] * 2,
+        in_specs=[vmem] * 3,
         out_specs=vmem,
         out_shape=pltpu.VMEM((size, 2 * rows.shape[1]), jnp.bfloat16),
         compiler_params=SMALL,
-    )(fast(rows), fast(other))
+    )(fast(rows), fast(other), fast(w_key))
     opposite = lax.ppermute(both, "head", across_y)
+    w_query, both = lax.optimization_barrier((w_query, both))
+    w_query = pl.pallas_call(
+        fetch_kernel,
+        in_specs=[pl.BlockSpec(memory_space=pl.ANY)],
+        out_specs=vmem,
+        out_shape=pltpu.VMEM(w_query.shape, w_query.dtype),
+        scratch_shapes=[pltpu.SemaphoreType.DMA],
+        compiler_params=SMALL,
+    )(slow(w_query))
     piece, q_set = pl.pallas_call(
         part_kernel,
-        in_specs=[vmem] * 2,
+        in_specs=[vmem] * 3,
         out_specs=[vmem] * 2,
         out_shape=[
             pltpu.VMEM((2 * size, 2 * kv_width), jnp.bfloat16),
             pltpu.VMEM((2 * size, 2 * q_width), jnp.bfloat16),
         ],
         compiler_params=SMALL,
-    )(fast(both), fast(opposite))
+    )(fast(both), fast(opposite), fast(w_query))
     coarse = [lax.ppermute(piece, "ctx", chip_shift(step)) for step in COARSE]
     set_shape = coarse[0].shape
     q_at = len(COARSE) * set_shape[1]
@@ -379,27 +410,17 @@
     near_swapped = lax.ppermute(near, "ctx", swap)
     got_swapped = lax.ppermute(got, "ctx", swap)
 
-    pairs = heads_here // 2
     queries = pl.pallas_call(
         lambda *refs: query_kernel(q_at, *refs),
-        in_specs=[
-            pl.BlockSpec(memory_space=pltpu.SMEM),
-            vmem,
-            vmem,
-            pl.BlockSpec(memory_space=pl.ANY),
-        ],
+        in_specs=[pl.BlockSpec(memory_space=pltpu.SMEM)] + [vmem] * 3,
         out_specs=vmem,
         out_shape=pltpu.VMEM((heads_here, tok_dev, 2 * LANES), jnp.bfloat16),
-        scratch_shapes=[
-            pltpu.VMEM((tok_dev, w_query.shape[0]), jnp.bfloat16),
-            pltpu.VMEM((pairs, w_query.shape[0], w_query.shape[1] // pairs), jnp.bfloat16),
-            pltpu.SemaphoreType.DMA((pairs,)),
-        ],
-        compiler_params=SMALL,
-    )(slow(doc_lengths), fast(q_set), fast(got), slow(w_query))
+        scratch_shapes=[pltpu.VMEM((tok_dev, w_query.shape[0]), jnp.bfloat16)],
+        compiler_params=SMALL,
+    )(slow(doc_lengths), fast(q_set), fast(got), fast(w_query))
 
     def attend_to(pieces, views, group, state, last=False):
-        return attend(doc_lengths, queries, w_kv, pieces, views, group, state, last)
+        return attend(doc_lengths, queries, w_key, w_value, pieces, views, group, state, last)
 
     near_slots = [*[k + 1 for k in COARSE], *[k - 1 for k in COARSE]]
     views = [(0, 0, 0, 0, COARSE), (1, 0, 0, 0, near_slots)]

time: 63.5 us -> 58.4 us (0.920)
  waiting for transfers between devices: 15.1 us -> 7.06 us
  starting transfers between devices: 27.4 us -> 29.1 us
  local copies, waits for them, and re-layouts: 0.02 us -> 1.61 us
    ppermute x1, starting transfers between devices: 0.26 us -> 3.57 us  [body(): sooner = lax.ppermute(coarse, 'ctx', chip_shift(-1))]
    ppermute x1, waiting for transfers between devices: 3.32 us -> 0.01 us  [body(): sooner = lax.ppermute(coarse, 'ctx', chip_shift(-1))]
    pallas_call x2 -> x4, Pallas kernels: 0.09 us -> 2.91 us  [the longest x1 2.34 us: body(): pl.pallas_call(fetch_kernel, in_specs=[pl.BlockSpec(memory_space=pl.ANY)]...]
    pallas_call x1, Pallas kernels: 4.26 us -> 1.94 us  [body(): pl.pallas_call(lambda *refs: query_kernel(q_at, *refs), in_specs=[pl.Bloc...]
    ppermute x1, waiting for transfers between devices: 2.4 us -> 0.1 us  [body(): opposite = lax.ppermute(both, 'head', across_y)]
    ppermute x1, waiting for transfers between devices: 1.7 us -> 0.01 us  [body(): other = lax.ppermute(rows, 'head', across_x)]
    ppermute x3, waiting for transfers between devices: 5.25 us -> 3.62 us  [body(): coarse = [lax.ppermute(piece, 'ctx', chip_shift(step)) for step in COARSE]]
    unnamed x8, local copies, waits for them, and re-layouts: 0.02 us -> 1.61 us
  transfers between devices with their start and end apart: 13 -> 13, of which waited for: 6 -> 3; matrix products, arithmetic and copies ran while one was open for 0% -> 0% of each run, Pallas kernels for 24% -> 26%
where the time goes in v6:
time: 58.4 us; the launch traced here: 58.2 us
  starting transfers between devices  29.1 us (50%)
  Pallas kernels  20.3 us (35%)
  waiting for transfers between devices  7.06 us (12%)
  local copies, waits for them, and re-layouts  1.61 us (3%)
    pallas_call x3, Pallas kernels, attend(): pl.pallas_call(kernel, in_specs=[pl.BlockSpec(memory_space=pltpu.SMEM)] +...  14.4 us
    ppermute x3, starting transfers between devices, body(): coarse = [lax.ppermute(piece, 'ctx', chip_shift(step)) for step in COARSE]  10.4 us
    ppermute x1, starting transfers between devices, body(): other = lax.ppermute(rows, 'head', across_x)  3.66 us
    ppermute x3, waiting for transfers between devices, body(): coarse = [lax.ppermute(piece, 'ctx', chip_shift(step)) for step in COARSE]  3.62 us
    ppermute x1, starting transfers between devices, body(): sooner = lax.ppermute(coarse, 'ctx', chip_shift(-1))  3.57 us
    ppermute x1, starting transfers between devices, body(): near_swapped = lax.ppermute(near, 'ctx', swap)  3.37 us
    ppermute x1, waiting for transfers between devices, body(): later = lax.ppermute(coarse, 'ctx', chip_shift(1))  3.32 us
    ppermute x1, starting transfers between devices, body(): opposite = lax.ppermute(both, 'head', across_y)  2.95 us
  transfers between devices with their start and end apart: 13, of which 3 were waited for; matrix products, arithmetic and copies ran while one was open for 0% of the time, Pallas kernels for 26%

profile of v6, /device:TPU:1, one launch (start us, length us, event | category | flops | bytes accessed | tf_op | source)
XLA Modules:
  0.0 58.2 jit_solution(2120659422478246655)
XLA Ops:
  0.0 0.9 %shard_map.100.own_ref = bf16[16,2112]{1,0:T(8,128)(2,1)S(1)} custom-call(bf16[16,1536]{1,0:T(8,128)(2,1)} %q_ref.1, f32[1536]{0:T(1024)} %q_gain_ref.1, bf16[16,576]{1,0:T(8,128)(2,1)} %kv_ref.1, f32[512]{0:T(512)} %kv_gain_ref.1), custom_call_target="tpu_custom_call" | custom-call | tf_op jit(solution)/shard_map/pallas_call | solution.py:346
  0.9 3.7 %collective-permute-start = (bf16[16,2112]{1,0:T(8,128)(2,1)S(1)}, bf16[16,2112]{1,0:T(8,128)(2,1)S(1)}, u32[]{:S(2)}, u32[]{:S(2)}) collective-permute-start(bf16[16,2112]{1,0:T(8,128)(2,1)S(1)} %shard_map.100.own_ref), channel_id=1, source_target_pairs={{0,1},{1,0},{2,3},{3,2},{4,5},{5,4},{6,7},{7,6},{8,9},{9,8},{10,11... | collective-permute-start | bytes 202760 | tf_op jit(solution)/shard_map/ppermute | solution.py:351
  4.6 0.0 copy-start
  4.6 1.6 %copy-done = bf16[512,2048]{1,0:T(8,128)(2,1)S(1)} copy-done((bf16[512,2048]{1,0:T(8,128)(2,1)S(1)}, bf16[512,2048]{1,0:T(8,128)(2,1)}, u32[]{:S(2)}) %copy-start) | copy-done | bytes 2097176
  6.2 0.5 shard_map.101
  6.7 0.0 collective-permute-done.other_ref
  6.7 0.1 shard_map.102.own_ref
  6.7 2.9 %collective-permute-start.1 = (bf16[16,4224]{1,0:T(8,128)(2,1)S(1)}, bf16[16,4224]{1,0:T(8,128)(2,1)S(1)}, u32[]{:S(2)}, u32[]{:S(2)}) collective-permute-start(bf16[16,4224]{1,0:T(8,128)(2,1)S(1)} %shard_map.102.own_ref), channel_id=1, source_target_pairs={{0,4},{1,5},{2,6},{3,7},{4,0},{5,1},{6,2},{7,3},{8,12},{9,13},{10,... | collective-permute-start | bytes 405512 | tf_op jit(solution)/shard_map/ppermute | solution.py:370
  9.7 2.3 %shard_map.103.ready_ref.refs_3_ = bf16[1536,1536]{1,0:T(8,128)(2,1)S(1)} custom-call(bf16[1536,1536]{1,0:T(8,128)(2,1)} %from_ref), custom_call_target="tpu_custom_call" | custom-call | tf_op jit(solution)/shard_map/pallas_call | solution.py:372
  12.0 0.1 collective-permute-done.1.got_ref
  12.2 0.0 copy-start.1
  12.2 7.0 %collective-permute-start.2 = (bf16[32,1152]{1,0:T(8,128)(2,1)S(1)}, bf16[32,1152]{1,0:T(8,128)(2,1)S(1)}, u32[]{:S(2)}, u32[]{:S(2)}) collective-permute-start(bf16[32,1152]{1,0:T(8,128)(2,1)S(1)} %get-tuple-element.31), channel_id=1, source_target_pairs={{0,64},{8,72},{16,80},{24,88},{32,96},{40,104},{48,112},{56,120},{... | collective-permute-start | bytes 221192 | tf_op jit(solution)/shard_map/ppermute | solution.py:390
  19.2 0.7 %collective-permute-start.3 = (bf16[32,1152]{1,0:T(8,128)(2,1)S(1)}, bf16[32,1152]{1,0:T(8,128)(2,1)S(1)}, u32[]{:S(2)}, u32[]{:S(2)}) collective-permute-start(bf16[32,1152]{1,0:T(8,128)(2,1)S(1)} %get-tuple-element.31), channel_id=1, source_target_pairs={{0,16},{8,24},{16,32},{24,40},{32,48},{40,56},{48,64},{56,72},{64,... | collective-permute-start | bytes 221192 | tf_op jit(solution)/shard_map/ppermute | solution.py:390
  19.9 2.7 %collective-permute-start.4 = (bf16[32,1152]{1,0:T(8,128)(2,1)S(1)}, bf16[32,1152]{1,0:T(8,128)(2,1)S(1)}, u32[]{:S(2)}, u32[]{:S(2)}) collective-permute-start(bf16[32,1152]{1,0:T(8,128)(2,1)S(1)} %get-tuple-element.31), channel_id=1, source_target_pairs={{0,112},{8,120},{16,128},{24,136},{32,144},{40,152},{48,160},{56,1... | collective-permute-start | bytes 221192 | tf_op jit(solution)/shard_map/ppermute | solution.py:390
  22.6 0.0 collective-permute-done.2.refs_0_
  22.6 3.6 %collective-permute-done.3.refs_1_ = bf16[32,1152]{1,0:T(8,128)(2,1)S(1)} collective-permute-done((bf16[32,1152]{1,0:T(8,128)(2,1)S(1)}, bf16[32,1152]{1,0:T(8,128)(2,1)S(1)}, u32[]{:S(2)}, u32[]{:S(2)}) %collective-permute-start.3) | collective-permute-done | bytes 73760 | tf_op jit(solution)/shard_map/ppermute | solution.py:390
  26.2 0.0 collective-permute-done.4.refs_2_
  26.3 2.6 %collective-permute-start.5 = (bf16[32,6528]{1,0:T(8,128)(2,1)S(1)}, bf16[32,6528]{1,0:T(8,128)(2,1)S(1)}, u32[]{:S(2)}, u32[]{:S(2)}) collective-permute-start(bf16[32,6528]{1,0:T(8,128)(2,1)S(1)} %get-tuple-element.32), channel_id=1, source_target_pairs={{0,2},{1,3},{2,4},{3,5},{4,6},{5,7},{6,0},{7,1},{8,14},{9,15},{10,... | collective-permute-start | bytes 1253384 | tf_op jit(solution)/shard_map/ppermute | solution.py:405
  28.9 0.0 collective-permute-start.6
  28.9 3.6 %collective-permute-start.7 = (bf16[96,1152]{1,0:T(8,128)(2,1)S(1)}, bf16[96,1152]{1,0:T(8,128)(2,1)S(1)}, u32[]{:S(2)}, u32[]{:S(2)}) collective-permute-start(bf16[96,1152]{1,0:T(8,128)(2,1)S(1)} %get-tuple-element.34.refs_5_), channel_id=1, source_target_pairs={{0,240},{8,248},{16,0},{24,8},{32,16},{40,24},{48,32},{56,40},{64,... | collective-permute-start | bytes 663560 | tf_op jit(solution)/shard_map/ppermute | solution.py:404
  32.5 3.3 %collective-permute-done.6.refs_0_ = bf16[96,1152]{1,0:T(8,128)(2,1)S(1)} collective-permute-done((bf16[96,1152]{1,0:T(8,128)(2,1)S(1)}, bf16[96,1152]{1,0:T(8,128)(2,1)S(1)}, u32[]{:S(2)}, u32[]{:S(2)}) %collective-permute-start.6) | collective-permute-done | bytes 221216 | tf_op jit(solution)/shard_map/ppermute | solution.py:403
  35.8 0.0 collective-permute-done.7.refs_1_
  35.8 0.0 copy-start.3
  35.8 3.4 %collective-permute-start.10 = (bf16[192,1152]{1,0:T(8,128)(2,1)S(1)}, bf16[192,1152]{1,0:T(8,128)(2,1)S(1)}, u32[]{:S(2)}, u32[]{:S(2)}) collective-permute-start(bf16[192,1152]{1,0:T(8,128)(2,1)S(1)} %shard_map.107.refs_6_), channel_id=1, source_target_pairs={{0,8},{8,0},{16,24},{24,16},{32,40},{40,32},{48,56},{56,48},{64,72... | collective-permute-start | bytes 1327112 | tf_op jit(solution)/shard_map/ppermute | solution.py:410
  39.2 1.4 %collective-permute-start.8 = (bf16[192,1152]{1,0:T(8,128)(2,1)S(1)}, bf16[192,1152]{1,0:T(8,128)(2,1)S(1)}, u32[]{:S(2)}, u32[]{:S(2)}) collective-permute-start(bf16[192,1152]{1,0:T(8,128)(2,1)S(1)} %shard_map.107.refs_6_), channel_id=1, source_target_pairs={{0,2},{1,3},{2,4},{3,5},{4,6},{5,7},{6,0},{7,1},{8,14},{9,15},{10,... | collective-permute-start | bytes 1327112 | tf_op jit(solution)/shard_map/ppermute | solution.py:409
  40.6 0.0 collective-permute-done.5.refs_2_.refs_9_
  40.6 0.3 collective-permute-start.11
  40.9 0.2 collective-permute-start.9
  41.1 1.9 %shard_map.106.refs_1_ = bf16[8,128,256]{2,1,0:T(8,128)(2,1)S(1)} custom-call(s32[3]{0:T(128)} %refs_0_.7, bf16[32,3072]{1,0:T(8,128)(2,1)S(1)} %get-tuple-element.30.refs_3_.refs_1_, bf16[32,6528]{1,0:T(8,128)(2,1)S(1)} %collective-permute-done.5.refs_2_.refs_9_, bf16[1536,1536]{1,0:T(8,128)(2,1)S(1)} %shard_map.103.ready_ref.refs_3_), custom_call_target="tpu_custom_call" | custom-call | tf_op jit(solution)/shard_map/pallas_call | solution.py:413
  43.1 0.0 collective-permute-done.9.refs_7_
  43.1 0.0 collective-permute-done.10.refs_8_
  43.1 0.0 collective-permute-done.11.refs_10_
  43.1 0.0 copy-done.1
  43.1 0.0 copy-start.2
  43.1 7.0 %shard_map.108 = (f32[8,128,128]{2,1,0:T(8,128)S(1)}, f32[8,128,128]{2,1,0:T(8,128)S(1)}, f32[8,128,128]{2,1,0:T(8,128)S(1)}) custom-call(s32[3]{0:T(128)} %refs_0_.7, bf16[8,128,256]{2,1,0:T(8,128)(2,1)S(1)} %shard_map.106.refs_1_, s32[5,1536]{1,0:T(8,128)S(1)} %copy-done.1, bf16[1024,512]{1,0:T(8,128)(2,1)S(1)} %get-tuple-element.27.ready_ref.refs_3_, ...), custom_call_target="tpu_custom_call" | custom-call | tf_op jit(solution)/shard_map/pallas_call | solution.py:302
  50.1 0.0 collective-permute-done.8.refs_5_
  50.1 0.6 %collective-permute-start.12 = (bf16[192,1152]{1,0:T(8,128)(2,1)S(1)}, bf16[192,1152]{1,0:T(8,128)(2,1)S(1)}, u32[]{:S(2)}, u32[]{:S(2)}) collective-permute-start(bf16[192,1152]{1,0:T(8,128)(2,1)S(1)} %collective-permute-done.8.refs_5_), channel_id=1, source_target_pairs={{0,8},{8,0},{16,24},{24,16},{32,40},{40,32},{48,56},{56,48},{64,72... | collective-permute-start | bytes 1327112 | tf_op jit(solution)/shard_map/ppermute | solution.py:434
  50.7 0.0 copy-done.3
  50.7 3.4 %shard_map.109 = (f32[8,128,128]{2,1,0:T(8,128)S(1)}, f32[8,128,128]{2,1,0:T(8,128)S(1)}, f32[8,128,128]{2,1,0:T(8,128)S(1)}) custom-call(s32[3]{0:T(128)} %refs_0_.7, bf16[8,128,256]{2,1,0:T(8,128)(2,1)S(1)} %shard_map.106.refs_1_, s32[5,384]{1,0:T(8,128)S(1)} %copy-done.3, bf16[1024,512]{1,0:T(8,128)(2,1)S(1)} %get-tuple-element.27.ready_ref.refs_3_, ...), custom_call_target="tpu_custom_call" | custom-call | tf_op jit(solution)/shard_map/pallas_call | solution.py:302
  54.1 0.0 collective-permute-done.12.refs_5_
  54.1 0.0 copy-done.2
  54.1 4.1 %shard_map.110 = bf16[128,1024]{1,0:T(8,128)(2,1)} custom-call(s32[3]{0:T(128)} %refs_0_.7, bf16[8,128,256]{2,1,0:T(8,128)(2,1)S(1)} %shard_map.106.refs_1_, s32[5,384]{1,0:T(8,128)S(1)} %copy-done.2, bf16[1024,512]{1,0:T(8,128)(2,1)S(1)} %get-tuple-element.27.ready_ref.refs_3_, bf16[512,1024]{1,0:T(8,128)(2,1)S(1)} %get-tuple-element.33.refs_4_, ...), custom_call_target="tpu_custom_call" | custom-call | tf_op jit(solution)/shard_map/pallas_call | solution.py:302
  (3 shorter events, 0.1 us)
Async XLA Ops:
  0.9 5.7 %collective-permute-start = (bf16[16,2112]{1,0:T(8,128)(2,1)S(1)}, bf16[16,2112]{1,0:T(8,128)(2,1)S(1)}, u32[]{:S(2)}, u32[]{:S(2)}) collective-permute-start(bf16[16,2112]{1,0:T(8,128)(2,1)S(1)} %shard_map.100.own_ref), channel_id=1, source_target_pairs={{0,1},{1,0},{2,3},{3,2},{4,5},{5,4},{6,7},{7,6},{8,9},{9,8},{10,11... | collective-permute-start | bytes 202760 | tf_op jit(solution)/shard_map/ppermute | solution.py:351
  4.6 1.6 %copy-start = (bf16[512,2048]{1,0:T(8,128)(2,1)S(1)}, bf16[512,2048]{1,0:T(8,128)(2,1)}, u32[]{:S(2)}) copy-start(bf16[512,2048]{1,0:T(8,128)(2,1)} %w_ref) | copy-start | bytes 6291460
  6.7 5.4 %collective-permute-start.1 = (bf16[16,4224]{1,0:T(8,128)(2,1)S(1)}, bf16[16,4224]{1,0:T(8,128)(2,1)S(1)}, u32[]{:S(2)}, u32[]{:S(2)}) collective-permute-start(bf16[16,4224]{1,0:T(8,128)(2,1)S(1)} %shard_map.102.own_ref), channel_id=1, source_target_pairs={{0,4},{1,5},{2,6},{3,7},{4,0},{5,1},{6,2},{7,3},{8,12},{9,13},{10,... | collective-permute-start | bytes 405512 | tf_op jit(solution)/shard_map/ppermute | solution.py:370
  12.2 30.9 %copy-start.1 = (s32[5,1536]{1,0:T(8,128)S(1)}, s32[5,1536]{1,0:T(8,128)}, u32[]{:S(2)}) copy-start(s32[5,1536]{1,0:T(8,128)} %constant.6.clone.refs_2_) | copy-start | bytes 92164
  12.2 10.4 %collective-permute-start.2 = (bf16[32,1152]{1,0:T(8,128)(2,1)S(1)}, bf16[32,1152]{1,0:T(8,128)(2,1)S(1)}, u32[]{:S(2)}, u32[]{:S(2)}) collective-permute-start(bf16[32,1152]{1,0:T(8,128)(2,1)S(1)} %get-tuple-element.31), channel_id=1, source_target_pairs={{0,64},{8,72},{16,80},{24,88},{32,96},{40,104},{48,112},{56,120},{... | collective-permute-start | bytes 221192 | tf_op jit(solution)/shard_map/ppermute | solution.py:390
  19.2 7.1 %collective-permute-start.3 = (bf16[32,1152]{1,0:T(8,128)(2,1)S(1)}, bf16[32,1152]{1,0:T(8,128)(2,1)S(1)}, u32[]{:S(2)}, u32[]{:S(2)}) collective-permute-start(bf16[32,1152]{1,0:T(8,128)(2,1)S(1)} %get-tuple-element.31), channel_id=1, source_target_pairs={{0,16},{8,24},{16,32},{24,40},{32,48},{40,56},{48,64},{56,72},{64,... | collective-permute-start | bytes 221192 | tf_op jit(solution)/shard_map/ppermute | solution.py:390
  19.9 6.3 %collective-permute-start.4 = (bf16[32,1152]{1,0:T(8,128)(2,1)S(1)}, bf16[32,1152]{1,0:T(8,128)(2,1)S(1)}, u32[]{:S(2)}, u32[]{:S(2)}) collective-permute-start(bf16[32,1152]{1,0:T(8,128)(2,1)S(1)} %get-tuple-element.31), channel_id=1, source_target_pairs={{0,112},{8,120},{16,128},{24,136},{32,144},{40,152},{48,160},{56,1... | collective-permute-start | bytes 221192 | tf_op jit(solution)/shard_map/ppermute | solution.py:390
  26.3 14.3 %collective-permute-start.5 = (bf16[32,6528]{1,0:T(8,128)(2,1)S(1)}, bf16[32,6528]{1,0:T(8,128)(2,1)S(1)}, u32[]{:S(2)}, u32[]{:S(2)}) collective-permute-start(bf16[32,6528]{1,0:T(8,128)(2,1)S(1)} %get-tuple-element.32), channel_id=1, source_target_pairs={{0,2},{1,3},{2,4},{3,5},{4,6},{5,7},{6,0},{7,1},{8,14},{9,15},{10,... | collective-permute-start | bytes 1253384 | tf_op jit(solution)/shard_map/ppermute | solution.py:405
  28.9 6.9 %collective-permute-start.6 = (bf16[96,1152]{1,0:T(8,128)(2,1)S(1)}, bf16[96,1152]{1,0:T(8,128)(2,1)S(1)}, u32[]{:S(2)}, u32[]{:S(2)}) collective-permute-start(bf16[96,1152]{1,0:T(8,128)(2,1)S(1)} %get-tuple-element.34.refs_5_), channel_id=1, source_target_pairs={{0,16},{8,24},{16,32},{24,40},{32,48},{40,56},{48,64},{56,72},{64,... | collective-permute-start | bytes 663560 | tf_op jit(solution)/shard_map/ppermute | solution.py:403
  28.9 6.9 %collective-permute-start.7 = (bf16[96,1152]{1,0:T(8,128)(2,1)S(1)}, bf16[96,1152]{1,0:T(8,128)(2,1)S(1)}, u32[]{:S(2)}, u32[]{:S(2)}) collective-permute-start(bf16[96,1152]{1,0:T(8,128)(2,1)S(1)} %get-tuple-element.34.refs_5_), channel_id=1, source_target_pairs={{0,240},{8,248},{16,0},{24,8},{32,16},{40,24},{48,32},{56,40},{64,... | collective-permute-start | bytes 663560 | tf_op jit(solution)/shard_map/ppermute | solution.py:404
  35.8 14.9 %copy-start.3 = (s32[5,384]{1,0:T(8,128)S(1)}, s32[5,384]{1,0:T(8,128)}, u32[]{:S(2)}) copy-start(s32[5,384]{1,0:T(8,128)} %constant.7.clone.refs_2_) | copy-start | bytes 23044
  35.8 7.2 %collective-permute-start.10 = (bf16[192,1152]{1,0:T(8,128)(2,1)S(1)}, bf16[192,1152]{1,0:T(8,128)(2,1)S(1)}, u32[]{:S(2)}, u32[]{:S(2)}) collective-permute-start(bf16[192,1152]{1,0:T(8,128)(2,1)S(1)} %shard_map.107.refs_6_), channel_id=1, source_target_pairs={{0,8},{8,0},{16,24},{24,16},{32,40},{40,32},{48,56},{56,48},{64,72... | collective-permute-start | bytes 1327112 | tf_op jit(solution)/shard_map/ppermute | solution.py:410
  39.2 10.9 %collective-permute-start.8 = (bf16[192,1152]{1,0:T(8,128)(2,1)S(1)}, bf16[192,1152]{1,0:T(8,128)(2,1)S(1)}, u32[]{:S(2)}, u32[]{:S(2)}) collective-permute-start(bf16[192,1152]{1,0:T(8,128)(2,1)S(1)} %shard_map.107.refs_6_), channel_id=1, source_target_pairs={{0,2},{1,3},{2,4},{3,5},{4,6},{5,7},{6,0},{7,1},{8,14},{9,15},{10,... | collective-permute-start | bytes 1327112 | tf_op jit(solution)/shard_map/ppermute | solution.py:409
  40.6 2.5 %collective-permute-start.11 = (bf16[32,6528]{1,0:T(8,128)(2,1)S(1)}, bf16[32,6528]{1,0:T(8,128)(2,1)S(1)}, u32[]{:S(2)}, u32[]{:S(2)}) collective-permute-start(bf16[32,6528]{1,0:T(8,128)(2,1)S(1)} %collective-permute-done.5.refs_2_.refs_9_), channel_id=1, source_target_pairs={{0,8},{8,0},{16,24},{24,16},{32,40},{40,32},{48,56},{56,48},{64,72... | collective-permute-start | bytes 1253384 | tf_op jit(solution)/shard_map/ppermute | solution.py:411
  40.9 2.2 %collective-permute-start.9 = (bf16[96,1152]{1,0:T(8,128)(2,1)S(1)}, bf16[96,1152]{1,0:T(8,128)(2,1)S(1)}, u32[]{:S(2)}, u32[]{:S(2)}) collective-permute-start(bf16[96,1152]{1,0:T(8,128)(2,1)S(1)} %get-tuple-element.34.refs_5_), channel_id=1, source_target_pairs={{0,8},{8,0},{16,24},{24,16},{32,40},{40,32},{48,56},{56,48},{64,72... | collective-permute-start | bytes 663560 | tf_op jit(solution)/shard_map/ppermute | solution.py:406
  43.1 11.0 %copy-start.2 = (s32[5,384]{1,0:T(8,128)S(1)}, s32[5,384]{1,0:T(8,128)}, u32[]{:S(2)}) copy-start(s32[5,384]{1,0:T(8,128)} %constant.8.clone.refs_2_) | copy-start | bytes 23044
  50.1 4.0 %collective-permute-start.12 = (bf16[192,1152]{1,0:T(8,128)(2,1)S(1)}, bf16[192,1152]{1,0:T(8,128)(2,1)S(1)}, u32[]{:S(2)}, u32[]{:S(2)}) collective-permute-start(bf16[192,1152]{1,0:T(8,128)(2,1)S(1)} %collective-permute-done.8.refs_5_), channel_id=1, source_target_pairs={{0,8},{8,0},{16,24},{24,16},{32,40},{40,32},{48,56},{56,48},{64,72... | collective-permute-start | bytes 1327112 | tf_op jit(solution)/shard_map/ppermute | solution.py:434

commit v7 on v6

--- a/solution.py
+++ b/solution.py
@@ -62,31 +62,24 @@
     pltpu.async_copy(from_ref, to_ref, arrived).wait()
 
 
-def pair_kernel(own_ref, other_ref, ready_ref, out_ref):
+def pair_kernel(own_ref, other_ref, ready_ref, kv_ref, q_ref):
     q_end = own_ref.shape[1] - RD
     q_size = q_end - KL
-    at = 2 * (KL + RD)
     for n, ref in enumerate((own_ref, other_ref)):
-        out_ref[:, n * KL : (n + 1) * KL] = ref[:, :KL]
-        out_ref[:, at + n * q_size : at + (n + 1) * q_size] = ref[:, KL:q_end]
-    rope = jnp.concatenate([own_ref[:, q_end:], other_ref[:, q_end:]], axis=1)
-    out_ref[:, 2 * KL : at] = rope
-
-
-def part_kernel(own_ref, got_ref, ready_ref, kv_ref, q_ref):
-    size, width = own_ref.shape[0], kv_ref.shape[1]
-    for n, ref in enumerate((own_ref, got_ref)):
-        kv_ref[n * size : (n + 1) * size, :] = ref[:, :width]
-        q_ref[n * size : (n + 1) * size, :] = ref[:, width:]
-
-
-def bundle_kernel(n_parts, *refs):
-    *parts, q_ref, coarse_ref, bundle_ref = refs
-    size, width = parts[0].shape
-    for n, ref in enumerate(parts):
-        coarse_ref[n * size : (n + 1) * size, :] = ref[...]
-        bundle_ref[:, n * width : (n + 1) * width] = ref[...]
-    bundle_ref[:, n_parts * width :] = q_ref[...]
+        kv_ref[:, n * KL : (n + 1) * KL] = ref[:, :KL]
+        q_ref[:, n * q_size : (n + 1) * q_size] = ref[:, KL:q_end]
+    kv_ref[:, 2 * KL :] = jnp.concatenate([own_ref[:, q_end:], other_ref[:, q_end:]], axis=1)
+
+
+def bundle_kernel(coarse_ref, q_own_ref, q_got_ref, q_ref, bundle_ref):
+    size, width = q_ref.shape[0], coarse_ref.shape[1]
+    n_parts = coarse_ref.shape[0] // size
+    for n in range(n_parts):
+        bundle_ref[:, n * width : (n + 1) * width] = coarse_ref[n * size : (n + 1) * size, :]
+    for n, ref in enumerate((q_own_ref, q_got_ref)):
+        rows = slice(n * ref.shape[0], (n + 1) * ref.shape[0])
+        q_ref[rows, :] = ref[...]
+        bundle_ref[rows, n_parts * width :] = ref[...]
 
 
 def join_kernel(sizes, n_after, *refs):
@@ -182,7 +175,9 @@
     else:
         max_out, sum_out, acc_out = refs[at : at + 3]
         at += 3
-    rows_ref, rope_ref, bias_ref, turned_ref, key_ref, value_ref, score_ref, weight_ref = refs[at:]
+    rows_ref, rope_ref, bias_ref, turned_ref, key_ref, value_ref, score_ref, weight_ref = refs[at : at + 8]
+    if last:
+        made_ref, gone = refs[at + 8 :]
     heads = q_ref.shape[0]
     tok_dev, n_keys = bias_ref.shape
 
@@ -244,12 +239,19 @@
         if not first:
             mixed = mixed + faded * acc_in[head]
         if last:
-            out_ref[:, head * VD : (head + 1) * VD] = (mixed * (1.0 / total)).astype(jnp.bfloat16)
+            made_ref[:, head * VD : (head + 1) * VD] = (mixed * (1.0 / total)).astype(jnp.bfloat16)
+            if head % 2 == 1:
+                copies[head // 2].start()
         else:
             max_out[head] = jnp.broadcast_to(new_max, mixed.shape)
             sum_out[head] = jnp.broadcast_to(total, mixed.shape)
             acc_out[head] = mixed
 
+    copies = []
+    for pair in range(heads // 2 if last else 0):
+        some = slice(pair * 2 * VD, (pair + 1) * 2 * VD)
+        copy = pltpu.make_async_copy(made_ref.at[:, some], out_ref.at[:, some], gone.at[pair])
+        copies.append(copy)
     groups = [range(low, low + group) for low in range(0, heads, group)]
     found = {}
     for step in range(len(groups) + 3):
@@ -266,6 +268,8 @@
         if 0 <= step - 3:
             for head in groups[step - 3]:
                 mix(head, *found[head])
+    for copy in copies:
+        copy.wait()
 
 
 def key_table(views, rows, tok_dev):
@@ -291,8 +295,13 @@
     args = [slow(doc_lengths), *[fast(a) for a in args]]
     if last:
         out_shape = jax.ShapeDtypeStruct((rows, heads * VD), jnp.bfloat16)
-        out_specs = vmem
+        out_specs = pl.BlockSpec(memory_space=pl.ANY)
+        leaving = [
+            pltpu.VMEM((rows, heads * VD), jnp.bfloat16),
+            pltpu.SemaphoreType.DMA((heads // 2,)),
+        ]
     else:
+        leaving = []
         out_shape = [pltpu.VMEM((heads, rows, VD), jnp.float32)] * 3
         out_specs = [vmem] * 3
 
@@ -313,6 +322,7 @@
             pltpu.VMEM((count, heads * VD), jnp.bfloat16),
             pltpu.VMEM((heads, rows, count), jnp.float32),
             pltpu.VMEM((heads, rows, count), jnp.bfloat16),
+            *leaving,
         ],
         compiler_params=LARGE,
     )(*args)
@@ -360,15 +370,18 @@
         ],
         compiler_params=SMALL,
     )(fast(w_kv))
-    both = pl.pallas_call(
+    piece, q_pair = pl.pallas_call(
         pair_kernel,
         in_specs=[vmem] * 3,
-        out_specs=vmem,
-        out_shape=pltpu.VMEM((size, 2 * rows.shape[1]), jnp.bfloat16),
+        out_specs=[vmem] * 2,
+        out_shape=[
+            pltpu.VMEM((size, 2 * kv_width), jnp.bfloat16),
+            pltpu.VMEM((size, 2 * q_width), jnp.bfloat16),
+        ],
         compiler_params=SMALL,
     )(fast(rows), fast(other), fast(w_key))
-    opposite = lax.ppermute(both, "head", across_y)
-    w_query, both = lax.optimization_barrier((w_query, both))
+    opposite = lax.ppermute(piece, "head", across_y)
+    w_query, piece = lax.optimization_barrier((w_query, piece))
     w_query = pl.pallas_call(
         fetch_kernel,
         in_specs=[pl.BlockSpec(memory_space=pl.ANY)],
@@ -377,38 +390,27 @@
         scratch_shapes=[pltpu.SemaphoreType.DMA],
         compiler_params=SMALL,
     )(slow(w_query))
-    piece, q_set = pl.pallas_call(
-        part_kernel,
+    (piece,) = join([[piece, opposite]], after=[w_query])
+    q_opposite = lax.ppermute(q_pair, "head", across_y)
+    coarse = [lax.ppermute(piece, "ctx", chip_shift(step)) for step in COARSE]
+
+    set_shape = coarse[0].shape
+    q_at = len(COARSE) * set_shape[1]
+    (coarse,) = join([coarse])
+    q_set, bundle = pl.pallas_call(
+        bundle_kernel,
         in_specs=[vmem] * 3,
         out_specs=[vmem] * 2,
         out_shape=[
-            pltpu.VMEM((2 * size, 2 * kv_width), jnp.bfloat16),
-            pltpu.VMEM((2 * size, 2 * q_width), jnp.bfloat16),
+            pltpu.VMEM((set_shape[0], q_pair.shape[1]), jnp.bfloat16),
+            pltpu.VMEM((set_shape[0], q_at + q_pair.shape[1]), jnp.bfloat16),
         ],
         compiler_params=SMALL,
-    )(fast(both), fast(opposite), fast(w_query))
-    coarse = [lax.ppermute(piece, "ctx", chip_shift(step)) for step in COARSE]
-    set_shape = coarse[0].shape
-    q_at = len(COARSE) * set_shape[1]
-    coarse, bundle = pl.pallas_call(
-        lambda *refs: bundle_kernel(len(COARSE), *refs),
-        in_specs=[vmem] * (len(COARSE) + 1),
-        out_specs=[vmem] * 2,
-        out_shape=[
-            pltpu.VMEM((len(COARSE) * set_shape[0], set_shape[1]), jnp.bfloat16),
-            pltpu.VMEM((set_shape[0], q_at + q_set.shape[1]), jnp.bfloat16),
-        ],
-        compiler_params=SMALL,
-    )(*[fast(a) for a in (*coarse, q_set)])
+    )(*[fast(a) for a in (coarse, q_pair, q_opposite)])
     later = lax.ppermute(coarse, "ctx", chip_shift(1))
     sooner = lax.ppermute(coarse, "ctx", chip_shift(-1))
     got = lax.ppermute(bundle, ("ctx", "head"), apart)
     coarse_swapped = lax.ppermute(coarse, "ctx", swap)
-
-    (near,) = join([[later, sooner]])
-    received = lax.ppermute(near, ("ctx", "head"), apart)
-    near_swapped = lax.ppermute(near, "ctx", swap)
-    got_swapped = lax.ppermute(got, "ctx", swap)
 
     queries = pl.pallas_call(
         lambda *refs: query_kernel(q_at, *refs),
@@ -418,6 +420,11 @@
         scratch_shapes=[pltpu.VMEM((tok_dev, w_query.shape[0]), jnp.bfloat16)],
         compiler_params=SMALL,
     )(slow(doc_lengths), fast(q_set), fast(got), fast(w_query))
+
+    (near,) = join([[later, sooner]], after=[queries])
+    received = lax.ppermute(near, ("ctx", "head"), apart)
+    near_swapped = lax.ppermute(near, "ctx", swap)
+    got_swapped = lax.ppermute(got, "ctx", swap)
 
     def attend_to(pieces, views, group, state, last=False):
         return attend(doc_lengths, queries, w_key, w_value, pieces, views, group, state, last)

time: 58.4 us -> 59.1 us (1.012)
  starting transfers between devices: 29.1 us -> 30.4 us
  waiting for transfers between devices: 7.06 us -> 6.07 us
    ppermute x1, waiting for transfers between devices: 3.32 us -> 0.01 us  [body(): later = lax.ppermute(coarse, 'ctx', chip_shift(1))]
    ppermute x1, waiting for transfers between devices: 0.01 us -> 1.56 us  [body(): coarse_swapped = lax.ppermute(coarse, 'ctx', swap)]
    ppermute x1, waiting for transfers between devices: 0.01 us -> 1.41 us  [body(): got = lax.ppermute(bundle, ('ctx', 'head'), apart)]
    ppermute x1, starting transfers between devices: 3.37 us -> 4.75 us  [body(): near_swapped = lax.ppermute(near, 'ctx', swap)]
    ppermute x1 -> x2, starting transfers between devices: 2.95 us -> 3.05 us  [the longest x1 2.95 us: body(): opposite = lax.ppermute(piece, 'head', across_y)]
  transfers between devices with their start and end apart: 13 -> 14, of which waited for: 3 -> 3; matrix products, arithmetic and copies ran while one was open for 0% -> 0% of each run, Pallas kernels for 26% -> 26%
where the time goes in v7:
time: 59.1 us; the launch traced here: 58.8 us
  starting transfers between devices  30.4 us (51%)
  Pallas kernels  20.4 us (35%)
  waiting for transfers between devices  6.07 us (10%)
  local copies, waits for them, and re-layouts  1.61 us (3%)
    pallas_call x3, Pallas kernels, attend(): pl.pallas_call(kernel, in_specs=[pl.BlockSpec(memory_space=pltpu.SMEM)] +...  14.4 us
    ppermute x3, starting transfers between devices, body(): coarse = [lax.ppermute(piece, 'ctx', chip_shift(step)) for step in COARSE]  10.4 us
    ppermute x1, starting transfers between devices, body(): near_swapped = lax.ppermute(near, 'ctx', swap)  4.75 us
    ppermute x1, starting transfers between devices, body(): other = lax.ppermute(rows, 'head', across_x)  3.66 us
    ppermute x1, starting transfers between devices, body(): sooner = lax.ppermute(coarse, 'ctx', chip_shift(-1))  3.57 us
    ppermute x3, waiting for transfers between devices, body(): coarse = [lax.ppermute(piece, 'ctx', chip_shift(step)) for step in COARSE]  3.08 us
    ppermute x1, starting transfers between devices, body(): opposite = lax.ppermute(piece, 'head', across_y)  2.95 us
    ppermute x1, starting transfers between devices, body(): got = lax.ppermute(bundle, ('ctx', 'head'), apart)  2.77 us
  transfers between devices with their start and end apart: 14, of which 3 were waited for; matrix products, arithmetic and copies ran while one was open for 0% of the time, Pallas kernels for 26%

profile of v7, /device:TPU:1, one launch (start us, length us, event | category | flops | bytes accessed | tf_op | source)
XLA Modules:
  0.0 58.8 jit_solution(14913897888722672175)
XLA Ops:
  0.0 0.9 %shard_map.100.own_ref = bf16[16,2112]{1,0:T(8,128)(2,1)S(1)} custom-call(bf16[16,1536]{1,0:T(8,128)(2,1)} %q_ref.1, f32[1536]{0:T(1024)} %q_gain_ref.1, bf16[16,576]{1,0:T(8,128)(2,1)} %kv_ref.1, f32[512]{0:T(512)} %kv_gain_ref.1), custom_call_target="tpu_custom_call" | custom-call | tf_op jit(solution)/shard_map/pallas_call | solution.py:356
  0.9 3.7 %collective-permute-start = (bf16[16,2112]{1,0:T(8,128)(2,1)S(1)}, bf16[16,2112]{1,0:T(8,128)(2,1)S(1)}, u32[]{:S(2)}, u32[]{:S(2)}) collective-permute-start(bf16[16,2112]{1,0:T(8,128)(2,1)S(1)} %shard_map.100.own_ref), channel_id=1, source_target_pairs={{0,1},{1,0},{2,3},{3,2},{4,5},{5,4},{6,7},{7,6},{8,9},{9,8},{10,11... | collective-permute-start | bytes 202760 | tf_op jit(solution)/shard_map/ppermute | solution.py:361
  4.6 0.0 copy-start
  4.6 1.6 %copy-done = bf16[512,2048]{1,0:T(8,128)(2,1)S(1)} copy-done((bf16[512,2048]{1,0:T(8,128)(2,1)S(1)}, bf16[512,2048]{1,0:T(8,128)(2,1)}, u32[]{:S(2)}) %copy-start) | copy-done | bytes 2097176
  6.2 0.5 shard_map.101
  6.7 0.0 collective-permute-done.other_ref
  6.7 0.1 shard_map.102
  6.7 2.9 %collective-permute-start.1 = (bf16[16,1152]{1,0:T(8,128)(2,1)S(1)}, bf16[16,1152]{1,0:T(8,128)(2,1)S(1)}, u32[]{:S(2)}, u32[]{:S(2)}) collective-permute-start(bf16[16,1152]{1,0:T(8,128)(2,1)S(1)} %get-tuple-element.29.refs_0_), channel_id=1, source_target_pairs={{0,4},{1,5},{2,6},{3,7},{4,0},{5,1},{6,2},{7,3},{8,12},{9,13},{10,... | collective-permute-start | bytes 110600 | tf_op jit(solution)/shard_map/ppermute | solution.py:383
  9.7 0.1 collective-permute-start.5
  9.8 2.3 %shard_map.103.refs_2_.refs_3_ = bf16[1536,1536]{1,0:T(8,128)(2,1)S(1)} custom-call(bf16[1536,1536]{1,0:T(8,128)(2,1)} %from_ref), custom_call_target="tpu_custom_call" | custom-call | tf_op jit(solution)/shard_map/pallas_call | solution.py:385
  12.1 0.0 collective-permute-done.1.refs_1_
  12.2 0.0 copy-start.1
  12.2 7.0 %collective-permute-start.2 = (bf16[32,1152]{1,0:T(8,128)(2,1)S(1)}, bf16[32,1152]{1,0:T(8,128)(2,1)S(1)}, u32[]{:S(2)}, u32[]{:S(2)}) collective-permute-start(bf16[32,1152]{1,0:T(8,128)(2,1)S(1)} %shard_map.104), channel_id=1, source_target_pairs={{0,64},{8,72},{16,80},{24,88},{32,96},{40,104},{48,112},{56,120},{... | collective-permute-start | bytes 221192 | tf_op jit(solution)/shard_map/ppermute | solution.py:395
  19.2 0.7 %collective-permute-start.3 = (bf16[32,1152]{1,0:T(8,128)(2,1)S(1)}, bf16[32,1152]{1,0:T(8,128)(2,1)S(1)}, u32[]{:S(2)}, u32[]{:S(2)}) collective-permute-start(bf16[32,1152]{1,0:T(8,128)(2,1)S(1)} %shard_map.104), channel_id=1, source_target_pairs={{0,16},{8,24},{16,32},{24,40},{32,48},{40,56},{48,64},{56,72},{64,... | collective-permute-start | bytes 221192 | tf_op jit(solution)/shard_map/ppermute | solution.py:395
  19.9 2.7 %collective-permute-start.4 = (bf16[32,1152]{1,0:T(8,128)(2,1)S(1)}, bf16[32,1152]{1,0:T(8,128)(2,1)S(1)}, u32[]{:S(2)}, u32[]{:S(2)}) collective-permute-start(bf16[32,1152]{1,0:T(8,128)(2,1)S(1)} %shard_map.104), channel_id=1, source_target_pairs={{0,112},{8,120},{16,128},{24,136},{32,144},{40,152},{48,160},{56,1... | collective-permute-start | bytes 221192 | tf_op jit(solution)/shard_map/ppermute | solution.py:395
  22.6 0.0 collective-permute-done.2.refs_0_
  22.6 3.1 %collective-permute-done.3.refs_1_ = bf16[32,1152]{1,0:T(8,128)(2,1)S(1)} collective-permute-done((bf16[32,1152]{1,0:T(8,128)(2,1)S(1)}, bf16[32,1152]{1,0:T(8,128)(2,1)S(1)}, u32[]{:S(2)}, u32[]{:S(2)}) %collective-permute-start.3) | collective-permute-done | bytes 73760 | tf_op jit(solution)/shard_map/ppermute | solution.py:395
  25.7 0.0 collective-permute-done.4.refs_2_
  25.7 0.0 collective-permute-done.5.q_got_ref
  25.8 2.8 %collective-permute-start.6 = (bf16[32,6528]{1,0:T(8,128)(2,1)S(1)}, bf16[32,6528]{1,0:T(8,128)(2,1)S(1)}, u32[]{:S(2)}, u32[]{:S(2)}) collective-permute-start(bf16[32,6528]{1,0:T(8,128)(2,1)S(1)} %get-tuple-element.33), channel_id=1, source_target_pairs={{0,2},{1,3},{2,4},{3,5},{4,6},{5,7},{6,0},{7,1},{8,14},{9,15},{10,... | collective-permute-start | bytes 1253384 | tf_op jit(solution)/shard_map/ppermute | solution.py:412
  28.5 0.0 collective-permute-start.7
  28.5 3.6 %collective-permute-start.8 = (bf16[96,1152]{1,0:T(8,128)(2,1)S(1)}, bf16[96,1152]{1,0:T(8,128)(2,1)S(1)}, u32[]{:S(2)}, u32[]{:S(2)}) collective-permute-start(bf16[96,1152]{1,0:T(8,128)(2,1)S(1)} %shard_map.105.coarse_ref.refs_5_), channel_id=1, source_target_pairs={{0,240},{8,248},{16,0},{24,8},{32,16},{40,24},{48,32},{56,40},{64,... | collective-permute-start | bytes 663560 | tf_op jit(solution)/shard_map/ppermute | solution.py:411
  32.1 1.4 %collective-permute-done.6.refs_2_.refs_9_ = bf16[32,6528]{1,0:T(8,128)(2,1)S(1)} collective-permute-done((bf16[32,6528]{1,0:T(8,128)(2,1)S(1)}, bf16[32,6528]{1,0:T(8,128)(2,1)S(1)}, u32[]{:S(2)}, u32[]{:S(2)}) %collective-permute-start.6) | collective-permute-done | bytes 417824 | tf_op jit(solution)/shard_map/ppermute | solution.py:412
  33.5 0.0 copy-start.3
  33.5 2.1 %shard_map.107.refs_2_.refs_1_ = bf16[8,128,256]{2,1,0:T(8,128)(2,1)S(1)} custom-call(s32[3]{0:T(128)} %refs_0_.7, bf16[32,3072]{1,0:T(8,128)(2,1)S(1)} %get-tuple-element.32.refs_1_, bf16[32,6528]{1,0:T(8,128)(2,1)S(1)} %collective-permute-done.6.refs_2_.refs_9_, bf16[1536,1536]{1,0:T(8,128)(2,1)S(1)} %shard_map.103.refs_2_.refs_3_), custom_call_target="tpu_custom_call" | custom-call | tf_op jit(solution)/shard_map/pallas_call | solution.py:415
  35.6 0.0 collective-permute-done.7.refs_0_
  35.6 0.0 collective-permute-done.8.refs_1_
  35.7 4.8 %collective-permute-start.11 = (bf16[192,1152]{1,0:T(8,128)(2,1)S(1)}, bf16[192,1152]{1,0:T(8,128)(2,1)S(1)}, u32[]{:S(2)}, u32[]{:S(2)}) collective-permute-start(bf16[192,1152]{1,0:T(8,128)(2,1)S(1)} %shard_map.108.refs_6_), channel_id=1, source_target_pairs={{0,8},{8,0},{16,24},{24,16},{32,40},{40,32},{48,56},{56,48},{64,72... | collective-permute-start | bytes 1327112 | tf_op jit(solution)/shard_map/ppermute | solution.py:426
  40.4 1.5 %collective-permute-start.9 = (bf16[192,1152]{1,0:T(8,128)(2,1)S(1)}, bf16[192,1152]{1,0:T(8,128)(2,1)S(1)}, u32[]{:S(2)}, u32[]{:S(2)}) collective-permute-start(bf16[192,1152]{1,0:T(8,128)(2,1)S(1)} %shard_map.108.refs_6_), channel_id=1, source_target_pairs={{0,2},{1,3},{2,4},{3,5},{4,6},{5,7},{6,0},{7,1},{8,14},{9,15},{10,... | collective-permute-start | bytes 1327112 | tf_op jit(solution)/shard_map/ppermute | solution.py:425
  41.9 0.0 collective-permute-start.12
  41.9 0.5 collective-permute-start.10
  42.4 1.6 %collective-permute-done.10.refs_7_ = bf16[96,1152]{1,0:T(8,128)(2,1)S(1)} collective-permute-done((bf16[96,1152]{1,0:T(8,128)(2,1)S(1)}, bf16[96,1152]{1,0:T(8,128)(2,1)S(1)}, u32[]{:S(2)}, u32[]{:S(2)}) %collective-permute-start.10) | collective-permute-done | bytes 221216 | tf_op jit(solution)/shard_map/ppermute | solution.py:413
  44.0 0.0 collective-permute-done.12.refs_10_
  44.0 0.0 collective-permute-done.11.refs_8_
  44.0 0.0 copy-done.1
  44.0 0.0 copy-start.2
  44.0 7.0 %shard_map.109 = (f32[8,128,128]{2,1,0:T(8,128)S(1)}, f32[8,128,128]{2,1,0:T(8,128)S(1)}, f32[8,128,128]{2,1,0:T(8,128)S(1)}) custom-call(s32[3]{0:T(128)} %refs_0_.7, bf16[8,128,256]{2,1,0:T(8,128)(2,1)S(1)} %shard_map.107.refs_2_.refs_1_, s32[5,1536]{1,0:T(8,128)S(1)} %copy-done.1, bf16[1024,512]{1,0:T(8,128)(2,1)S(1)} %get-tuple-element.27.ready_ref.refs_3_, ...), custom_call_target="tpu_custom_call" | custom-call | tf_op jit(solution)/shard_map/pallas_call | solution.py:311
  51.0 0.0 collective-permute-done.9.refs_5_
  51.0 0.2 collective-permute-start.13
  51.2 0.0 copy-done.3
  51.2 3.4 %shard_map.110 = (f32[8,128,128]{2,1,0:T(8,128)S(1)}, f32[8,128,128]{2,1,0:T(8,128)S(1)}, f32[8,128,128]{2,1,0:T(8,128)S(1)}) custom-call(s32[3]{0:T(128)} %refs_0_.7, bf16[8,128,256]{2,1,0:T(8,128)(2,1)S(1)} %shard_map.107.refs_2_.refs_1_, s32[5,384]{1,0:T(8,128)S(1)} %copy-done.3, bf16[1024,512]{1,0:T(8,128)(2,1)S(1)} %get-tuple-element.27.ready_ref.refs_3_, ...), custom_call_target="tpu_custom_call" | custom-call | tf_op jit(solution)/shard_map/pallas_call | solution.py:311
  54.6 0.0 collective-permute-done.13.refs_5_
  54.6 0.0 copy-done.2
  54.6 4.0 %shard_map.111 = bf16[128,1024]{1,0:T(8,128)(2,1)} custom-call(s32[3]{0:T(128)} %refs_0_.7, bf16[8,128,256]{2,1,0:T(8,128)(2,1)S(1)} %shard_map.107.refs_2_.refs_1_, s32[5,384]{1,0:T(8,128)S(1)} %copy-done.2, bf16[1024,512]{1,0:T(8,128)(2,1)S(1)} %get-tuple-element.27.ready_ref.refs_3_, bf16[512,1024]{1,0:T(8,128)(2,1)S(1)} %get-tuple-element.34.refs_4_, ...), custom_call_target="tpu_custom_call" | custom-call | tf_op jit(solution)/shard_map/pallas_call | solution.py:311
  (4 shorter events, 0.1 us)
Async XLA Ops:
  0.9 5.7 %collective-permute-start = (bf16[16,2112]{1,0:T(8,128)(2,1)S(1)}, bf16[16,2112]{1,0:T(8,128)(2,1)S(1)}, u32[]{:S(2)}, u32[]{:S(2)}) collective-permute-start(bf16[16,2112]{1,0:T(8,128)(2,1)S(1)} %shard_map.100.own_ref), channel_id=1, source_target_pairs={{0,1},{1,0},{2,3},{3,2},{4,5},{5,4},{6,7},{7,6},{8,9},{9,8},{10,11... | collective-permute-start | bytes 202760 | tf_op jit(solution)/shard_map/ppermute | solution.py:361
  4.6 1.6 %copy-start = (bf16[512,2048]{1,0:T(8,128)(2,1)S(1)}, bf16[512,2048]{1,0:T(8,128)(2,1)}, u32[]{:S(2)}) copy-start(bf16[512,2048]{1,0:T(8,128)(2,1)} %w_ref) | copy-start | bytes 6291460
  6.7 5.4 %collective-permute-start.1 = (bf16[16,1152]{1,0:T(8,128)(2,1)S(1)}, bf16[16,1152]{1,0:T(8,128)(2,1)S(1)}, u32[]{:S(2)}, u32[]{:S(2)}) collective-permute-start(bf16[16,1152]{1,0:T(8,128)(2,1)S(1)} %get-tuple-element.29.refs_0_), channel_id=1, source_target_pairs={{0,4},{1,5},{2,6},{3,7},{4,0},{5,1},{6,2},{7,3},{8,12},{9,13},{10,... | collective-permute-start | bytes 110600 | tf_op jit(solution)/shard_map/ppermute | solution.py:383
  9.7 16.0 %collective-permute-start.5 = (bf16[16,3072]{1,0:T(8,128)(2,1)S(1)}, bf16[16,3072]{1,0:T(8,128)(2,1)S(1)}, u32[]{:S(2)}, u32[]{:S(2)}) collective-permute-start(bf16[16,3072]{1,0:T(8,128)(2,1)S(1)} %get-tuple-element.31.q_own_ref), channel_id=1, source_target_pairs={{0,4},{1,5},{2,6},{3,7},{4,0},{5,1},{6,2},{7,3},{8,12},{9,13},{10,... | collective-permute-start | bytes 294920 | tf_op jit(solution)/shard_map/ppermute | solution.py:394
  12.2 31.8 %copy-start.1 = (s32[5,1536]{1,0:T(8,128)S(1)}, s32[5,1536]{1,0:T(8,128)}, u32[]{:S(2)}) copy-start(s32[5,1536]{1,0:T(8,128)} %constant.6.clone.refs_2_) | copy-start | bytes 92164
  12.2 10.4 %collective-permute-start.2 = (bf16[32,1152]{1,0:T(8,128)(2,1)S(1)}, bf16[32,1152]{1,0:T(8,128)(2,1)S(1)}, u32[]{:S(2)}, u32[]{:S(2)}) collective-permute-start(bf16[32,1152]{1,0:T(8,128)(2,1)S(1)} %shard_map.104), channel_id=1, source_target_pairs={{0,64},{8,72},{16,80},{24,88},{32,96},{40,104},{48,112},{56,120},{... | collective-permute-start | bytes 221192 | tf_op jit(solution)/shard_map/ppermute | solution.py:395
  19.2 6.5 %collective-permute-start.3 = (bf16[32,1152]{1,0:T(8,128)(2,1)S(1)}, bf16[32,1152]{1,0:T(8,128)(2,1)S(1)}, u32[]{:S(2)}, u32[]{:S(2)}) collective-permute-start(bf16[32,1152]{1,0:T(8,128)(2,1)S(1)} %shard_map.104), channel_id=1, source_target_pairs={{0,16},{8,24},{16,32},{24,40},{32,48},{40,56},{48,64},{56,72},{64,... | collective-permute-start | bytes 221192 | tf_op jit(solution)/shard_map/ppermute | solution.py:395
  19.9 5.8 %collective-permute-start.4 = (bf16[32,1152]{1,0:T(8,128)(2,1)S(1)}, bf16[32,1152]{1,0:T(8,128)(2,1)S(1)}, u32[]{:S(2)}, u32[]{:S(2)}) collective-permute-start(bf16[32,1152]{1,0:T(8,128)(2,1)S(1)} %shard_map.104), channel_id=1, source_target_pairs={{0,112},{8,120},{16,128},{24,136},{32,144},{40,152},{48,160},{56,1... | collective-permute-start | bytes 221192 | tf_op jit(solution)/shard_map/ppermute | solution.py:395
  25.8 7.8 %collective-permute-start.6 = (bf16[32,6528]{1,0:T(8,128)(2,1)S(1)}, bf16[32,6528]{1,0:T(8,128)(2,1)S(1)}, u32[]{:S(2)}, u32[]{:S(2)}) collective-permute-start(bf16[32,6528]{1,0:T(8,128)(2,1)S(1)} %get-tuple-element.33), channel_id=1, source_target_pairs={{0,2},{1,3},{2,4},{3,5},{4,6},{5,7},{6,0},{7,1},{8,14},{9,15},{10,... | collective-permute-start | bytes 1253384 | tf_op jit(solution)/shard_map/ppermute | solution.py:412
  28.5 7.1 %collective-permute-start.7 = (bf16[96,1152]{1,0:T(8,128)(2,1)S(1)}, bf16[96,1152]{1,0:T(8,128)(2,1)S(1)}, u32[]{:S(2)}, u32[]{:S(2)}) collective-permute-start(bf16[96,1152]{1,0:T(8,128)(2,1)S(1)} %shard_map.105.coarse_ref.refs_5_), channel_id=1, source_target_pairs={{0,16},{8,24},{16,32},{24,40},{32,48},{40,56},{48,64},{56,72},{64,... | collective-permute-start | bytes 663560 | tf_op jit(solution)/shard_map/ppermute | solution.py:410
  28.5 7.1 %collective-permute-start.8 = (bf16[96,1152]{1,0:T(8,128)(2,1)S(1)}, bf16[96,1152]{1,0:T(8,128)(2,1)S(1)}, u32[]{:S(2)}, u32[]{:S(2)}) collective-permute-start(bf16[96,1152]{1,0:T(8,128)(2,1)S(1)} %shard_map.105.coarse_ref.refs_5_), channel_id=1, source_target_pairs={{0,240},{8,248},{16,0},{24,8},{32,16},{40,24},{48,32},{56,40},{64,... | collective-permute-start | bytes 663560 | tf_op jit(solution)/shard_map/ppermute | solution.py:411
  33.5 17.7 %copy-start.3 = (s32[5,384]{1,0:T(8,128)S(1)}, s32[5,384]{1,0:T(8,128)}, u32[]{:S(2)}) copy-start(s32[5,384]{1,0:T(8,128)} %constant.7.clone.refs_2_) | copy-start | bytes 23044
  35.7 8.3 %collective-permute-start.11 = (bf16[192,1152]{1,0:T(8,128)(2,1)S(1)}, bf16[192,1152]{1,0:T(8,128)(2,1)S(1)}, u32[]{:S(2)}, u32[]{:S(2)}) collective-permute-start(bf16[192,1152]{1,0:T(8,128)(2,1)S(1)} %shard_map.108.refs_6_), channel_id=1, source_target_pairs={{0,8},{8,0},{16,24},{24,16},{32,40},{40,32},{48,56},{56,48},{64,72... | collective-permute-start | bytes 1327112 | tf_op jit(solution)/shard_map/ppermute | solution.py:426
  40.4 10.6 %collective-permute-start.9 = (bf16[192,1152]{1,0:T(8,128)(2,1)S(1)}, bf16[192,1152]{1,0:T(8,128)(2,1)S(1)}, u32[]{:S(2)}, u32[]{:S(2)}) collective-permute-start(bf16[192,1152]{1,0:T(8,128)(2,1)S(1)} %shard_map.108.refs_6_), channel_id=1, source_target_pairs={{0,2},{1,3},{2,4},{3,5},{4,6},{5,7},{6,0},{7,1},{8,14},{9,15},{10,... | collective-permute-start | bytes 1327112 | tf_op jit(solution)/shard_map/ppermute | solution.py:425
  41.9 2.1 %collective-permute-start.12 = (bf16[32,6528]{1,0:T(8,128)(2,1)S(1)}, bf16[32,6528]{1,0:T(8,128)(2,1)S(1)}, u32[]{:S(2)}, u32[]{:S(2)}) collective-permute-start(bf16[32,6528]{1,0:T(8,128)(2,1)S(1)} %collective-permute-done.6.refs_2_.refs_9_), channel_id=1, source_target_pairs={{0,8},{8,0},{16,24},{24,16},{32,40},{40,32},{48,56},{56,48},{64,72... | collective-permute-start | bytes 1253384 | tf_op jit(solution)/shard_map/ppermute | solution.py:427
  41.9 2.1 %collective-permute-start.10 = (bf16[96,1152]{1,0:T(8,128)(2,1)S(1)}, bf16[96,1152]{1,0:T(8,128)(2,1)S(1)}, u32[]{:S(2)}, u32[]{:S(2)}) collective-permute-start(bf16[96,1152]{1,0:T(8,128)(2,1)S(1)} %shard_map.105.coarse_ref.refs_5_), channel_id=1, source_target_pairs={{0,8},{8,0},{16,24},{24,16},{32,40},{40,32},{48,56},{56,48},{64,72... | collective-permute-start | bytes 663560 | tf_op jit(solution)/shard_map/ppermute | solution.py:413
  44.0 10.6 %copy-start.2 = (s32[5,384]{1,0:T(8,128)S(1)}, s32[5,384]{1,0:T(8,128)}, u32[]{:S(2)}) copy-start(s32[5,384]{1,0:T(8,128)} %constant.8.clone.refs_2_) | copy-start | bytes 23044
  51.0 3.6 %collective-permute-start.13 = (bf16[192,1152]{1,0:T(8,128)(2,1)S(1)}, bf16[192,1152]{1,0:T(8,128)(2,1)S(1)}, u32[]{:S(2)}, u32[]{:S(2)}) collective-permute-start(bf16[192,1152]{1,0:T(8,128)(2,1)S(1)} %collective-permute-done.9.refs_5_), channel_id=1, source_target_pairs={{0,8},{8,0},{16,24},{24,16},{32,40},{40,32},{48,56},{56,48},{64,72... | collective-permute-start | bytes 1327112 | tf_op jit(solution)/shard_map/ppermute | solution.py:441

commit v8 on v7

--- a/solution.py
+++ b/solution.py
@@ -16,7 +16,7 @@
 EPSILON = 1e-06
 MASKED = -1e30
 FLOOR = -1e29
-COARSE = (4, 1, 7)
+COARSE = (7, 1, 4)
 SCORE_SCALE = math.log2(math.e) / math.sqrt(ND + RD)
 
 
@@ -69,17 +69,6 @@
         kv_ref[:, n * KL : (n + 1) * KL] = ref[:, :KL]
         q_ref[:, n * q_size : (n + 1) * q_size] = ref[:, KL:q_end]
     kv_ref[:, 2 * KL :] = jnp.concatenate([own_ref[:, q_end:], other_ref[:, q_end:]], axis=1)
-
-
-def bundle_kernel(coarse_ref, q_own_ref, q_got_ref, q_ref, bundle_ref):
-    size, width = q_ref.shape[0], coarse_ref.shape[1]
-    n_parts = coarse_ref.shape[0] // size
-    for n in range(n_parts):
-        bundle_ref[:, n * width : (n + 1) * width] = coarse_ref[n * size : (n + 1) * size, :]
-    for n, ref in enumerate((q_own_ref, q_got_ref)):
-        rows = slice(n * ref.shape[0], (n + 1) * ref.shape[0])
-        q_ref[rows, :] = ref[...]
-        bundle_ref[rows, n_parts * width :] = ref[...]
 
 
 def join_kernel(sizes, n_after, *refs):
@@ -122,16 +111,15 @@
     return start
 
 
-def query_kernel(q_at, lengths, own, got, w_ref, out_ref, rows_ref):
+def query_kernel(lengths, own, got, w_ref, out_ref, rows_ref):
     chip, core, y, xh = here()
     width = rows_ref.shape[1]
-    for base, ref, lane_at in ((y, own, 0), (y + jnp.where(core == 0, 3, 1), got, q_at)):
+    for base, ref in ((y, own), (y + jnp.where(core == 0, 3, 1), got)):
         for n in range(4):
             turn, half = n // 2, n % 2
             place = lax.rem(base + 2 * turn, 4) * 32 + lax.rem(xh + half, 2) * 16
             at = pl.multiple_of(place, 16)
-            lanes = slice(lane_at + half * width, lane_at + (half + 1) * width)
-            rows = ref[16 * turn : 16 * turn + 16, lanes]
+            rows = ref[16 * turn : 16 * turn + 16, half * width : (half + 1) * width]
             rows_ref[pl.ds(at, 16), :] = rows
 
     shape = (rows_ref.shape[0], LANES)
@@ -381,6 +369,7 @@
         compiler_params=SMALL,
     )(fast(rows), fast(other), fast(w_key))
     opposite = lax.ppermute(piece, "head", across_y)
+    (piece,) = join([[piece, opposite]])
     w_query, piece = lax.optimization_barrier((w_query, piece))
     w_query = pl.pallas_call(
         fetch_kernel,
@@ -390,38 +379,28 @@
         scratch_shapes=[pltpu.SemaphoreType.DMA],
         compiler_params=SMALL,
     )(slow(w_query))
-    (piece,) = join([[piece, opposite]], after=[w_query])
     q_opposite = lax.ppermute(q_pair, "head", across_y)
     coarse = [lax.ppermute(piece, "ctx", chip_shift(step)) for step in COARSE]
 
-    set_shape = coarse[0].shape
-    q_at = len(COARSE) * set_shape[1]
-    (coarse,) = join([coarse])
-    q_set, bundle = pl.pallas_call(
-        bundle_kernel,
-        in_specs=[vmem] * 3,
-        out_specs=[vmem] * 2,
-        out_shape=[
-            pltpu.VMEM((set_shape[0], q_pair.shape[1]), jnp.bfloat16),
-            pltpu.VMEM((set_shape[0], q_at + q_pair.shape[1]), jnp.bfloat16),
-        ],
-        compiler_params=SMALL,
-    )(*[fast(a) for a in (coarse, q_pair, q_opposite)])
+    (coarse,) = join([coarse], after=[w_query])
+    (q_set,) = join([[q_pair, q_opposite]], after=[coarse])
+    coarse, q_set = lax.optimization_barrier((coarse, q_set))
     later = lax.ppermute(coarse, "ctx", chip_shift(1))
     sooner = lax.ppermute(coarse, "ctx", chip_shift(-1))
-    got = lax.ppermute(bundle, ("ctx", "head"), apart)
+    q_got = lax.ppermute(q_set, ("ctx", "head"), apart)
+    got = lax.ppermute(coarse, ("ctx", "head"), apart)
     coarse_swapped = lax.ppermute(coarse, "ctx", swap)
 
     queries = pl.pallas_call(
-        lambda *refs: query_kernel(q_at, *refs),
+        query_kernel,
         in_specs=[pl.BlockSpec(memory_space=pltpu.SMEM)] + [vmem] * 3,
         out_specs=vmem,
         out_shape=pltpu.VMEM((heads_here, tok_dev, 2 * LANES), jnp.bfloat16),
         scratch_shapes=[pltpu.VMEM((tok_dev, w_query.shape[0]), jnp.bfloat16)],
         compiler_params=SMALL,
-    )(slow(doc_lengths), fast(q_set), fast(got), fast(w_query))
-
-    (near,) = join([[later, sooner]], after=[queries])
+    )(slow(doc_lengths), fast(q_set), fast(q_got), fast(w_query))
+
+    (near,) = join([[later, sooner]], after=[q_got])
     received = lax.ppermute(near, ("ctx", "head"), apart)
     near_swapped = lax.ppermute(near, "ctx", swap)
     got_swapped = lax.ppermute(got, "ctx", swap)
@@ -432,9 +411,7 @@
     near_slots = [*[k + 1 for k in COARSE], *[k - 1 for k in COARSE]]
     views = [(0, 0, 0, 0, COARSE), (1, 0, 0, 0, near_slots)]
     views += [(2, 0, 1, 0, COARSE), (3, 0, 1, 0, near_slots)]
-    for partner in range(2):
-        for n, k in enumerate(COARSE):
-            views.append((4 + partner, n * set_shape[1], partner, 1, [k]))
+    views += [(4, 0, 0, 1, COARSE), (5, 0, 1, 1, COARSE)]
     pieces = [coarse, near, coarse_swapped, near_swapped, got, got_swapped]
     state = attend_to(pieces, views, 2, None)
     received, state = lax.optimization_barrier((received, state))

time: 59.1 us -> 59.8 us (1.012)
  starting transfers between devices: 30.4 us -> 31.3 us
    ppermute x1, starting transfers between devices: 3.57 us -> 1.12 us  [body(): sooner = lax.ppermute(coarse, 'ctx', chip_shift(-1))]
    ppermute x3, waiting for transfers between devices: 3.08 us -> 1.15 us  [body(): coarse = [lax.ppermute(piece, 'ctx', chip_shift(step)) for step in COARSE]]
    ppermute x1, waiting for transfers between devices: 1.56 us -> 0.01 us  [body(): coarse_swapped = lax.ppermute(coarse, 'ctx', swap)]
    ppermute x1, waiting for transfers between devices: 0.01 us -> 1.3 us  [body(): opposite = lax.ppermute(piece, 'head', across_y)]
    ppermute x1, starting transfers between devices: 4.75 us -> 6.03 us  [body(): near_swapped = lax.ppermute(near, 'ctx', swap)]
    ppermute x1, starting transfers between devices: 1.48 us -> 2.73 us  [body(): received = lax.ppermute(near, ('ctx', 'head'), apart)]
    ppermute x1, waiting for transfers between devices: 0.01 us -> 1.21 us  [body(): later = lax.ppermute(coarse, 'ctx', chip_shift(1))]
    ppermute x1 -> x2, waiting for transfers between devices: 1.41 us -> 2.15 us  [the longest x1 2.15 us: body(): q_got = lax.ppermute(q_set, ('ctx', 'head'), apart)]
  transfers between devices with their start and end apart: 14 -> 15, of which waited for: 3 -> 4; matrix products, arithmetic and copies ran while one was open for 0% -> 0% of each run, Pallas kernels for 26% -> 26%
where the time goes in v8:
time: 59.8 us; the launch traced here: 59.5 us
  starting transfers between devices  31.3 us (52%)
  Pallas kernels  20.4 us (34%)
  waiting for transfers between devices  5.83 us (10%)
  local copies, waits for them, and re-layouts  1.61 us (3%)
    pallas_call x3, Pallas kernels, attend(): pl.pallas_call(kernel, in_specs=[pl.BlockSpec(memory_space=pltpu.SMEM)] +...  14.6 us
    ppermute x3, starting transfers between devices, body(): coarse = [lax.ppermute(piece, 'ctx', chip_shift(step)) for step in COARSE]  10.3 us
    ppermute x1, starting transfers between devices, body(): near_swapped = lax.ppermute(near, 'ctx', swap)  6.03 us
    ppermute x1, starting transfers between devices, body(): other = lax.ppermute(rows, 'head', across_x)  3.66 us
    ppermute x1, starting transfers between devices, body(): opposite = lax.ppermute(piece, 'head', across_y)  2.95 us
    ppermute x1, starting transfers between devices, body(): received = lax.ppermute(near, ('ctx', 'head'), apart)  2.73 us
    ppermute x1, starting transfers between devices, body(): q_got = lax.ppermute(q_set, ('ctx', 'head'), apart)  2.65 us
    pallas_call x1, Pallas kernels, body(): pl.pallas_call(fetch_kernel, in_specs=[pl.BlockSpec(memory_space=pl.ANY)]...  2.34 us
  transfers between devices with their start and end apart: 15, of which 4 were waited for; matrix products, arithmetic and copies ran while one was open for 0% of the time, Pallas kernels for 26%

profile of v8, /device:TPU:1, one launch (start us, length us, event | category | flops | bytes accessed | tf_op | source)
XLA Modules:
  0.0 59.5 jit_solution(4613623267587827462)
XLA Ops:
  0.0 0.9 %shard_map.100.own_ref = bf16[16,2112]{1,0:T(8,128)(2,1)S(1)} custom-call(bf16[16,1536]{1,0:T(8,128)(2,1)} %q_ref.1, f32[1536]{0:T(1024)} %q_gain_ref.1, bf16[16,576]{1,0:T(8,128)(2,1)} %kv_ref.1, f32[512]{0:T(512)} %kv_gain_ref.1), custom_call_target="tpu_custom_call" | custom-call | tf_op jit(solution)/shard_map/pallas_call | solution.py:344
  0.9 3.7 %collective-permute-start = (bf16[16,2112]{1,0:T(8,128)(2,1)S(1)}, bf16[16,2112]{1,0:T(8,128)(2,1)S(1)}, u32[]{:S(2)}, u32[]{:S(2)}) collective-permute-start(bf16[16,2112]{1,0:T(8,128)(2,1)S(1)} %shard_map.100.own_ref), channel_id=1, source_target_pairs={{0,1},{1,0},{2,3},{3,2},{4,5},{5,4},{6,7},{7,6},{8,9},{9,8},{10,11... | collective-permute-start | bytes 202760 | tf_op jit(solution)/shard_map/ppermute | solution.py:349
  4.6 0.0 copy-start
  4.6 1.6 %copy-done = bf16[512,2048]{1,0:T(8,128)(2,1)S(1)} copy-done((bf16[512,2048]{1,0:T(8,128)(2,1)S(1)}, bf16[512,2048]{1,0:T(8,128)(2,1)}, u32[]{:S(2)}) %copy-start) | copy-done | bytes 2097176
  6.2 0.5 shard_map.101
  6.7 0.0 collective-permute-done.other_ref
  6.7 0.1 shard_map.102
  6.8 2.9 %collective-permute-start.1 = (bf16[16,1152]{1,0:T(8,128)(2,1)S(1)}, bf16[16,1152]{1,0:T(8,128)(2,1)S(1)}, u32[]{:S(2)}, u32[]{:S(2)}) collective-permute-start(bf16[16,1152]{1,0:T(8,128)(2,1)S(1)} %get-tuple-element.28.refs_0_), channel_id=1, source_target_pairs={{0,4},{1,5},{2,6},{3,7},{4,0},{5,1},{6,2},{7,3},{8,12},{9,13},{10,... | collective-permute-start | bytes 110600 | tf_op jit(solution)/shard_map/ppermute | solution.py:371
  9.7 0.1 collective-permute-start.5
  9.8 1.3 %collective-permute-done.1.refs_1_ = bf16[16,1152]{1,0:T(8,128)(2,1)S(1)} collective-permute-done((bf16[16,1152]{1,0:T(8,128)(2,1)S(1)}, bf16[16,1152]{1,0:T(8,128)(2,1)S(1)}, u32[]{:S(2)}, u32[]{:S(2)}) %collective-permute-start.1) | collective-permute-done | bytes 36896 | tf_op jit(solution)/shard_map/ppermute | solution.py:371
  11.1 6.9 %collective-permute-start.4 = (bf16[32,1152]{1,0:T(8,128)(2,1)S(1)}, bf16[32,1152]{1,0:T(8,128)(2,1)S(1)}, u32[]{:S(2)}, u32[]{:S(2)}) collective-permute-start(bf16[32,1152]{1,0:T(8,128)(2,1)S(1)} %shard_map.103), channel_id=1, source_target_pairs={{0,64},{8,72},{16,80},{24,88},{32,96},{40,104},{48,112},{56,120},{... | collective-permute-start | bytes 221192 | tf_op jit(solution)/shard_map/ppermute | solution.py:383
  18.0 0.7 %collective-permute-start.3 = (bf16[32,1152]{1,0:T(8,128)(2,1)S(1)}, bf16[32,1152]{1,0:T(8,128)(2,1)S(1)}, u32[]{:S(2)}, u32[]{:S(2)}) collective-permute-start(bf16[32,1152]{1,0:T(8,128)(2,1)S(1)} %shard_map.103), channel_id=1, source_target_pairs={{0,16},{8,24},{16,32},{24,40},{32,48},{40,56},{48,64},{56,72},{64,... | collective-permute-start | bytes 221192 | tf_op jit(solution)/shard_map/ppermute | solution.py:383
  18.8 2.7 %collective-permute-start.2 = (bf16[32,1152]{1,0:T(8,128)(2,1)S(1)}, bf16[32,1152]{1,0:T(8,128)(2,1)S(1)}, u32[]{:S(2)}, u32[]{:S(2)}) collective-permute-start(bf16[32,1152]{1,0:T(8,128)(2,1)S(1)} %shard_map.103), channel_id=1, source_target_pairs={{0,112},{8,120},{16,128},{24,136},{32,144},{40,152},{48,160},{56,1... | collective-permute-start | bytes 221192 | tf_op jit(solution)/shard_map/ppermute | solution.py:383
  21.5 2.3 %shard_map.104.refs_3_.w_ref = bf16[1536,1536]{1,0:T(8,128)(2,1)S(1)} custom-call(bf16[1536,1536]{1,0:T(8,128)(2,1)} %from_ref), custom_call_target="tpu_custom_call" | custom-call | tf_op jit(solution)/shard_map/pallas_call | solution.py:374
  23.8 0.0 collective-permute-done.4.refs_2_
  23.8 1.1 %collective-permute-done.3.refs_1_ = bf16[32,1152]{1,0:T(8,128)(2,1)S(1)} collective-permute-done((bf16[32,1152]{1,0:T(8,128)(2,1)S(1)}, bf16[32,1152]{1,0:T(8,128)(2,1)S(1)}, u32[]{:S(2)}, u32[]{:S(2)}) %collective-permute-start.3) | collective-permute-done | bytes 73760 | tf_op jit(solution)/shard_map/ppermute | solution.py:383
  25.0 0.0 collective-permute-done.2.refs_0_
  25.0 0.0 copy-start.1
  25.0 0.0 collective-permute-done.5.refs_1_
  25.0 1.1 %collective-permute-start.8 = (bf16[96,1152]{1,0:T(8,128)(2,1)S(1)}, bf16[96,1152]{1,0:T(8,128)(2,1)S(1)}, u32[]{:S(2)}, u32[]{:S(2)}) collective-permute-start(bf16[96,1152]{1,0:T(8,128)(2,1)S(1)} %shard_map.105.refs_2_.refs_5_), channel_id=1, source_target_pairs={{0,240},{8,248},{16,0},{24,8},{32,16},{40,24},{48,32},{56,40},{64,... | collective-permute-start | bytes 663560 | tf_op jit(solution)/shard_map/ppermute | solution.py:389
  26.2 0.4 collective-permute-start.7
  26.6 2.6 %collective-permute-start.6 = (bf16[32,3072]{1,0:T(8,128)(2,1)S(1)}, bf16[32,3072]{1,0:T(8,128)(2,1)S(1)}, u32[]{:S(2)}, u32[]{:S(2)}) collective-permute-start(bf16[32,3072]{1,0:T(8,128)(2,1)S(1)} %shard_map.106.own), channel_id=1, source_target_pairs={{0,2},{1,3},{2,4},{3,5},{4,6},{5,7},{6,0},{7,1},{8,14},{9,15},{10,... | collective-permute-start | bytes 589832 | tf_op jit(solution)/shard_map/ppermute | solution.py:390
  29.2 0.5 collective-permute-start.12
  29.7 2.2 %collective-permute-done.6.got.refs_2_ = bf16[32,3072]{1,0:T(8,128)(2,1)S(1)} collective-permute-done((bf16[32,3072]{1,0:T(8,128)(2,1)S(1)}, bf16[32,3072]{1,0:T(8,128)(2,1)S(1)}, u32[]{:S(2)}, u32[]{:S(2)}) %collective-permute-start.6) | collective-permute-done | bytes 196640 | tf_op jit(solution)/shard_map/ppermute | solution.py:390
  31.8 0.0 collective-permute-done.8.refs_1_
  31.8 1.2 %collective-permute-done.7.refs_0_ = bf16[96,1152]{1,0:T(8,128)(2,1)S(1)} collective-permute-done((bf16[96,1152]{1,0:T(8,128)(2,1)S(1)}, bf16[96,1152]{1,0:T(8,128)(2,1)S(1)}, u32[]{:S(2)}, u32[]{:S(2)}) %collective-permute-start.7) | collective-permute-done | bytes 221216 | tf_op jit(solution)/shard_map/ppermute | solution.py:388
  33.1 0.0 copy-start.3
  33.1 6.0 %collective-permute-start.11 = (bf16[192,1152]{1,0:T(8,128)(2,1)S(1)}, bf16[192,1152]{1,0:T(8,128)(2,1)S(1)}, u32[]{:S(2)}, u32[]{:S(2)}) collective-permute-start(bf16[192,1152]{1,0:T(8,128)(2,1)S(1)} %shard_map.108.refs_6_), channel_id=1, source_target_pairs={{0,8},{8,0},{16,24},{24,16},{32,40},{40,32},{48,56},{56,48},{64,72... | collective-permute-start | bytes 1327112 | tf_op jit(solution)/shard_map/ppermute | solution.py:405
  39.1 2.7 %collective-permute-start.9 = (bf16[192,1152]{1,0:T(8,128)(2,1)S(1)}, bf16[192,1152]{1,0:T(8,128)(2,1)S(1)}, u32[]{:S(2)}, u32[]{:S(2)}) collective-permute-start(bf16[192,1152]{1,0:T(8,128)(2,1)S(1)} %shard_map.108.refs_6_), channel_id=1, source_target_pairs={{0,2},{1,3},{2,4},{3,5},{4,6},{5,7},{6,0},{7,1},{8,14},{9,15},{10,... | collective-permute-start | bytes 1327112 | tf_op jit(solution)/shard_map/ppermute | solution.py:404
  41.9 0.0 collective-permute-start.10
  41.9 0.0 collective-permute-done.12.refs_9_
  41.9 0.5 collective-permute-start.13
  42.4 1.9 %shard_map.107.refs_1_ = bf16[8,128,256]{2,1,0:T(8,128)(2,1)S(1)} custom-call(s32[3]{0:T(128)} %refs_0_.5, bf16[32,3072]{1,0:T(8,128)(2,1)S(1)} %shard_map.106.own, bf16[32,3072]{1,0:T(8,128)(2,1)S(1)} %collective-permute-done.6.got.refs_2_, bf16[1536,1536]{1,0:T(8,128)(2,1)S(1)} %shard_map.104.refs_3_.w_ref), custom_call_target="tpu_custom_call" | custom-call | tf_op jit(solution)/shard_map/pallas_call | solution.py:394
  44.3 0.0 copy-start.2
  44.3 0.0 collective-permute-done.10.refs_7_
  44.3 0.0 collective-permute-done.13.refs_10_
  44.4 0.0 collective-permute-done.11.refs_8_
  44.4 0.0 copy-done.1
  44.4 7.1 %shard_map.109 = (f32[8,128,128]{2,1,0:T(8,128)S(1)}, f32[8,128,128]{2,1,0:T(8,128)S(1)}, f32[8,128,128]{2,1,0:T(8,128)S(1)}) custom-call(s32[3]{0:T(128)} %refs_0_.5, bf16[8,128,256]{2,1,0:T(8,128)(2,1)S(1)} %shard_map.107.refs_1_, s32[5,1536]{1,0:T(8,128)S(1)} %copy-done.1, bf16[1024,512]{1,0:T(8,128)(2,1)S(1)} %get-tuple-element.27.ready_ref.refs_3_, ...), custom_call_target="tpu_custom_call" | custom-call | tf_op jit(solution)/shard_map/pallas_call | solution.py:299
  51.5 0.0 collective-permute-done.9.refs_5_
  51.5 0.3 collective-permute-start.14
  51.8 0.0 copy-done.3
  51.8 3.4 %shard_map.110 = (f32[8,128,128]{2,1,0:T(8,128)S(1)}, f32[8,128,128]{2,1,0:T(8,128)S(1)}, f32[8,128,128]{2,1,0:T(8,128)S(1)}) custom-call(s32[3]{0:T(128)} %refs_0_.5, bf16[8,128,256]{2,1,0:T(8,128)(2,1)S(1)} %shard_map.107.refs_1_, s32[5,384]{1,0:T(8,128)S(1)} %copy-done.3, bf16[1024,512]{1,0:T(8,128)(2,1)S(1)} %get-tuple-element.27.ready_ref.refs_3_, ...), custom_call_target="tpu_custom_call" | custom-call | tf_op jit(solution)/shard_map/pallas_call | solution.py:299
  55.2 0.0 collective-permute-done.14.refs_5_
  55.2 0.0 copy-done.2
  55.2 4.1 %shard_map.111 = bf16[128,1024]{1,0:T(8,128)(2,1)} custom-call(s32[3]{0:T(128)} %refs_0_.5, bf16[8,128,256]{2,1,0:T(8,128)(2,1)S(1)} %shard_map.107.refs_1_, s32[5,384]{1,0:T(8,128)S(1)} %copy-done.2, bf16[1024,512]{1,0:T(8,128)(2,1)S(1)} %get-tuple-element.27.ready_ref.refs_3_, bf16[512,1024]{1,0:T(8,128)(2,1)S(1)} %get-tuple-element.33.refs_4_, ...), custom_call_target="tpu_custom_call" | custom-call | tf_op jit(solution)/shard_map/pallas_call | solution.py:299
  (4 shorter events, 0.1 us)
Async XLA Ops:
  0.9 5.7 %collective-permute-start = (bf16[16,2112]{1,0:T(8,128)(2,1)S(1)}, bf16[16,2112]{1,0:T(8,128)(2,1)S(1)}, u32[]{:S(2)}, u32[]{:S(2)}) collective-permute-start(bf16[16,2112]{1,0:T(8,128)(2,1)S(1)} %shard_map.100.own_ref), channel_id=1, source_target_pairs={{0,1},{1,0},{2,3},{3,2},{4,5},{5,4},{6,7},{7,6},{8,9},{9,8},{10,11... | collective-permute-start | bytes 202760 | tf_op jit(solution)/shard_map/ppermute | solution.py:349
  4.6 1.6 %copy-start = (bf16[512,2048]{1,0:T(8,128)(2,1)S(1)}, bf16[512,2048]{1,0:T(8,128)(2,1)}, u32[]{:S(2)}) copy-start(bf16[512,2048]{1,0:T(8,128)(2,1)} %w_ref) | copy-start | bytes 6291460
  6.8 4.3 %collective-permute-start.1 = (bf16[16,1152]{1,0:T(8,128)(2,1)S(1)}, bf16[16,1152]{1,0:T(8,128)(2,1)S(1)}, u32[]{:S(2)}, u32[]{:S(2)}) collective-permute-start(bf16[16,1152]{1,0:T(8,128)(2,1)S(1)} %get-tuple-element.28.refs_0_), channel_id=1, source_target_pairs={{0,4},{1,5},{2,6},{3,7},{4,0},{5,1},{6,2},{7,3},{8,12},{9,13},{10,... | collective-permute-start | bytes 110600 | tf_op jit(solution)/shard_map/ppermute | solution.py:371
  9.7 15.3 %collective-permute-start.5 = (bf16[16,3072]{1,0:T(8,128)(2,1)S(1)}, bf16[16,3072]{1,0:T(8,128)(2,1)S(1)}, u32[]{:S(2)}, u32[]{:S(2)}) collective-permute-start(bf16[16,3072]{1,0:T(8,128)(2,1)S(1)} %get-tuple-element.31.refs_0_), channel_id=1, source_target_pairs={{0,4},{1,5},{2,6},{3,7},{4,0},{5,1},{6,2},{7,3},{8,12},{9,13},{10,... | collective-permute-start | bytes 294920 | tf_op jit(solution)/shard_map/ppermute | solution.py:382
  11.1 12.7 %collective-permute-start.4 = (bf16[32,1152]{1,0:T(8,128)(2,1)S(1)}, bf16[32,1152]{1,0:T(8,128)(2,1)S(1)}, u32[]{:S(2)}, u32[]{:S(2)}) collective-permute-start(bf16[32,1152]{1,0:T(8,128)(2,1)S(1)} %shard_map.103), channel_id=1, source_target_pairs={{0,64},{8,72},{16,80},{24,88},{32,96},{40,104},{48,112},{56,120},{... | collective-permute-start | bytes 221192 | tf_op jit(solution)/shard_map/ppermute | solution.py:383
  18.0 6.9 %collective-permute-start.3 = (bf16[32,1152]{1,0:T(8,128)(2,1)S(1)}, bf16[32,1152]{1,0:T(8,128)(2,1)S(1)}, u32[]{:S(2)}, u32[]{:S(2)}) collective-permute-start(bf16[32,1152]{1,0:T(8,128)(2,1)S(1)} %shard_map.103), channel_id=1, source_target_pairs={{0,16},{8,24},{16,32},{24,40},{32,48},{40,56},{48,64},{56,72},{64,... | collective-permute-start | bytes 221192 | tf_op jit(solution)/shard_map/ppermute | solution.py:383
  18.8 6.2 %collective-permute-start.2 = (bf16[32,1152]{1,0:T(8,128)(2,1)S(1)}, bf16[32,1152]{1,0:T(8,128)(2,1)S(1)}, u32[]{:S(2)}, u32[]{:S(2)}) collective-permute-start(bf16[32,1152]{1,0:T(8,128)(2,1)S(1)} %shard_map.103), channel_id=1, source_target_pairs={{0,112},{8,120},{16,128},{24,136},{32,144},{40,152},{48,160},{56,1... | collective-permute-start | bytes 221192 | tf_op jit(solution)/shard_map/ppermute | solution.py:383
  25.0 19.4 %copy-start.1 = (s32[5,1536]{1,0:T(8,128)S(1)}, s32[5,1536]{1,0:T(8,128)}, u32[]{:S(2)}) copy-start(s32[5,1536]{1,0:T(8,128)} %constant.6.clone.refs_2_) | copy-start | bytes 92164
  25.0 6.8 %collective-permute-start.8 = (bf16[96,1152]{1,0:T(8,128)(2,1)S(1)}, bf16[96,1152]{1,0:T(8,128)(2,1)S(1)}, u32[]{:S(2)}, u32[]{:S(2)}) collective-permute-start(bf16[96,1152]{1,0:T(8,128)(2,1)S(1)} %shard_map.105.refs_2_.refs_5_), channel_id=1, source_target_pairs={{0,240},{8,248},{16,0},{24,8},{32,16},{40,24},{48,32},{56,40},{64,... | collective-permute-start | bytes 663560 | tf_op jit(solution)/shard_map/ppermute | solution.py:389
  26.2 6.9 %collective-permute-start.7 = (bf16[96,1152]{1,0:T(8,128)(2,1)S(1)}, bf16[96,1152]{1,0:T(8,128)(2,1)S(1)}, u32[]{:S(2)}, u32[]{:S(2)}) collective-permute-start(bf16[96,1152]{1,0:T(8,128)(2,1)S(1)} %shard_map.105.refs_2_.refs_5_), channel_id=1, source_target_pairs={{0,16},{8,24},{16,32},{24,40},{32,48},{40,56},{48,64},{56,72},{64,... | collective-permute-start | bytes 663560 | tf_op jit(solution)/shard_map/ppermute | solution.py:388
  26.6 5.3 %collective-permute-start.6 = (bf16[32,3072]{1,0:T(8,128)(2,1)S(1)}, bf16[32,3072]{1,0:T(8,128)(2,1)S(1)}, u32[]{:S(2)}, u32[]{:S(2)}) collective-permute-start(bf16[32,3072]{1,0:T(8,128)(2,1)S(1)} %shard_map.106.own), channel_id=1, source_target_pairs={{0,2},{1,3},{2,4},{3,5},{4,6},{5,7},{6,0},{7,1},{8,14},{9,15},{10,... | collective-permute-start | bytes 589832 | tf_op jit(solution)/shard_map/ppermute | solution.py:390
  29.2 12.6 %collective-permute-start.12 = (bf16[96,1152]{1,0:T(8,128)(2,1)S(1)}, bf16[96,1152]{1,0:T(8,128)(2,1)S(1)}, u32[]{:S(2)}, u32[]{:S(2)}) collective-permute-start(bf16[96,1152]{1,0:T(8,128)(2,1)S(1)} %shard_map.105.refs_2_.refs_5_), channel_id=1, source_target_pairs={{0,2},{1,3},{2,4},{3,5},{4,6},{5,7},{6,0},{7,1},{8,14},{9,15},{10,... | collective-permute-start | bytes 663560 | tf_op jit(solution)/shard_map/ppermute | solution.py:391
  33.1 18.7 %copy-start.3 = (s32[5,384]{1,0:T(8,128)S(1)}, s32[5,384]{1,0:T(8,128)}, u32[]{:S(2)}) copy-start(s32[5,384]{1,0:T(8,128)} %constant.7.clone.refs_2_) | copy-start | bytes 23044
  33.1 11.3 %collective-permute-start.11 = (bf16[192,1152]{1,0:T(8,128)(2,1)S(1)}, bf16[192,1152]{1,0:T(8,128)(2,1)S(1)}, u32[]{:S(2)}, u32[]{:S(2)}) collective-permute-start(bf16[192,1152]{1,0:T(8,128)(2,1)S(1)} %shard_map.108.refs_6_), channel_id=1, source_target_pairs={{0,8},{8,0},{16,24},{24,16},{32,40},{40,32},{48,56},{56,48},{64,72... | collective-permute-start | bytes 1327112 | tf_op jit(solution)/shard_map/ppermute | solution.py:405
  39.1 12.3 %collective-permute-start.9 = (bf16[192,1152]{1,0:T(8,128)(2,1)S(1)}, bf16[192,1152]{1,0:T(8,128)(2,1)S(1)}, u32[]{:S(2)}, u32[]{:S(2)}) collective-permute-start(bf16[192,1152]{1,0:T(8,128)(2,1)S(1)} %shard_map.108.refs_6_), channel_id=1, source_target_pairs={{0,2},{1,3},{2,4},{3,5},{4,6},{5,7},{6,0},{7,1},{8,14},{9,15},{10,... | collective-permute-start | bytes 1327112 | tf_op jit(solution)/shard_map/ppermute | solution.py:404
  41.9 2.5 %collective-permute-start.10 = (bf16[96,1152]{1,0:T(8,128)(2,1)S(1)}, bf16[96,1152]{1,0:T(8,128)(2,1)S(1)}, u32[]{:S(2)}, u32[]{:S(2)}) collective-permute-start(bf16[96,1152]{1,0:T(8,128)(2,1)S(1)} %shard_map.105.refs_2_.refs_5_), channel_id=1, source_target_pairs={{0,8},{8,0},{16,24},{24,16},{32,40},{40,32},{48,56},{56,48},{64,72... | collective-permute-start | bytes 663560 | tf_op jit(solution)/shard_map/ppermute | solution.py:392
  41.9 2.5 %collective-permute-start.13 = (bf16[96,1152]{1,0:T(8,128)(2,1)S(1)}, bf16[96,1152]{1,0:T(8,128)(2,1)S(1)}, u32[]{:S(2)}, u32[]{:S(2)}) collective-permute-start(bf16[96,1152]{1,0:T(8,128)(2,1)S(1)} %collective-permute-done.12.refs_9_), channel_id=1, source_target_pairs={{0,8},{8,0},{16,24},{24,16},{32,40},{40,32},{48,56},{56,48},{64,72... | collective-permute-start | bytes 663560 | tf_op jit(solution)/shard_map/ppermute | solution.py:406
  44.3 10.9 %copy-start.2 = (s32[5,384]{1,0:T(8,128)S(1)}, s32[5,384]{1,0:T(8,128)}, u32[]{:S(2)}) copy-start(s32[5,384]{1,0:T(8,128)} %constant.8.clone.refs_2_) | copy-start | bytes 23044
  51.5 3.8 %collective-permute-start.14 = (bf16[192,1152]{1,0:T(8,128)(2,1)S(1)}, bf16[192,1152]{1,0:T(8,128)(2,1)S(1)}, u32[]{:S(2)}, u32[]{:S(2)}) collective-permute-start(bf16[192,1152]{1,0:T(8,128)(2,1)S(1)} %collective-permute-done.9.refs_5_), channel_id=1, source_target_pairs={{0,8},{8,0},{16,24},{24,16},{32,40},{40,32},{48,56},{56,48},{64,72... | collective-permute-start | bytes 1327112 | tf_op jit(solution)/shard_map/ppermute | solution.py:418

commit v9 on v6

--- a/solution.py
+++ b/solution.py
@@ -227,18 +227,24 @@
 
     def weigh(head):
         scores = score_ref[head]
-        top = jnp.max(scores, axis=1, keepdims=True)
-        old_max = FLOOR if first else max_in[head][:, :1]
+        top = jnp.broadcast_to(jnp.max(scores, axis=1, keepdims=True), (tok_dev, LANES))
+        old_max = FLOOR if first else max_in[head]
         new_max = jnp.maximum(top, old_max)
-        weights = jnp.exp2(scores - new_max)
-        total = jnp.sum(weights, axis=1, keepdims=True)
+        weights = jnp.exp2(scores - jnp.concatenate([new_max] * (n_keys // LANES), axis=1))
+        total = jnp.broadcast_to(jnp.sum(weights, axis=1, keepdims=True), (tok_dev, LANES))
         weight_ref[head] = weights.astype(jnp.bfloat16)
+        if not last:
+            max_out[head] = new_max
         if first:
-            return new_max, total, None
+            sum_out[head] = total
+            return total, None
         faded = jnp.exp2(old_max - new_max)
-        return new_max, total + faded * sum_in[head][:, :1], faded
-
-    def mix(head, new_max, total, faded):
+        total = total + faded * sum_in[head]
+        if not last:
+            sum_out[head] = total
+        return total, faded
+
+    def mix(head, total, faded):
         values = value_ref[:, head * VD : (head + 1) * VD]
         mixed = jnp.dot(weight_ref[head], values, preferred_element_type=jnp.float32)
         if not first:
@@ -246,8 +252,6 @@
         if last:
             out_ref[:, head * VD : (head + 1) * VD] = (mixed * (1.0 / total)).astype(jnp.bfloat16)
         else:
-            max_out[head] = jnp.broadcast_to(new_max, mixed.shape)
-            sum_out[head] = jnp.broadcast_to(total, mixed.shape)
             acc_out[head] = mixed
 
     groups = [range(low, low + group) for low in range(0, heads, group)]
@@ -432,8 +436,8 @@
     state = attend_to(pieces, views, 2, None)
     received, state = lax.optimization_barrier((received, state))
     swapped = lax.ppermute(received, "ctx", swap)
-    state = attend_to([received], [(0, 0, 0, 1, near_slots)], 1, state)
-    return attend_to([swapped], [(0, 0, 1, 1, near_slots)], 1, state, last=True)
+    state = attend_to([received], [(0, 0, 0, 1, near_slots)], 2, state)
+    return attend_to([swapped], [(0, 0, 1, 1, near_slots)], 2, state, last=True)
 
 
 def solution(mesh):

time: 58.4 us -> 56.8 us (0.973)
  Pallas kernels: 20.3 us -> 18.9 us
    pallas_call x3, Pallas kernels: 14.4 us -> 13 us  [attend(): pl.pallas_call(kernel, in_specs=[pl.BlockSpec(memory_space=pltpu.SMEM)] +...]
  transfers between devices with their start and end apart: 13 -> 13, of which waited for: 3 -> 3; matrix products, arithmetic and copies ran while one was open for 0% -> 0% of each run, Pallas kernels for 26% -> 25%
where the time goes in v9:
time: 56.8 us; the launch traced here: 56.5 us
  starting transfers between devices  28.9 us (51%)
  Pallas kernels  18.9 us (33%)
  waiting for transfers between devices  7.06 us (12%)
  local copies, waits for them, and re-layouts  1.61 us (3%)
    pallas_call x3, Pallas kernels, attend(): pl.pallas_call(kernel, in_specs=[pl.BlockSpec(memory_space=pltpu.SMEM)] +...  13 us
    ppermute x3, starting transfers between devices, body(): coarse = [lax.ppermute(piece, 'ctx', chip_shift(step)) for step in COARSE]  10.4 us
    ppermute x1, starting transfers between devices, body(): other = lax.ppermute(rows, 'head', across_x)  3.66 us
    ppermute x3, waiting for transfers between devices, body(): coarse = [lax.ppermute(piece, 'ctx', chip_shift(step)) for step in COARSE]  3.62 us
    ppermute x1, starting transfers between devices, body(): sooner = lax.ppermute(coarse, 'ctx', chip_shift(-1))  3.57 us
    ppermute x1, starting transfers between devices, body(): near_swapped = lax.ppermute(near, 'ctx', swap)  3.37 us
    ppermute x1, waiting for transfers between devices, body(): later = lax.ppermute(coarse, 'ctx', chip_shift(1))  3.32 us
    ppermute x1, starting transfers between devices, body(): opposite = lax.ppermute(both, 'head', across_y)  2.95 us
  transfers between devices with their start and end apart: 13, of which 3 were waited for; matrix products, arithmetic and copies ran while one was open for 0% of the time, Pallas kernels for 25%

profile of v9, /device:TPU:1, one launch (start us, length us, event | category | flops | bytes accessed | tf_op | source)
XLA Modules:
  0.0 56.5 jit_solution(5707071695849506165)
XLA Ops:
  0.0 0.9 %shard_map.100.own_ref = bf16[16,2112]{1,0:T(8,128)(2,1)S(1)} custom-call(bf16[16,1536]{1,0:T(8,128)(2,1)} %q_ref.1, f32[1536]{0:T(1024)} %q_gain_ref.1, bf16[16,576]{1,0:T(8,128)(2,1)} %kv_ref.1, f32[512]{0:T(512)} %kv_gain_ref.1), custom_call_target="tpu_custom_call" | custom-call | tf_op jit(solution)/shard_map/pallas_call | solution.py:350
  0.9 3.7 %collective-permute-start = (bf16[16,2112]{1,0:T(8,128)(2,1)S(1)}, bf16[16,2112]{1,0:T(8,128)(2,1)S(1)}, u32[]{:S(2)}, u32[]{:S(2)}) collective-permute-start(bf16[16,2112]{1,0:T(8,128)(2,1)S(1)} %shard_map.100.own_ref), channel_id=1, source_target_pairs={{0,1},{1,0},{2,3},{3,2},{4,5},{5,4},{6,7},{7,6},{8,9},{9,8},{10,11... | collective-permute-start | bytes 202760 | tf_op jit(solution)/shard_map/ppermute | solution.py:355
  4.6 0.0 copy-start
  4.6 1.6 %copy-done = bf16[512,2048]{1,0:T(8,128)(2,1)S(1)} copy-done((bf16[512,2048]{1,0:T(8,128)(2,1)S(1)}, bf16[512,2048]{1,0:T(8,128)(2,1)}, u32[]{:S(2)}) %copy-start) | copy-done | bytes 2097176
  6.2 0.5 shard_map.101
  6.7 0.0 collective-permute-done.other_ref
  6.7 0.1 shard_map.102.own_ref
  6.7 2.9 %collective-permute-start.1 = (bf16[16,4224]{1,0:T(8,128)(2,1)S(1)}, bf16[16,4224]{1,0:T(8,128)(2,1)S(1)}, u32[]{:S(2)}, u32[]{:S(2)}) collective-permute-start(bf16[16,4224]{1,0:T(8,128)(2,1)S(1)} %shard_map.102.own_ref), channel_id=1, source_target_pairs={{0,4},{1,5},{2,6},{3,7},{4,0},{5,1},{6,2},{7,3},{8,12},{9,13},{10,... | collective-permute-start | bytes 405512 | tf_op jit(solution)/shard_map/ppermute | solution.py:374
  9.7 2.3 %shard_map.103.ready_ref.refs_3_ = bf16[1536,1536]{1,0:T(8,128)(2,1)S(1)} custom-call(bf16[1536,1536]{1,0:T(8,128)(2,1)} %from_ref), custom_call_target="tpu_custom_call" | custom-call | tf_op jit(solution)/shard_map/pallas_call | solution.py:376
  12.0 0.1 collective-permute-done.1.got_ref
  12.2 0.0 copy-start.1
  12.2 7.0 %collective-permute-start.2 = (bf16[32,1152]{1,0:T(8,128)(2,1)S(1)}, bf16[32,1152]{1,0:T(8,128)(2,1)S(1)}, u32[]{:S(2)}, u32[]{:S(2)}) collective-permute-start(bf16[32,1152]{1,0:T(8,128)(2,1)S(1)} %get-tuple-element.31), channel_id=1, source_target_pairs={{0,64},{8,72},{16,80},{24,88},{32,96},{40,104},{48,112},{56,120},{... | collective-permute-start | bytes 221192 | tf_op jit(solution)/shard_map/ppermute | solution.py:394
  19.2 0.7 %collective-permute-start.3 = (bf16[32,1152]{1,0:T(8,128)(2,1)S(1)}, bf16[32,1152]{1,0:T(8,128)(2,1)S(1)}, u32[]{:S(2)}, u32[]{:S(2)}) collective-permute-start(bf16[32,1152]{1,0:T(8,128)(2,1)S(1)} %get-tuple-element.31), channel_id=1, source_target_pairs={{0,16},{8,24},{16,32},{24,40},{32,48},{40,56},{48,64},{56,72},{64,... | collective-permute-start | bytes 221192 | tf_op jit(solution)/shard_map/ppermute | solution.py:394
  19.9 2.7 %collective-permute-start.4 = (bf16[32,1152]{1,0:T(8,128)(2,1)S(1)}, bf16[32,1152]{1,0:T(8,128)(2,1)S(1)}, u32[]{:S(2)}, u32[]{:S(2)}) collective-permute-start(bf16[32,1152]{1,0:T(8,128)(2,1)S(1)} %get-tuple-element.31), channel_id=1, source_target_pairs={{0,112},{8,120},{16,128},{24,136},{32,144},{40,152},{48,160},{56,1... | collective-permute-start | bytes 221192 | tf_op jit(solution)/shard_map/ppermute | solution.py:394
  22.6 0.0 collective-permute-done.2.refs_0_
  22.6 3.6 %collective-permute-done.3.refs_1_ = bf16[32,1152]{1,0:T(8,128)(2,1)S(1)} collective-permute-done((bf16[32,1152]{1,0:T(8,128)(2,1)S(1)}, bf16[32,1152]{1,0:T(8,128)(2,1)S(1)}, u32[]{:S(2)}, u32[]{:S(2)}) %collective-permute-start.3) | collective-permute-done | bytes 73760 | tf_op jit(solution)/shard_map/ppermute | solution.py:394
  26.2 0.0 collective-permute-done.4.refs_2_
  26.3 2.6 %collective-permute-start.5 = (bf16[32,6528]{1,0:T(8,128)(2,1)S(1)}, bf16[32,6528]{1,0:T(8,128)(2,1)S(1)}, u32[]{:S(2)}, u32[]{:S(2)}) collective-permute-start(bf16[32,6528]{1,0:T(8,128)(2,1)S(1)} %get-tuple-element.32), channel_id=1, source_target_pairs={{0,2},{1,3},{2,4},{3,5},{4,6},{5,7},{6,0},{7,1},{8,14},{9,15},{10,... | collective-permute-start | bytes 1253384 | tf_op jit(solution)/shard_map/ppermute | solution.py:409
  28.9 0.0 collective-permute-start.6
  28.9 3.6 %collective-permute-start.7 = (bf16[96,1152]{1,0:T(8,128)(2,1)S(1)}, bf16[96,1152]{1,0:T(8,128)(2,1)S(1)}, u32[]{:S(2)}, u32[]{:S(2)}) collective-permute-start(bf16[96,1152]{1,0:T(8,128)(2,1)S(1)} %get-tuple-element.34.refs_5_), channel_id=1, source_target_pairs={{0,240},{8,248},{16,0},{24,8},{32,16},{40,24},{48,32},{56,40},{64,... | collective-permute-start | bytes 663560 | tf_op jit(solution)/shard_map/ppermute | solution.py:408
  32.5 3.3 %collective-permute-done.6.refs_0_ = bf16[96,1152]{1,0:T(8,128)(2,1)S(1)} collective-permute-done((bf16[96,1152]{1,0:T(8,128)(2,1)S(1)}, bf16[96,1152]{1,0:T(8,128)(2,1)S(1)}, u32[]{:S(2)}, u32[]{:S(2)}) %collective-permute-start.6) | collective-permute-done | bytes 221216 | tf_op jit(solution)/shard_map/ppermute | solution.py:407
  35.8 0.0 collective-permute-done.7.refs_1_
  35.8 0.0 copy-start.3
  35.8 3.4 %collective-permute-start.10 = (bf16[192,1152]{1,0:T(8,128)(2,1)S(1)}, bf16[192,1152]{1,0:T(8,128)(2,1)S(1)}, u32[]{:S(2)}, u32[]{:S(2)}) collective-permute-start(bf16[192,1152]{1,0:T(8,128)(2,1)S(1)} %shard_map.107.refs_6_), channel_id=1, source_target_pairs={{0,8},{8,0},{16,24},{24,16},{32,40},{40,32},{48,56},{56,48},{64,72... | collective-permute-start | bytes 1327112 | tf_op jit(solution)/shard_map/ppermute | solution.py:414
  39.2 1.4 %collective-permute-start.8 = (bf16[192,1152]{1,0:T(8,128)(2,1)S(1)}, bf16[192,1152]{1,0:T(8,128)(2,1)S(1)}, u32[]{:S(2)}, u32[]{:S(2)}) collective-permute-start(bf16[192,1152]{1,0:T(8,128)(2,1)S(1)} %shard_map.107.refs_6_), channel_id=1, source_target_pairs={{0,2},{1,3},{2,4},{3,5},{4,6},{5,7},{6,0},{7,1},{8,14},{9,15},{10,... | collective-permute-start | bytes 1327112 | tf_op jit(solution)/shard_map/ppermute | solution.py:413
  40.6 0.0 collective-permute-done.5.refs_2_.refs_9_
  40.6 0.3 collective-permute-start.11
  40.9 0.2 collective-permute-start.9
  41.1 1.9 %shard_map.106.refs_1_ = bf16[8,128,256]{2,1,0:T(8,128)(2,1)S(1)} custom-call(s32[3]{0:T(128)} %refs_0_.7, bf16[32,3072]{1,0:T(8,128)(2,1)S(1)} %get-tuple-element.30.refs_3_.refs_1_, bf16[32,6528]{1,0:T(8,128)(2,1)S(1)} %collective-permute-done.5.refs_2_.refs_9_, bf16[1536,1536]{1,0:T(8,128)(2,1)S(1)} %shard_map.103.ready_ref.refs_3_), custom_call_target="tpu_custom_call" | custom-call | tf_op jit(solution)/shard_map/pallas_call | solution.py:417
  43.1 0.0 collective-permute-done.9.refs_7_
  43.1 0.0 collective-permute-done.10.refs_8_
  43.1 0.0 collective-permute-done.11.refs_10_
  43.1 0.0 copy-done.1
  43.1 0.0 copy-start.2
  43.1 7.0 %shard_map.108 = (f32[8,128,128]{2,1,0:T(8,128)S(1)}, f32[8,128,128]{2,1,0:T(8,128)S(1)}, f32[8,128,128]{2,1,0:T(8,128)S(1)}) custom-call(s32[3]{0:T(128)} %refs_0_.7, bf16[8,128,256]{2,1,0:T(8,128)(2,1)S(1)} %shard_map.106.refs_1_, s32[5,1536]{1,0:T(8,128)S(1)} %copy-done.1, bf16[1024,512]{1,0:T(8,128)(2,1)S(1)} %get-tuple-element.27.ready_ref.refs_3_, ...), custom_call_target="tpu_custom_call" | custom-call | tf_op jit(solution)/shard_map/pallas_call | solution.py:306
  50.1 0.0 collective-permute-done.8.refs_5_
  50.1 0.4 collective-permute-start.12
  50.5 0.0 copy-done.3
  50.5 2.6 %shard_map.109 = (f32[8,128,128]{2,1,0:T(8,128)S(1)}, f32[8,128,128]{2,1,0:T(8,128)S(1)}, f32[8,128,128]{2,1,0:T(8,128)S(1)}) custom-call(s32[3]{0:T(128)} %refs_0_.7, bf16[8,128,256]{2,1,0:T(8,128)(2,1)S(1)} %shard_map.106.refs_1_, s32[5,384]{1,0:T(8,128)S(1)} %copy-done.3, bf16[1024,512]{1,0:T(8,128)(2,1)S(1)} %get-tuple-element.27.ready_ref.refs_3_, ...), custom_call_target="tpu_custom_call" | custom-call | tf_op jit(solution)/shard_map/pallas_call | solution.py:306
  53.1 0.0 collective-permute-done.12.refs_5_
  53.1 0.0 copy-done.2
  53.1 3.4 %shard_map.110 = bf16[128,1024]{1,0:T(8,128)(2,1)} custom-call(s32[3]{0:T(128)} %refs_0_.7, bf16[8,128,256]{2,1,0:T(8,128)(2,1)S(1)} %shard_map.106.refs_1_, s32[5,384]{1,0:T(8,128)S(1)} %copy-done.2, bf16[1024,512]{1,0:T(8,128)(2,1)S(1)} %get-tuple-element.27.ready_ref.refs_3_, bf16[512,1024]{1,0:T(8,128)(2,1)S(1)} %get-tuple-element.33.refs_4_, ...), custom_call_target="tpu_custom_call" | custom-call | tf_op jit(solution)/shard_map/pallas_call | solution.py:306
  (3 shorter events, 0.1 us)
Async XLA Ops:
  0.9 5.7 %collective-permute-start = (bf16[16,2112]{1,0:T(8,128)(2,1)S(1)}, bf16[16,2112]{1,0:T(8,128)(2,1)S(1)}, u32[]{:S(2)}, u32[]{:S(2)}) collective-permute-start(bf16[16,2112]{1,0:T(8,128)(2,1)S(1)} %shard_map.100.own_ref), channel_id=1, source_target_pairs={{0,1},{1,0},{2,3},{3,2},{4,5},{5,4},{6,7},{7,6},{8,9},{9,8},{10,11... | collective-permute-start | bytes 202760 | tf_op jit(solution)/shard_map/ppermute | solution.py:355
  4.6 1.6 %copy-start = (bf16[512,2048]{1,0:T(8,128)(2,1)S(1)}, bf16[512,2048]{1,0:T(8,128)(2,1)}, u32[]{:S(2)}) copy-start(bf16[512,2048]{1,0:T(8,128)(2,1)} %w_ref) | copy-start | bytes 6291460
  6.7 5.4 %collective-permute-start.1 = (bf16[16,4224]{1,0:T(8,128)(2,1)S(1)}, bf16[16,4224]{1,0:T(8,128)(2,1)S(1)}, u32[]{:S(2)}, u32[]{:S(2)}) collective-permute-start(bf16[16,4224]{1,0:T(8,128)(2,1)S(1)} %shard_map.102.own_ref), channel_id=1, source_target_pairs={{0,4},{1,5},{2,6},{3,7},{4,0},{5,1},{6,2},{7,3},{8,12},{9,13},{10,... | collective-permute-start | bytes 405512 | tf_op jit(solution)/shard_map/ppermute | solution.py:374
  12.2 30.9 %copy-start.1 = (s32[5,1536]{1,0:T(8,128)S(1)}, s32[5,1536]{1,0:T(8,128)}, u32[]{:S(2)}) copy-start(s32[5,1536]{1,0:T(8,128)} %constant.6.clone.refs_2_) | copy-start | bytes 92164
  12.2 10.4 %collective-permute-start.2 = (bf16[32,1152]{1,0:T(8,128)(2,1)S(1)}, bf16[32,1152]{1,0:T(8,128)(2,1)S(1)}, u32[]{:S(2)}, u32[]{:S(2)}) collective-permute-start(bf16[32,1152]{1,0:T(8,128)(2,1)S(1)} %get-tuple-element.31), channel_id=1, source_target_pairs={{0,64},{8,72},{16,80},{24,88},{32,96},{40,104},{48,112},{56,120},{... | collective-permute-start | bytes 221192 | tf_op jit(solution)/shard_map/ppermute | solution.py:394
  19.2 7.1 %collective-permute-start.3 = (bf16[32,1152]{1,0:T(8,128)(2,1)S(1)}, bf16[32,1152]{1,0:T(8,128)(2,1)S(1)}, u32[]{:S(2)}, u32[]{:S(2)}) collective-permute-start(bf16[32,1152]{1,0:T(8,128)(2,1)S(1)} %get-tuple-element.31), channel_id=1, source_target_pairs={{0,16},{8,24},{16,32},{24,40},{32,48},{40,56},{48,64},{56,72},{64,... | collective-permute-start | bytes 221192 | tf_op jit(solution)/shard_map/ppermute | solution.py:394
  19.9 6.3 %collective-permute-start.4 = (bf16[32,1152]{1,0:T(8,128)(2,1)S(1)}, bf16[32,1152]{1,0:T(8,128)(2,1)S(1)}, u32[]{:S(2)}, u32[]{:S(2)}) collective-permute-start(bf16[32,1152]{1,0:T(8,128)(2,1)S(1)} %get-tuple-element.31), channel_id=1, source_target_pairs={{0,112},{8,120},{16,128},{24,136},{32,144},{40,152},{48,160},{56,1... | collective-permute-start | bytes 221192 | tf_op jit(solution)/shard_map/ppermute | solution.py:394
  26.3 14.3 %collective-permute-start.5 = (bf16[32,6528]{1,0:T(8,128)(2,1)S(1)}, bf16[32,6528]{1,0:T(8,128)(2,1)S(1)}, u32[]{:S(2)}, u32[]{:S(2)}) collective-permute-start(bf16[32,6528]{1,0:T(8,128)(2,1)S(1)} %get-tuple-element.32), channel_id=1, source_target_pairs={{0,2},{1,3},{2,4},{3,5},{4,6},{5,7},{6,0},{7,1},{8,14},{9,15},{10,... | collective-permute-start | bytes 1253384 | tf_op jit(solution)/shard_map/ppermute | solution.py:409
  28.9 6.9 %collective-permute-start.6 = (bf16[96,1152]{1,0:T(8,128)(2,1)S(1)}, bf16[96,1152]{1,0:T(8,128)(2,1)S(1)}, u32[]{:S(2)}, u32[]{:S(2)}) collective-permute-start(bf16[96,1152]{1,0:T(8,128)(2,1)S(1)} %get-tuple-element.34.refs_5_), channel_id=1, source_target_pairs={{0,16},{8,24},{16,32},{24,40},{32,48},{40,56},{48,64},{56,72},{64,... | collective-permute-start | bytes 663560 | tf_op jit(solution)/shard_map/ppermute | solution.py:407
  28.9 6.9 %collective-permute-start.7 = (bf16[96,1152]{1,0:T(8,128)(2,1)S(1)}, bf16[96,1152]{1,0:T(8,128)(2,1)S(1)}, u32[]{:S(2)}, u32[]{:S(2)}) collective-permute-start(bf16[96,1152]{1,0:T(8,128)(2,1)S(1)} %get-tuple-element.34.refs_5_), channel_id=1, source_target_pairs={{0,240},{8,248},{16,0},{24,8},{32,16},{40,24},{48,32},{56,40},{64,... | collective-permute-start | bytes 663560 | tf_op jit(solution)/shard_map/ppermute | solution.py:408
  35.8 14.7 %copy-start.3 = (s32[5,384]{1,0:T(8,128)S(1)}, s32[5,384]{1,0:T(8,128)}, u32[]{:S(2)}) copy-start(s32[5,384]{1,0:T(8,128)} %constant.7.clone.refs_2_) | copy-start | bytes 23044
  35.8 7.2 %collective-permute-start.10 = (bf16[192,1152]{1,0:T(8,128)(2,1)S(1)}, bf16[192,1152]{1,0:T(8,128)(2,1)S(1)}, u32[]{:S(2)}, u32[]{:S(2)}) collective-permute-start(bf16[192,1152]{1,0:T(8,128)(2,1)S(1)} %shard_map.107.refs_6_), channel_id=1, source_target_pairs={{0,8},{8,0},{16,24},{24,16},{32,40},{40,32},{48,56},{56,48},{64,72... | collective-permute-start | bytes 1327112 | tf_op jit(solution)/shard_map/ppermute | solution.py:414
  39.2 10.9 %collective-permute-start.8 = (bf16[192,1152]{1,0:T(8,128)(2,1)S(1)}, bf16[192,1152]{1,0:T(8,128)(2,1)S(1)}, u32[]{:S(2)}, u32[]{:S(2)}) collective-permute-start(bf16[192,1152]{1,0:T(8,128)(2,1)S(1)} %shard_map.107.refs_6_), channel_id=1, source_target_pairs={{0,2},{1,3},{2,4},{3,5},{4,6},{5,7},{6,0},{7,1},{8,14},{9,15},{10,... | collective-permute-start | bytes 1327112 | tf_op jit(solution)/shard_map/ppermute | solution.py:413
  40.6 2.5 %collective-permute-start.11 = (bf16[32,6528]{1,0:T(8,128)(2,1)S(1)}, bf16[32,6528]{1,0:T(8,128)(2,1)S(1)}, u32[]{:S(2)}, u32[]{:S(2)}) collective-permute-start(bf16[32,6528]{1,0:T(8,128)(2,1)S(1)} %collective-permute-done.5.refs_2_.refs_9_), channel_id=1, source_target_pairs={{0,8},{8,0},{16,24},{24,16},{32,40},{40,32},{48,56},{56,48},{64,72... | collective-permute-start | bytes 1253384 | tf_op jit(solution)/shard_map/ppermute | solution.py:415
  40.9 2.2 %collective-permute-start.9 = (bf16[96,1152]{1,0:T(8,128)(2,1)S(1)}, bf16[96,1152]{1,0:T(8,128)(2,1)S(1)}, u32[]{:S(2)}, u32[]{:S(2)}) collective-permute-start(bf16[96,1152]{1,0:T(8,128)(2,1)S(1)} %get-tuple-element.34.refs_5_), channel_id=1, source_target_pairs={{0,8},{8,0},{16,24},{24,16},{32,40},{40,32},{48,56},{56,48},{64,72... | collective-permute-start | bytes 663560 | tf_op jit(solution)/shard_map/ppermute | solution.py:410
  43.1 10.0 %copy-start.2 = (s32[5,384]{1,0:T(8,128)S(1)}, s32[5,384]{1,0:T(8,128)}, u32[]{:S(2)}) copy-start(s32[5,384]{1,0:T(8,128)} %constant.8.clone.refs_2_) | copy-start | bytes 23044
  50.1 3.0 %collective-permute-start.12 = (bf16[192,1152]{1,0:T(8,128)(2,1)S(1)}, bf16[192,1152]{1,0:T(8,128)(2,1)S(1)}, u32[]{:S(2)}, u32[]{:S(2)}) collective-permute-start(bf16[192,1152]{1,0:T(8,128)(2,1)S(1)} %collective-permute-done.8.refs_5_), channel_id=1, source_target_pairs={{0,8},{8,0},{16,24},{24,16},{32,40},{40,32},{48,56},{56,48},{64,72... | collective-permute-start | bytes 1327112 | tf_op jit(solution)/shard_map/ppermute | solution.py:438

commit v10 on v7

--- a/solution.py
+++ b/solution.py
@@ -222,18 +222,24 @@
 
     def weigh(head):
         scores = score_ref[head]
-        top = jnp.max(scores, axis=1, keepdims=True)
-        old_max = FLOOR if first else max_in[head][:, :1]
+        top = jnp.broadcast_to(jnp.max(scores, axis=1, keepdims=True), (tok_dev, LANES))
+        old_max = FLOOR if first else max_in[head]
         new_max = jnp.maximum(top, old_max)
-        weights = jnp.exp2(scores - new_max)
-        total = jnp.sum(weights, axis=1, keepdims=True)
+        weights = jnp.exp2(scores - jnp.concatenate([new_max] * (n_keys // LANES), axis=1))
+        total = jnp.broadcast_to(jnp.sum(weights, axis=1, keepdims=True), (tok_dev, LANES))
         weight_ref[head] = weights.astype(jnp.bfloat16)
+        if not last:
+            max_out[head] = new_max
         if first:
-            return new_max, total, None
+            sum_out[head] = total
+            return total, None
         faded = jnp.exp2(old_max - new_max)
-        return new_max, total + faded * sum_in[head][:, :1], faded
-
-    def mix(head, new_max, total, faded):
+        total = total + faded * sum_in[head]
+        if not last:
+            sum_out[head] = total
+        return total, faded
+
+    def mix(head, total, faded):
         values = value_ref[:, head * VD : (head + 1) * VD]
         mixed = jnp.dot(weight_ref[head], values, preferred_element_type=jnp.float32)
         if not first:
@@ -243,8 +249,6 @@
             if head % 2 == 1:
                 copies[head // 2].start()
         else:
-            max_out[head] = jnp.broadcast_to(new_max, mixed.shape)
-            sum_out[head] = jnp.broadcast_to(total, mixed.shape)
             acc_out[head] = mixed
 
     copies = []
@@ -381,6 +385,7 @@
         compiler_params=SMALL,
     )(fast(rows), fast(other), fast(w_key))
     opposite = lax.ppermute(piece, "head", across_y)
+    (piece,) = join([[piece, opposite]])
     w_query, piece = lax.optimization_barrier((w_query, piece))
     w_query = pl.pallas_call(
         fetch_kernel,
@@ -390,13 +395,12 @@
         scratch_shapes=[pltpu.SemaphoreType.DMA],
         compiler_params=SMALL,
     )(slow(w_query))
-    (piece,) = join([[piece, opposite]], after=[w_query])
     q_opposite = lax.ppermute(q_pair, "head", across_y)
     coarse = [lax.ppermute(piece, "ctx", chip_shift(step)) for step in COARSE]
 
     set_shape = coarse[0].shape
     q_at = len(COARSE) * set_shape[1]
-    (coarse,) = join([coarse])
+    (coarse,) = join([coarse], after=[w_query])
     q_set, bundle = pl.pallas_call(
         bundle_kernel,
         in_specs=[vmem] * 3,
@@ -407,6 +411,7 @@
         ],
         compiler_params=SMALL,
     )(*[fast(a) for a in (coarse, q_pair, q_opposite)])
+    coarse, bundle = lax.optimization_barrier((coarse, bundle))
     later = lax.ppermute(coarse, "ctx", chip_shift(1))
     sooner = lax.ppermute(coarse, "ctx", chip_shift(-1))
     got = lax.ppermute(bundle, ("ctx", "head"), apart)
@@ -421,7 +426,7 @@
         compiler_params=SMALL,
     )(slow(doc_lengths), fast(q_set), fast(got), fast(w_query))
 
-    (near,) = join([[later, sooner]], after=[queries])
+    (near,) = join([[later, sooner]], after=[got])
     received = lax.ppermute(near, ("ctx", "head"), apart)
     near_swapped = lax.ppermute(near, "ctx", swap)
     got_swapped = lax.ppermute(got, "ctx", swap)
@@ -432,15 +437,17 @@
     near_slots = [*[k + 1 for k in COARSE], *[k - 1 for k in COARSE]]
     views = [(0, 0, 0, 0, COARSE), (1, 0, 0, 0, near_slots)]
     views += [(2, 0, 1, 0, COARSE), (3, 0, 1, 0, near_slots)]
+    pieces = [coarse, near, coarse_swapped, near_swapped]
+    state = attend_to(pieces, views, 2, None)
+    received, got_swapped, state = lax.optimization_barrier((received, got_swapped, state))
+    swapped = lax.ppermute(received, "ctx", swap)
+    views = []
     for partner in range(2):
         for n, k in enumerate(COARSE):
-            views.append((4 + partner, n * set_shape[1], partner, 1, [k]))
-    pieces = [coarse, near, coarse_swapped, near_swapped, got, got_swapped]
-    state = attend_to(pieces, views, 2, None)
-    received, state = lax.optimization_barrier((received, state))
-    swapped = lax.ppermute(received, "ctx", swap)
-    state = attend_to([received], [(0, 0, 0, 1, near_slots)], 1, state)
-    return attend_to([swapped], [(0, 0, 1, 1, near_slots)], 1, state, last=True)
+            views.append((partner, n * set_shape[1], partner, 1, [k]))
+    state = attend_to([got, got_swapped], views, 2, state)
+    views = [(n, 0, n, 1, near_slots) for n in range(2)]
+    return attend_to([received, swapped], views, 2, state, last=True)
 
 
 def solution(mesh):

time: 59.1 us -> 56.4 us (0.954)
  starting transfers between devices: 30.4 us -> 29 us
  Pallas kernels: 20.4 us -> 19.3 us
    ppermute x1, waiting for transfers between devices: 0.01 us -> 3.32 us  [body(): later = lax.ppermute(coarse, 'ctx', chip_shift(1))]
    ppermute x3, waiting for transfers between devices: 3.08 us -> 1.15 us  [body(): coarse = [lax.ppermute(piece, 'ctx', chip_shift(step)) for step in COARSE]]
    ppermute x1, waiting for transfers between devices: 1.56 us -> 0.01 us  [body(): coarse_swapped = lax.ppermute(coarse, 'ctx', swap)]
    ppermute x1, waiting for transfers between devices: 1.41 us -> 0.01 us  [body(): got = lax.ppermute(bundle, ('ctx', 'head'), apart)]
    ppermute x1, waiting for transfers between devices: 0.01 us -> 1.3 us  [body(): opposite = lax.ppermute(piece, 'head', across_y)]
    pallas_call x3, Pallas kernels: 14.4 us -> 13.4 us  [attend(): pl.pallas_call(kernel, in_specs=[pl.BlockSpec(memory_space=pltpu.SMEM)] +...]
    ppermute x1, starting transfers between devices: 4.75 us -> 3.76 us  [body(): near_swapped = lax.ppermute(near, 'ctx', swap)]
  transfers between devices with their start and end apart: 14 -> 14, of which waited for: 3 -> 3; matrix products, arithmetic and copies ran while one was open for 0% -> 0% of each run, Pallas kernels for 26% -> 24%
where the time goes in v10:
time: 56.4 us; the launch traced here: 56 us
  starting transfers between devices  29 us (51%)
  Pallas kernels  19.3 us (34%)
  waiting for transfers between devices  5.79 us (10%)
  local copies, waits for them, and re-layouts  1.61 us (3%)
    pallas_call x3, Pallas kernels, attend(): pl.pallas_call(kernel, in_specs=[pl.BlockSpec(memory_space=pltpu.SMEM)] +...  13.4 us
    ppermute x3, starting transfers between devices, body(): coarse = [lax.ppermute(piece, 'ctx', chip_shift(step)) for step in COARSE]  10.3 us
    ppermute x1, starting transfers between devices, body(): near_swapped = lax.ppermute(near, 'ctx', swap)  3.76 us
    ppermute x1, starting transfers between devices, body(): other = lax.ppermute(rows, 'head', across_x)  3.66 us
    ppermute x1, starting transfers between devices, body(): sooner = lax.ppermute(coarse, 'ctx', chip_shift(-1))  3.57 us
    ppermute x1, waiting for transfers between devices, body(): later = lax.ppermute(coarse, 'ctx', chip_shift(1))  3.32 us
    ppermute x1, starting transfers between devices, body(): opposite = lax.ppermute(piece, 'head', across_y)  2.95 us
    ppermute x1, starting transfers between devices, body(): got = lax.ppermute(bundle, ('ctx', 'head'), apart)  2.73 us
  transfers between devices with their start and end apart: 14, of which 3 were waited for; matrix products, arithmetic and copies ran while one was open for 0% of the time, Pallas kernels for 24%

profile of v10, /device:TPU:1, one launch (start us, length us, event | category | flops | bytes accessed | tf_op | source)
XLA Modules:
  0.0 56.0 jit_solution(9391257742726283208)
XLA Ops:
  0.0 0.9 %shard_map.100.own_ref = bf16[16,2112]{1,0:T(8,128)(2,1)S(1)} custom-call(bf16[16,1536]{1,0:T(8,128)(2,1)} %q_ref.1, f32[1536]{0:T(1024)} %q_gain_ref.1, bf16[16,576]{1,0:T(8,128)(2,1)} %kv_ref.1, f32[512]{0:T(512)} %kv_gain_ref.1), custom_call_target="tpu_custom_call" | custom-call | tf_op jit(solution)/shard_map/pallas_call | solution.py:360
  0.9 3.7 %collective-permute-start = (bf16[16,2112]{1,0:T(8,128)(2,1)S(1)}, bf16[16,2112]{1,0:T(8,128)(2,1)S(1)}, u32[]{:S(2)}, u32[]{:S(2)}) collective-permute-start(bf16[16,2112]{1,0:T(8,128)(2,1)S(1)} %shard_map.100.own_ref), channel_id=1, source_target_pairs={{0,1},{1,0},{2,3},{3,2},{4,5},{5,4},{6,7},{7,6},{8,9},{9,8},{10,11... | collective-permute-start | bytes 202760 | tf_op jit(solution)/shard_map/ppermute | solution.py:365
  4.6 0.0 copy-start
  4.6 1.6 %copy-done = bf16[512,2048]{1,0:T(8,128)(2,1)S(1)} copy-done((bf16[512,2048]{1,0:T(8,128)(2,1)S(1)}, bf16[512,2048]{1,0:T(8,128)(2,1)}, u32[]{:S(2)}) %copy-start) | copy-done | bytes 2097176
  6.2 0.5 shard_map.101
  6.7 0.0 collective-permute-done.other_ref
  6.7 0.1 shard_map.102
  6.8 2.9 %collective-permute-start.1 = (bf16[16,1152]{1,0:T(8,128)(2,1)S(1)}, bf16[16,1152]{1,0:T(8,128)(2,1)S(1)}, u32[]{:S(2)}, u32[]{:S(2)}) collective-permute-start(bf16[16,1152]{1,0:T(8,128)(2,1)S(1)} %get-tuple-element.31.refs_0_), channel_id=1, source_target_pairs={{0,4},{1,5},{2,6},{3,7},{4,0},{5,1},{6,2},{7,3},{8,12},{9,13},{10,... | collective-permute-start | bytes 110600 | tf_op jit(solution)/shard_map/ppermute | solution.py:387
  9.7 0.1 collective-permute-start.5
  9.8 1.3 %collective-permute-done.1.refs_1_ = bf16[16,1152]{1,0:T(8,128)(2,1)S(1)} collective-permute-done((bf16[16,1152]{1,0:T(8,128)(2,1)S(1)}, bf16[16,1152]{1,0:T(8,128)(2,1)S(1)}, u32[]{:S(2)}, u32[]{:S(2)}) %collective-permute-start.1) | collective-permute-done | bytes 36896 | tf_op jit(solution)/shard_map/ppermute | solution.py:387
  11.1 6.9 %collective-permute-start.2 = (bf16[32,1152]{1,0:T(8,128)(2,1)S(1)}, bf16[32,1152]{1,0:T(8,128)(2,1)S(1)}, u32[]{:S(2)}, u32[]{:S(2)}) collective-permute-start(bf16[32,1152]{1,0:T(8,128)(2,1)S(1)} %shard_map.103), channel_id=1, source_target_pairs={{0,64},{8,72},{16,80},{24,88},{32,96},{40,104},{48,112},{56,120},{... | collective-permute-start | bytes 221192 | tf_op jit(solution)/shard_map/ppermute | solution.py:399
  18.0 0.7 %collective-permute-start.3 = (bf16[32,1152]{1,0:T(8,128)(2,1)S(1)}, bf16[32,1152]{1,0:T(8,128)(2,1)S(1)}, u32[]{:S(2)}, u32[]{:S(2)}) collective-permute-start(bf16[32,1152]{1,0:T(8,128)(2,1)S(1)} %shard_map.103), channel_id=1, source_target_pairs={{0,16},{8,24},{16,32},{24,40},{32,48},{40,56},{48,64},{56,72},{64,... | collective-permute-start | bytes 221192 | tf_op jit(solution)/shard_map/ppermute | solution.py:399
  18.8 2.7 %collective-permute-start.4 = (bf16[32,1152]{1,0:T(8,128)(2,1)S(1)}, bf16[32,1152]{1,0:T(8,128)(2,1)S(1)}, u32[]{:S(2)}, u32[]{:S(2)}) collective-permute-start(bf16[32,1152]{1,0:T(8,128)(2,1)S(1)} %shard_map.103), channel_id=1, source_target_pairs={{0,112},{8,120},{16,128},{24,136},{32,144},{40,152},{48,160},{56,1... | collective-permute-start | bytes 221192 | tf_op jit(solution)/shard_map/ppermute | solution.py:399
  21.5 2.3 %shard_map.104.refs_3_ = bf16[1536,1536]{1,0:T(8,128)(2,1)S(1)} custom-call(bf16[1536,1536]{1,0:T(8,128)(2,1)} %from_ref), custom_call_target="tpu_custom_call" | custom-call | tf_op jit(solution)/shard_map/pallas_call | solution.py:390
  23.8 0.0 collective-permute-done.2.refs_0_
  23.8 1.1 %collective-permute-done.3.refs_1_ = bf16[32,1152]{1,0:T(8,128)(2,1)S(1)} collective-permute-done((bf16[32,1152]{1,0:T(8,128)(2,1)S(1)}, bf16[32,1152]{1,0:T(8,128)(2,1)S(1)}, u32[]{:S(2)}, u32[]{:S(2)}) %collective-permute-start.3) | collective-permute-done | bytes 73760 | tf_op jit(solution)/shard_map/ppermute | solution.py:399
  25.0 0.0 collective-permute-done.4.refs_2_
  25.0 0.0 copy-start.1
  25.0 0.0 collective-permute-done.5.q_got_ref
  25.1 2.7 %collective-permute-start.6 = (bf16[32,6528]{1,0:T(8,128)(2,1)S(1)}, bf16[32,6528]{1,0:T(8,128)(2,1)S(1)}, u32[]{:S(2)}, u32[]{:S(2)}) collective-permute-start(bf16[32,6528]{1,0:T(8,128)(2,1)S(1)} %get-tuple-element.37), channel_id=1, source_target_pairs={{0,2},{1,3},{2,4},{3,5},{4,6},{5,7},{6,0},{7,1},{8,14},{9,15},{10,... | collective-permute-start | bytes 1253384 | tf_op jit(solution)/shard_map/ppermute | solution.py:417
  27.8 0.0 collective-permute-start.7
  27.8 3.6 %collective-permute-start.8 = (bf16[96,1152]{1,0:T(8,128)(2,1)S(1)}, bf16[96,1152]{1,0:T(8,128)(2,1)S(1)}, u32[]{:S(2)}, u32[]{:S(2)}) collective-permute-start(bf16[96,1152]{1,0:T(8,128)(2,1)S(1)} %shard_map.105.coarse_ref.refs_5_), channel_id=1, source_target_pairs={{0,240},{8,248},{16,0},{24,8},{32,16},{40,24},{48,32},{56,40},{64,... | collective-permute-start | bytes 663560 | tf_op jit(solution)/shard_map/ppermute | solution.py:416
  31.4 3.3 %collective-permute-done.7.refs_0_ = bf16[96,1152]{1,0:T(8,128)(2,1)S(1)} collective-permute-done((bf16[96,1152]{1,0:T(8,128)(2,1)S(1)}, bf16[96,1152]{1,0:T(8,128)(2,1)S(1)}, u32[]{:S(2)}, u32[]{:S(2)}) %collective-permute-start.7) | collective-permute-done | bytes 221216 | tf_op jit(solution)/shard_map/ppermute | solution.py:415
  34.7 0.0 collective-permute-done.8.refs_1_
  34.7 0.0 collective-permute-done.6.refs_2_.refs_5_
  34.7 3.8 %collective-permute-start.12 = (bf16[192,1152]{1,0:T(8,128)(2,1)S(1)}, bf16[192,1152]{1,0:T(8,128)(2,1)S(1)}, u32[]{:S(2)}, u32[]{:S(2)}) collective-permute-start(bf16[192,1152]{1,0:T(8,128)(2,1)S(1)} %shard_map.108.refs_6_), channel_id=1, source_target_pairs={{0,8},{8,0},{16,24},{24,16},{32,40},{40,32},{48,56},{56,48},{64,72... | collective-permute-start | bytes 1327112 | tf_op jit(solution)/shard_map/ppermute | solution.py:431
  38.5 1.0 %collective-permute-start.9 = (bf16[192,1152]{1,0:T(8,128)(2,1)S(1)}, bf16[192,1152]{1,0:T(8,128)(2,1)S(1)}, u32[]{:S(2)}, u32[]{:S(2)}) collective-permute-start(bf16[192,1152]{1,0:T(8,128)(2,1)S(1)} %shard_map.108.refs_6_), channel_id=1, source_target_pairs={{0,2},{1,3},{2,4},{3,5},{4,6},{5,7},{6,0},{7,1},{8,14},{9,15},{10,... | collective-permute-start | bytes 1327112 | tf_op jit(solution)/shard_map/ppermute | solution.py:430
  39.5 0.3 collective-permute-start.10
  39.8 0.2 collective-permute-start.11
  40.0 0.0 copy-start.3
  40.0 2.1 %shard_map.107.refs_1_ = bf16[8,128,256]{2,1,0:T(8,128)(2,1)S(1)} custom-call(s32[3]{0:T(128)} %refs_0_.7, bf16[32,3072]{1,0:T(8,128)(2,1)S(1)} %get-tuple-element.35.refs_1_, bf16[32,6528]{1,0:T(8,128)(2,1)S(1)} %collective-permute-done.6.refs_2_.refs_5_, bf16[1536,1536]{1,0:T(8,128)(2,1)S(1)} %shard_map.104.refs_3_), custom_call_target="tpu_custom_call" | custom-call | tf_op jit(solution)/shard_map/pallas_call | solution.py:420
  42.1 0.0 copy-start.2
  42.1 0.0 collective-permute-done.11.refs_7_
  42.1 0.0 collective-permute-done.12.refs_8_
  42.1 0.0 copy-done.1
  42.1 5.8 %shard_map.109 = (f32[8,128,128]{2,1,0:T(8,128)S(1)}, f32[8,128,128]{2,1,0:T(8,128)S(1)}, f32[8,128,128]{2,1,0:T(8,128)S(1)}) custom-call(s32[3]{0:T(128)} %refs_0_.7, bf16[8,128,256]{2,1,0:T(8,128)(2,1)S(1)} %shard_map.107.refs_1_, s32[5,1152]{1,0:T(8,128)S(1)} %copy-done.1, bf16[1024,512]{1,0:T(8,128)(2,1)S(1)} %get-tuple-element.30.ready_ref.refs_3_, ...), custom_call_target="tpu_custom_call" | custom-call | tf_op jit(solution)/shard_map/pallas_call | solution.py:315
  47.9 0.0 collective-permute-done.10.refs_6_
  47.9 0.0 collective-permute-done.9.refs_5_
  48.0 0.4 collective-permute-start.13
  48.3 0.0 copy-done.3
  48.3 2.7 %shard_map.110 = (f32[8,128,128]{2,1,0:T(8,128)S(1)}, f32[8,128,128]{2,1,0:T(8,128)S(1)}, f32[8,128,128]{2,1,0:T(8,128)S(1)}) custom-call(s32[3]{0:T(128)} %refs_0_.7, bf16[8,128,256]{2,1,0:T(8,128)(2,1)S(1)} %shard_map.107.refs_1_, s32[5,384]{1,0:T(8,128)S(1)} %copy-done.3, bf16[1024,512]{1,0:T(8,128)(2,1)S(1)} %get-tuple-element.30.ready_ref.refs_3_, ...), custom_call_target="tpu_custom_call" | custom-call | tf_op jit(solution)/shard_map/pallas_call | solution.py:315
  51.0 0.0 collective-permute-done.13.refs_6_
  51.1 0.0 copy-done.2
  51.1 4.8 %shard_map.111 = bf16[128,1024]{1,0:T(8,128)(2,1)} custom-call(s32[3]{0:T(128)} %refs_0_.7, bf16[8,128,256]{2,1,0:T(8,128)(2,1)S(1)} %shard_map.107.refs_1_, s32[5,768]{1,0:T(8,128)S(1)} %copy-done.2, bf16[1024,512]{1,0:T(8,128)(2,1)S(1)} %get-tuple-element.30.ready_ref.refs_3_, bf16[512,1024]{1,0:T(8,128)(2,1)S(1)} %get-tuple-element.38.refs_4_, ...), custom_call_target="tpu_custom_call" | custom-call | tf_op jit(solution)/shard_map/pallas_call | solution.py:315
  (4 shorter events, 0.1 us)
Async XLA Ops:
  0.9 5.7 %collective-permute-start = (bf16[16,2112]{1,0:T(8,128)(2,1)S(1)}, bf16[16,2112]{1,0:T(8,128)(2,1)S(1)}, u32[]{:S(2)}, u32[]{:S(2)}) collective-permute-start(bf16[16,2112]{1,0:T(8,128)(2,1)S(1)} %shard_map.100.own_ref), channel_id=1, source_target_pairs={{0,1},{1,0},{2,3},{3,2},{4,5},{5,4},{6,7},{7,6},{8,9},{9,8},{10,11... | collective-permute-start | bytes 202760 | tf_op jit(solution)/shard_map/ppermute | solution.py:365
  4.6 1.6 %copy-start = (bf16[512,2048]{1,0:T(8,128)(2,1)S(1)}, bf16[512,2048]{1,0:T(8,128)(2,1)}, u32[]{:S(2)}) copy-start(bf16[512,2048]{1,0:T(8,128)(2,1)} %w_ref) | copy-start | bytes 6291460
  6.8 4.3 %collective-permute-start.1 = (bf16[16,1152]{1,0:T(8,128)(2,1)S(1)}, bf16[16,1152]{1,0:T(8,128)(2,1)S(1)}, u32[]{:S(2)}, u32[]{:S(2)}) collective-permute-start(bf16[16,1152]{1,0:T(8,128)(2,1)S(1)} %get-tuple-element.31.refs_0_), channel_id=1, source_target_pairs={{0,4},{1,5},{2,6},{3,7},{4,0},{5,1},{6,2},{7,3},{8,12},{9,13},{10,... | collective-permute-start | bytes 110600 | tf_op jit(solution)/shard_map/ppermute | solution.py:387
  9.7 15.3 %collective-permute-start.5 = (bf16[16,3072]{1,0:T(8,128)(2,1)S(1)}, bf16[16,3072]{1,0:T(8,128)(2,1)S(1)}, u32[]{:S(2)}, u32[]{:S(2)}) collective-permute-start(bf16[16,3072]{1,0:T(8,128)(2,1)S(1)} %get-tuple-element.34.q_own_ref), channel_id=1, source_target_pairs={{0,4},{1,5},{2,6},{3,7},{4,0},{5,1},{6,2},{7,3},{8,12},{9,13},{10,... | collective-permute-start | bytes 294920 | tf_op jit(solution)/shard_map/ppermute | solution.py:398
  11.1 12.7 %collective-permute-start.2 = (bf16[32,1152]{1,0:T(8,128)(2,1)S(1)}, bf16[32,1152]{1,0:T(8,128)(2,1)S(1)}, u32[]{:S(2)}, u32[]{:S(2)}) collective-permute-start(bf16[32,1152]{1,0:T(8,128)(2,1)S(1)} %shard_map.103), channel_id=1, source_target_pairs={{0,64},{8,72},{16,80},{24,88},{32,96},{40,104},{48,112},{56,120},{... | collective-permute-start | bytes 221192 | tf_op jit(solution)/shard_map/ppermute | solution.py:399
  18.0 6.9 %collective-permute-start.3 = (bf16[32,1152]{1,0:T(8,128)(2,1)S(1)}, bf16[32,1152]{1,0:T(8,128)(2,1)S(1)}, u32[]{:S(2)}, u32[]{:S(2)}) collective-permute-start(bf16[32,1152]{1,0:T(8,128)(2,1)S(1)} %shard_map.103), channel_id=1, source_target_pairs={{0,16},{8,24},{16,32},{24,40},{32,48},{40,56},{48,64},{56,72},{64,... | collective-permute-start | bytes 221192 | tf_op jit(solution)/shard_map/ppermute | solution.py:399
  18.8 6.2 %collective-permute-start.4 = (bf16[32,1152]{1,0:T(8,128)(2,1)S(1)}, bf16[32,1152]{1,0:T(8,128)(2,1)S(1)}, u32[]{:S(2)}, u32[]{:S(2)}) collective-permute-start(bf16[32,1152]{1,0:T(8,128)(2,1)S(1)} %shard_map.103), channel_id=1, source_target_pairs={{0,112},{8,120},{16,128},{24,136},{32,144},{40,152},{48,160},{56,1... | collective-permute-start | bytes 221192 | tf_op jit(solution)/shard_map/ppermute | solution.py:399
  25.0 17.1 %copy-start.1 = (s32[5,1152]{1,0:T(8,128)S(1)}, s32[5,1152]{1,0:T(8,128)}, u32[]{:S(2)}) copy-start(s32[5,1152]{1,0:T(8,128)} %constant.6.clone.refs_2_) | copy-start | bytes 69124
  25.1 9.6 %collective-permute-start.6 = (bf16[32,6528]{1,0:T(8,128)(2,1)S(1)}, bf16[32,6528]{1,0:T(8,128)(2,1)S(1)}, u32[]{:S(2)}, u32[]{:S(2)}) collective-permute-start(bf16[32,6528]{1,0:T(8,128)(2,1)S(1)} %get-tuple-element.37), channel_id=1, source_target_pairs={{0,2},{1,3},{2,4},{3,5},{4,6},{5,7},{6,0},{7,1},{8,14},{9,15},{10,... | collective-permute-start | bytes 1253384 | tf_op jit(solution)/shard_map/ppermute | solution.py:417
  27.8 6.9 %collective-permute-start.7 = (bf16[96,1152]{1,0:T(8,128)(2,1)S(1)}, bf16[96,1152]{1,0:T(8,128)(2,1)S(1)}, u32[]{:S(2)}, u32[]{:S(2)}) collective-permute-start(bf16[96,1152]{1,0:T(8,128)(2,1)S(1)} %shard_map.105.coarse_ref.refs_5_), channel_id=1, source_target_pairs={{0,16},{8,24},{16,32},{24,40},{32,48},{40,56},{48,64},{56,72},{64,... | collective-permute-start | bytes 663560 | tf_op jit(solution)/shard_map/ppermute | solution.py:415
  27.8 6.9 %collective-permute-start.8 = (bf16[96,1152]{1,0:T(8,128)(2,1)S(1)}, bf16[96,1152]{1,0:T(8,128)(2,1)S(1)}, u32[]{:S(2)}, u32[]{:S(2)}) collective-permute-start(bf16[96,1152]{1,0:T(8,128)(2,1)S(1)} %shard_map.105.coarse_ref.refs_5_), channel_id=1, source_target_pairs={{0,240},{8,248},{16,0},{24,8},{32,16},{40,24},{48,32},{56,40},{64,... | collective-permute-start | bytes 663560 | tf_op jit(solution)/shard_map/ppermute | solution.py:416
  34.7 7.4 %collective-permute-start.12 = (bf16[192,1152]{1,0:T(8,128)(2,1)S(1)}, bf16[192,1152]{1,0:T(8,128)(2,1)S(1)}, u32[]{:S(2)}, u32[]{:S(2)}) collective-permute-start(bf16[192,1152]{1,0:T(8,128)(2,1)S(1)} %shard_map.108.refs_6_), channel_id=1, source_target_pairs={{0,8},{8,0},{16,24},{24,16},{32,40},{40,32},{48,56},{56,48},{64,72... | collective-permute-start | bytes 1327112 | tf_op jit(solution)/shard_map/ppermute | solution.py:431
  38.5 9.5 %collective-permute-start.9 = (bf16[192,1152]{1,0:T(8,128)(2,1)S(1)}, bf16[192,1152]{1,0:T(8,128)(2,1)S(1)}, u32[]{:S(2)}, u32[]{:S(2)}) collective-permute-start(bf16[192,1152]{1,0:T(8,128)(2,1)S(1)} %shard_map.108.refs_6_), channel_id=1, source_target_pairs={{0,2},{1,3},{2,4},{3,5},{4,6},{5,7},{6,0},{7,1},{8,14},{9,15},{10,... | collective-permute-start | bytes 1327112 | tf_op jit(solution)/shard_map/ppermute | solution.py:430
  39.5 8.5 %collective-permute-start.10 = (bf16[32,6528]{1,0:T(8,128)(2,1)S(1)}, bf16[32,6528]{1,0:T(8,128)(2,1)S(1)}, u32[]{:S(2)}, u32[]{:S(2)}) collective-permute-start(bf16[32,6528]{1,0:T(8,128)(2,1)S(1)} %collective-permute-done.6.refs_2_.refs_5_), channel_id=1, source_target_pairs={{0,8},{8,0},{16,24},{24,16},{32,40},{40,32},{48,56},{56,48},{64,72... | collective-permute-start | bytes 1253384 | tf_op jit(solution)/shard_map/ppermute | solution.py:432
  39.8 2.3 %collective-permute-start.11 = (bf16[96,1152]{1,0:T(8,128)(2,1)S(1)}, bf16[96,1152]{1,0:T(8,128)(2,1)S(1)}, u32[]{:S(2)}, u32[]{:S(2)}) collective-permute-start(bf16[96,1152]{1,0:T(8,128)(2,1)S(1)} %shard_map.105.coarse_ref.refs_5_), channel_id=1, source_target_pairs={{0,8},{8,0},{16,24},{24,16},{32,40},{40,32},{48,56},{56,48},{64,72... | collective-permute-start | bytes 663560 | tf_op jit(solution)/shard_map/ppermute | solution.py:418
  40.0 8.3 %copy-start.3 = (s32[5,384]{1,0:T(8,128)S(1)}, s32[5,384]{1,0:T(8,128)}, u32[]{:S(2)}) copy-start(s32[5,384]{1,0:T(8,128)} %constant.7.clone.refs_2_) | copy-start | bytes 23044
  42.1 9.0 %copy-start.2 = (s32[5,768]{1,0:T(8,128)S(1)}, s32[5,768]{1,0:T(8,128)}, u32[]{:S(2)}) copy-start(s32[5,768]{1,0:T(8,128)} %constant.8.clone.refs_2_) | copy-start | bytes 46084
  48.0 3.1 %collective-permute-start.13 = (bf16[192,1152]{1,0:T(8,128)(2,1)S(1)}, bf16[192,1152]{1,0:T(8,128)(2,1)S(1)}, u32[]{:S(2)}, u32[]{:S(2)}) collective-permute-start(bf16[192,1152]{1,0:T(8,128)(2,1)S(1)} %collective-permute-done.9.refs_5_), channel_id=1, source_target_pairs={{0,8},{8,0},{16,24},{24,16},{32,40},{40,32},{48,56},{56,48},{64,72... | collective-permute-start | bytes 1327112 | tf_op jit(solution)/shard_map/ppermute | solution.py:443
